TPU v7x, 32 devices: a whole 2x2x4 slice. The times are simulated.
32 devices in a mesh: page: 8 (over z, x), tok: 4 (over y, core).
Axes of the slice: x: 2, y: 2, z: 4, core: 2. Of those that a mesh axis runs over, the one named last changes fastest.
Arguments:
- tile_tokens: bfloat16 [8, 4096, 1024], P('page', 'tok'), may hold values from -6 to 6
- page_lengths: int32 [8], P('page'), may hold values from 1 to 4096, as said below
- occupancy: int32 [8, 32], P('page', 'tok'), may hold values 0 or 1
- block_mix: bfloat16 [32, 128, 128], P('tok'), may hold values from -0.5 to 0.5
- stride_mix: bfloat16 [128, 32, 32], P('tok'), may hold values from -1 to 1
- w_gate_up: bfloat16 [2, 1024, 2048], P(None, None, ('page', 'tok')), may hold values from -0.1875 to 0.1875
- w_down: bfloat16 [2048, 1024], P(None, ('page', 'tok')), may hold values from -0.125 to 0.125
Outputs:
- packed_lanes: bfloat16 [4, 8192, 1024], P('tok', 'page')
Inputs may be any that keep to these rules, and one draw needn't show every extreme that they name: `page_lengths`: some page has exactly 4096 used tokens in every draw; page 0 has fewer than 1024 used tokens in every draw.
All inputs are finite; a program needn't handle non-finite values. No bound on the sum of `occupancy` on one device may be relied on, other than what follows from the above.
Results may differ from a plain program's by a relative error of at most 0.012.
Values may be sent and summed in bfloat16 or wider, within the bound.
No kernel may reach another device: no remote copies, remote signals or barrier semaphores. Data moves between devices by JAX's collectives and lax.ppermute only.
A program may use at most 64 MiB of HBM per device.

v0:
```python
import jax
import jax.numpy as jnp
from jax import lax
from jax.sharding import PartitionSpec as P

epsilon = 1e-05


def entering(value, axis, join, neutral):
    count, mine = (lax.axis_size(axis), lax.axis_index(axis))
    pieces = lax.all_gather(value, axis)
    so_far = jnp.full_like(value, 0) + jnp.asarray(neutral, value.dtype)

    def hop(position, so_far):
        longer = join(so_far, pieces[position])
        return jnp.where(position < mine, longer, so_far)

    return lax.fori_loop(0, count - 1, hop, so_far)


def from_behind(value, axis, by):
    length = lax.axis_size(axis)
    pairs = [(i, i + by) for i in range(length) if 0 <= i + by < length]
    return lax.ppermute(value, axis, pairs)


def rms_round(values):
    scale = lax.rsqrt(jnp.mean(values * values, axis=-1, keepdims=True) + epsilon)
    return (values * scale).astype(jnp.bfloat16)


def add_counts(earlier, later):
    return earlier + later


def channel_mlp(mixed, w_gate_up, w_down):
    mixed_float = mixed.astype(jnp.float32)
    normed_two = rms_round(mixed_float)
    shard_part = lax.all_gather(w_gate_up, ("page", "tok"), axis=2, tiled=True)
    gate_vals = jnp.dot(normed_two, shard_part[0], preferred_element_type=jnp.float32)
    up_vals = jnp.dot(normed_two, shard_part[1], preferred_element_type=jnp.float32)
    hidden = (jax.nn.silu(gate_vals) * up_vals).astype(jnp.bfloat16)
    down_vals = jnp.dot(
        hidden,
        lax.all_gather(w_down, ("page", "tok"), axis=1, tiled=True),
        preferred_element_type=jnp.float32,
    )
    return (mixed_float + down_vals).astype(jnp.bfloat16)


def lane_relay(row_data, length, lane_index):
    row_count = row_data.shape[0]
    page_here = lax.axis_index("page")
    live_rows = jnp.clip(length - lane_index * row_count, 0, row_count)
    before = entering(live_rows.reshape(1), "page", add_counts, jnp.zeros((1,), jnp.int32))[0]
    distance = page_here * row_count - before
    in_shift = distance % row_count
    hop_count = distance // row_count
    row_ids = jnp.arange(row_count, dtype=jnp.int32)
    live_flag = row_ids < live_rows
    kept_data = jnp.where(live_flag[:, None], row_data, jnp.zeros_like(row_data))
    kept_tags = jnp.where(live_flag, hop_count + 1, 0).astype(jnp.int32)
    zero_data = jnp.zeros_like(row_data)
    zero_tags = jnp.zeros_like(kept_tags)
    here_data = lax.dynamic_slice_in_dim(
        jnp.concatenate([kept_data, zero_data], 0), in_shift, row_count, 0
    )
    here_tags = lax.dynamic_slice_in_dim(
        jnp.concatenate([kept_tags, zero_tags], 0), in_shift, row_count, 0
    )
    spill_data = lax.dynamic_slice_in_dim(
        jnp.concatenate([zero_data, kept_data], 0), in_shift, row_count, 0
    )
    spill_tags = lax.dynamic_slice_in_dim(
        jnp.concatenate([zero_tags, kept_tags], 0), in_shift, row_count, 0
    )
    got_data, got_tags = from_behind((spill_data, spill_tags), "page", -1)
    arrived = got_tags > 0
    cur_data = jnp.where(arrived[:, None], got_data, here_data)
    cur_tags = jnp.where(arrived, got_tags, here_tags)
    for bit_pos in range((lax.axis_size("page") - 1).bit_length()):
        stride_len = 1 << bit_pos
        present = cur_tags > 0
        moving = present & ((cur_tags - 1) // stride_len % 2 == 1)
        staying = present & jnp.logical_not(moving)
        out_data = jnp.where(moving[:, None], cur_data, jnp.zeros_like(cur_data))
        out_tags = jnp.where(moving, cur_tags, 0)
        got_data, got_tags = from_behind((out_data, out_tags), "page", -stride_len)
        arrived = got_tags > 0
        kept_now = jnp.where(staying[:, None], cur_data, jnp.zeros_like(cur_data))
        cur_data = jnp.where(arrived[:, None], got_data, kept_now)
        cur_tags = jnp.where(arrived, got_tags, jnp.where(staying, cur_tags, 0))
    return cur_data


def per_device(tile_tokens, page_lengths, occupancy, block_mix, stride_mix, w_gate_up, w_down):
    lane_index = lax.axis_index("tok")
    row_count = tile_tokens.shape[1]
    feat_width = tile_tokens.shape[2]
    blocks_here = block_mix.shape[0]
    blk_size = block_mix.shape[1]
    length = page_lengths[0]
    positions = lane_index * row_count + jnp.arange(row_count, dtype=jnp.int32)
    live_mask = (positions < length) & (jnp.repeat(occupancy[0], blk_size) > 0)
    masked = jnp.where(live_mask[:, None], tile_tokens[0].astype(jnp.float32), 0.0)
    normed = rms_round(masked).reshape(blocks_here, blk_size, feat_width)
    first = jnp.einsum(
        "bji,bic->bjc", block_mix, normed, preferred_element_type=jnp.float32
    ).astype(jnp.bfloat16)
    second = jnp.einsum(
        "jkb,bjc->jkc",
        stride_mix,
        lax.all_to_all(first, "tok", split_axis=1, concat_axis=0, tiled=True),
        preferred_element_type=jnp.float32,
    )
    mixed = (masked + second.reshape(row_count, feat_width)).astype(jnp.bfloat16)
    layer_out = channel_mlp(mixed, w_gate_up, w_down)
    packed = lane_relay(layer_out, length, lane_index)
    return packed.reshape(1, row_count, feat_width)


def solution(mesh):
    return jax.shard_map(
        per_device,
        mesh=mesh,
        in_specs=(
            P("page", "tok", None),
            P("page"),
            P("page", "tok"),
            P("tok", None, None),
            P("tok", None, None),
            P(None, None, ("page", "tok")),
            P(None, ("page", "tok")),
        ),
        out_specs=P("tok", "page", None),
        check_vma=False,
    )
```

profile of v0, /device:TPU:0, one launch (start us, length us, event | category | flops | bytes accessed | tf_op | source)
XLA Modules:
  0.0 436.6 jit_solution(2538574586861370304)
XLA Ops:
  8.7 4.0 convert_element_type.76
  12.7 5.5 %copy.13 = f32[8,128,1024]{1,2,0:T(8,128)} copy(f32[8,128,1024]{2,1,0:T(8,128)} %bitcast.76) | data formatting | bytes 8388608 | tf_op jit(solution)/shard_map/convert_element_type | solution.py:105
  19.1 3.0 convert_bitcast_fusion
  22.1 2.9 copy.14
  25.0 4.4 %all-to-all-start = ((bf16[8,128,1024]{2,0,1:T(8,128)(2,1)}), bf16[8,128,1024]{2,0,1:T(8,128)(2,1)S(1)}, u32[]{:S(2)}, u32[]{:S(2)}) async-start(bf16[8,128,1024]{2,0,1:T(8,128)(2,1)} %copy.14), calls=%async_computation | async-start | bytes 4194304 | tf_op jit(solution)/shard_map/all_to_all | solution.py:113
  30.1 0.8 dynamic-update-slice
  30.9 12.7 %all-reduce.4 = s32[8]{0:T(128)S(1)} all-reduce(s32[8]{0:T(128)S(1)} %dynamic-update-slice), channel_id=1, replica_groups=mesh['page'=8,'tok'=4] {'page'}, use_global_device_ids=true, to_apply=%add.4 | all-reduce | flops 8 | bytes 64
  43.6 9.4 %while.13 = (s32[]{:T(128)}, s32[1]{0:T(128)}, s32[]{:T(128)}, s32[8,1]{0,1:T(1,128)S(1)}, s32[]{:T(128)}) while((s32[]{:T(128)}, s32[1]{0:T(128)}, s32[]{:T(128)}, s32[8,1]{0,1:T(1,128)S(1)}, s32[]{:T(128)}) %tuple.47), condition=%wide.region_1.2_spmd, body=%wide.region_0.1_spmd.sunk | while | flops 5 | bytes 107 | solution.py:18
  53.3 5.6 %all-to-all-done = bf16[8,128,1024]{2,0,1:T(8,128)(2,1)S(1)} async-done(((bf16[8,128,1024]{2,0,1:T(8,128)(2,1)}), bf16[8,128,1024]{2,0,1:T(8,128)(2,1)S(1)}, u32[]{:S(2)}, u32[]{:S(2)}) %all-to-all-start) | async-done | bytes 2097184 | tf_op jit(solution)/shard_map/all_to_all | solution.py:113
  58.9 4.5 %fusion = (f32[32,32]{1,0:T(8,128)S(1)}, bf16[32,32,1024]{2,1,0:T(8,128)(2,1)S(1)}, f32[32,1024,32]{1,2,0:T(8,128)}) fusion(f32[32,32,1024]{2,1,0:T(8,128)} %bitcast.77, pred[32,32]{1,0:T(8,128)(4,1)S(1)} %fusion.14, bf16[32,32,32]{2,1,0:T(8,128)(2,1)S(1)} %copy-done, bf16[4,8,32,1024]{3,1,2,0:T(8,128)(2,1)S(1)} %bitcast.78), kind=kOutput, calls=%fused_computation.4 | convolution fusion | flops 73399296 | bytes 12653568 | tf_op jit(solution)/shard_map/jkb,bjc->jkc/dot_general | solution.py:110
  63.9 28.4 %all-gather.3.cloned.1.call-done = bf16[2,1024,2048]{1,2,0:T(8,128)(2,1)} async-done(((bf16[2,1024,64]{1,2,0:T(8,128)(2,1)}), bf16[2,1024,2048]{1,2,0:T(8,128)(2,1)}) %all-gather.3.cloned.1.call-update) | async-done | bytes 8388624 | tf_op jit(solution)/shard_map/all_gather | solution.py:39
  92.3 8.9 %fusion.2 = f32[1024,2048]{1,0:T(8,128)} fusion(bf16[1024,1024]{1,0:T(8,128)(2,1)S(1)} %bitcast.79, bf16[2,1024,2048]{1,2,0:T(8,128)(2,1)} %all-gather.3.cloned.1.call-done), kind=kOutput, calls=%fused_computation.8 | convolution fusion | flops 4294967296 | bytes 14680064 | tf_op jit(solution)/shard_map/dot_general | solution.py:40
  101.1 54.6 %all-gather.5.cloned.1.call-done = bf16[2048,1024]{0,1:T(8,128)(2,1)} async-done(((bf16[2048,32]{0,1:T(8,128)(2,1)}), bf16[2048,1024]{0,1:T(8,128)(2,1)}) %all-gather.5.cloned.1.call-update) | async-done | bytes 4194320 | tf_op jit(solution)/shard_map/all_gather | solution.py:45
  155.8 16.6 %fusion.6 = bf16[1024,1024]{1,0:T(8,128)(2,1)S(1)} fusion(f32[32,1024,32]{1,2,0:T(8,128)} %get-tuple-element.108, bf16[1,1024,1024]{2,1,0:T(8,128)(2,1)} %param.9, pred[1024]{0:T(1024)(128)(4,1)S(1)} %get-tuple-element.110, pred[1024]{0:T(1024)(128)(4,1)S(1)} %get-tuple-element.109, bf16[2048,1024]{0,1:T(8,128)(2,1)} %all-gather.5.cloned.1.call-done, ...), kind=kOutput, calls=%fused_computation.20 | convolution fusion | flops 8610906112 | bytes 27265024 | tf_op jit(solution)/shard_map/dot_general | solution.py:43
  172.4 2.9 pad_dynamic-slice_fusion.1
  175.3 1.3 collective-permute-start.4
  176.7 1.3 collective-permute-start
  178.0 47.3 %collective-permute-done = s32[1024]{0:T(1024)S(1)} collective-permute-done((s32[1024]{0:T(1024)S(1)}, s32[1024]{0:T(1024)S(1)}, u32[]{:S(2)}, u32[]{:S(2)}) %collective-permute-start) | collective-permute-done | bytes 4128 | tf_op jit(solution)/shard_map/ppermute | solution.py:24
  225.5 1.3 collective-permute-start.1
  226.8 4.3 collective-permute-done.1
  231.2 2.9 broadcast_select_fusion
  234.1 1.3 collective-permute-start.5
  235.4 47.7 %collective-permute-done.5 = bf16[1024,1024]{1,0:T(8,128)(2,1)S(1)} collective-permute-done((bf16[1024,1024]{1,0:T(8,128)(2,1)S(1)}, bf16[1024,1024]{1,0:T(8,128)(2,1)S(1)}, u32[]{:S(2)}, u32[]{:S(2)}) %collective-permute-start.5) | collective-permute-done | bytes 2097184 | tf_op jit(solution)/shard_map/ppermute | solution.py:24
  283.1 3.7 broadcast_select_fusion.1
  286.8 1.3 collective-permute-start.6
  288.1 1.3 collective-permute-start.2
  289.4 44.6 %collective-permute-done.2 = s32[1024]{0:T(1024)S(1)} collective-permute-done((s32[1024]{0:T(1024)S(1)}, s32[1024]{0:T(1024)S(1)}, u32[]{:S(2)}, u32[]{:S(2)}) %collective-permute-start.2) | collective-permute-done | bytes 4128 | tf_op jit(solution)/shard_map/ppermute | solution.py:24
  334.1 0.9 broadcast_select_fusion.2
  335.0 1.3 collective-permute-start.7
  336.3 1.3 collective-permute-start.3
  337.6 89.6 %collective-permute-done.3 = s32[1024]{0:T(1024)S(1)} collective-permute-done((s32[1024]{0:T(1024)S(1)}, s32[1024]{0:T(1024)S(1)}, u32[]{:S(2)}, u32[]{:S(2)}) %collective-permute-start.3) | collective-permute-done | bytes 4128 | tf_op jit(solution)/shard_map/ppermute | solution.py:24
  427.2 2.6 select_bitcast_fusion
  (50 shorter events, 8.5 us)
Async XLA Ops:
  6.5 52.4 %copy-start = (bf16[32,32,32]{2,1,0:T(8,128)(2,1)S(1)}, bf16[32,32,32]{2,1,0:T(8,128)(2,1)}, u32[]{:S(2)}) copy-start(bf16[32,32,32]{2,1,0:T(8,128)(2,1)} %param.13) | copy-start | bytes 196612
  6.5 85.7 %all-gather.3.cloned.1.call-start = ((), (), s32[]{:S(2)}) async-start(), calls=%async_computation.1 | async-start | bytes 8650752 | tf_op jit(solution)/shard_map/all_gather | solution.py:39
  7.3 148.5 %all-gather.5.cloned.1.call-start = ((), (), s32[]{:S(2)}) async-start(), calls=%async_computation.2 | async-start | bytes 4325376 | tf_op jit(solution)/shard_map/all_gather | solution.py:45
  12.7 5.5 %copy-start.5 = (s32[1,8]{1,0:T(1,128)S(1)}, s32[1,8]{1,0:T(1,128)}, u32[]{:S(2)}) copy-start(s32[1,8]{1,0:T(1,128)} %param.11) | copy-start | bytes 100
  12.7 5.6 %copy-start.2 = (bf16[1,1024,1024]{2,1,0:T(8,128)(2,1)S(1)}, bf16[1,1024,1024]{2,1,0:T(8,128)(2,1)}, u32[]{:S(2)}) copy-start(bf16[1,1024,1024]{2,1,0:T(8,128)(2,1)} %param.9) | copy-start | bytes 6291460
  18.2 1.0 copy-start.4
  25.0 4.4 %copy-start.6 = (u32[32]{0:T(128)S(1)}, u32[32]{0:T(128)}, u32[]{:S(2)}) copy-start(u32[32]{0:T(128)} %constant.149) | copy-start | bytes 388
  25.0 33.9 %all-to-all-start = ((bf16[8,128,1024]{2,0,1:T(8,128)(2,1)}), bf16[8,128,1024]{2,0,1:T(8,128)(2,1)S(1)}, u32[]{:S(2)}, u32[]{:S(2)}) async-start(bf16[8,128,1024]{2,0,1:T(8,128)(2,1)} %copy.14), calls=%async_computation | async-start | bytes 4194304 | tf_op jit(solution)/shard_map/all_to_all | solution.py:113
  63.9 37.3 %copy-start.3 = (bf16[32,32,1024]{2,1,0:T(8,128)(2,1)}, bf16[32,32,1024]{2,1,0:T(8,128)(2,1)S(1)}, u32[]{:S(2)}) copy-start(bf16[32,32,1024]{2,1,0:T(8,128)(2,1)S(1)} %fusion.1) | copy-start | bytes 6291460
  175.3 55.8 %collective-permute-start.4 = (bf16[1024,1024]{1,0:T(8,128)(2,1)}, bf16[1024,1024]{1,0:T(8,128)(2,1)}, u32[]{:S(2)}, u32[]{:S(2)}) collective-permute-start(bf16[1024,1024]{1,0:T(8,128)(2,1)} %pad_dynamic-slice_fusion.1), channel_id=1, source_target_pairs={{4,0},{8,4},{12,8},{16,12},{20,16},{24,20},{28,24},{5,1},{9,5},{13... | collective-permute-start | bytes 6291464 | tf_op jit(solution)/shard_map/ppermute | solution.py:24
  176.7 48.6 %collective-permute-start = (s32[1024]{0:T(1024)S(1)}, s32[1024]{0:T(1024)S(1)}, u32[]{:S(2)}, u32[]{:S(2)}) collective-permute-start(s32[1024]{0:T(1024)S(1)} %pad_dynamic-slice_fusion.3), channel_id=1, source_target_pairs={{4,0},{8,4},{12,8},{16,12},{20,16},{24,20},{28,24},{5,1},{9,5},{13... | collective-permute-start | bytes 12296 | tf_op jit(solution)/shard_map/ppermute | solution.py:24
  225.5 5.6 %collective-permute-start.1 = (s32[1024]{0:T(1024)S(1)}, s32[1024]{0:T(1024)S(1)}, u32[]{:S(2)}, u32[]{:S(2)}) collective-permute-start(s32[1024]{0:T(1024)S(1)} %broadcast_select_fusion.5), channel_id=1, source_target_pairs={{4,0},{8,4},{12,8},{16,12},{20,16},{24,20},{28,24},{5,1},{9,5},{13... | collective-permute-start | bytes 12296 | tf_op jit(solution)/shard_map/ppermute | solution.py:24
  234.1 49.0 %collective-permute-start.5 = (bf16[1024,1024]{1,0:T(8,128)(2,1)S(1)}, bf16[1024,1024]{1,0:T(8,128)(2,1)S(1)}, u32[]{:S(2)}, u32[]{:S(2)}) collective-permute-start(bf16[1024,1024]{1,0:T(8,128)(2,1)S(1)} %broadcast_select_fusion), channel_id=1, source_target_pairs={{4,0},{8,4},{12,8},{16,12},{20,16},{24,20},{28,24},{5,1},{9,5},{13... | collective-permute-start | bytes 6291464 | tf_op jit(solution)/shard_map/ppermute | solution.py:24
  286.8 47.3 %collective-permute-start.6 = (bf16[1024,1024]{1,0:T(8,128)(2,1)S(1)}, bf16[1024,1024]{1,0:T(8,128)(2,1)S(1)}, u32[]{:S(2)}, u32[]{:S(2)}) collective-permute-start(bf16[1024,1024]{1,0:T(8,128)(2,1)S(1)} %get-tuple-element.99), channel_id=1, source_target_pairs={{8,0},{12,4},{16,8},{20,12},{24,16},{28,20},{9,1},{13,5},{17,9},{2... | collective-permute-start | bytes 6291464 | tf_op jit(solution)/shard_map/ppermute | solution.py:24
  288.1 45.9 %collective-permute-start.2 = (s32[1024]{0:T(1024)S(1)}, s32[1024]{0:T(1024)S(1)}, u32[]{:S(2)}, u32[]{:S(2)}) collective-permute-start(s32[1024]{0:T(1024)S(1)} %broadcast_select_fusion.3), channel_id=1, source_target_pairs={{8,0},{12,4},{16,8},{20,12},{24,16},{28,20},{9,1},{13,5},{17,9},{2... | collective-permute-start | bytes 12296 | tf_op jit(solution)/shard_map/ppermute | solution.py:24
  335.0 92.2 %collective-permute-start.7 = (bf16[1024,1024]{1,0:T(8,128)(2,1)S(1)}, bf16[1024,1024]{1,0:T(8,128)(2,1)S(1)}, u32[]{:S(2)}, u32[]{:S(2)}) collective-permute-start(bf16[1024,1024]{1,0:T(8,128)(2,1)S(1)} %broadcast_select_fusion.2), channel_id=1, source_target_pairs={{16,0},{20,4},{24,8},{28,12},{17,1},{21,5},{25,9},{29,13},{18,2},{... | collective-permute-start | bytes 6291464 | tf_op jit(solution)/shard_map/ppermute | solution.py:24
  336.3 90.9 %collective-permute-start.3 = (s32[1024]{0:T(1024)S(1)}, s32[1024]{0:T(1024)S(1)}, u32[]{:S(2)}, u32[]{:S(2)}) collective-permute-start(s32[1024]{0:T(1024)S(1)} %get-tuple-element.93), channel_id=1, source_target_pairs={{16,0},{20,4},{24,8},{28,12},{17,1},{21,5},{25,9},{29,13},{18,2},{... | collective-permute-start | bytes 12296 | tf_op jit(solution)/shard_map/ppermute | solution.py:24
  427.2 2.6 copy-start.1
Sparse Core Ops, SparseCore 0:
  10.3 81.9 all-gather.2
  95.1 60.5 all-gather.4
where the time goes:
time: 437 us
  waiting for transfers between devices  324 us (74%)
  matrix products  33 us (8%)
  local copies, waits for them, and re-layouts  17.6 us (4%)
  other arithmetic  15.7 us (4%)
  starting transfers between devices  14.8 us (3%)
  between operations  14.3 us (3%)
  blocking collectives  12.7 us (3%)
  loops' own time  4.86 us (1%)
    ppermute x8, waiting for transfers between devices, from_behind(): return lax.ppermute(value, axis, pairs)  234 us
    all_gather x1, waiting for transfers between devices, channel_mlp(): lax.all_gather(w_down, ('page', 'tok'), axis=1, tiled=True)  54.6 us
    all_gather x1, waiting for transfers between devices, channel_mlp(): shard_part = lax.all_gather(w_gate_up, ('page', 'tok'), axis=2, tiled=True)  28.4 us
    dot_general x1, matrix products, channel_mlp(): jnp.dot(hidden, lax.all_gather(w_down, ('page', 'tok'), axis=1, tiled=Tru...  16.6 us
    unnamed x1, blocking collectives  12.7 us
    ppermute x8, starting transfers between devices, from_behind(): return lax.ppermute(value, axis, pairs)  10.3 us
    dot_general x1, matrix products, channel_mlp(): jnp.dot(normed_two, shard_part[0], preferred_element_type=jnp.float32)  8.88 us
  transfers between devices with their start and end apart: 11, of which 8 were waited for; matrix products, arithmetic and copies ran while one was open for 8% of the time, Pallas kernels for 0%

commit v1 on v0

--- a/solution.py
+++ b/solution.py
@@ -1,6 +1,10 @@
+import functools
+
 import jax
 import jax.numpy as jnp
 from jax import lax
+from jax.experimental import pallas as pl
+from jax.experimental.pallas import tpu as pltpu
 from jax.sharding import PartitionSpec as P
 
 epsilon = 1e-05
@@ -119,9 +123,359 @@
     return packed.reshape(1, row_count, feat_width)
 
 
+SMEM = pl.BlockSpec(memory_space=pltpu.SMEM)
+VMEM = pl.BlockSpec(memory_space=pltpu.VMEM)
+ANY = pl.BlockSpec(memory_space=pl.ANY)
+VMEM_LIMIT = 56 * 1024 * 1024
+
+
+def params():
+    return pltpu.CompilerParams(vmem_limit_bytes=VMEM_LIMIT)
+
+
+def live_rows(start, rows, length, occupied):
+    ids = start + lax.broadcasted_iota(jnp.int32, (rows, 1), 0)
+    return (ids < length) & (occupied > 0)
+
+
+def first_kernel(ids_ref, length_ref, occ_ref, tile_ref, mix_ref, *out_refs):
+    block = pl.program_id(0)
+    blk_size = tile_ref.shape[1]
+    rows_here = pl.num_programs(0) * blk_size
+    start = ids_ref[1] * rows_here + block * blk_size
+    live = live_rows(start, blk_size, length_ref[0], occ_ref[0, block])
+    masked = jnp.where(live, tile_ref[0].astype(jnp.float32), 0.0)
+    normed = rms_round(masked)
+    first = jnp.dot(mix_ref[0], normed, preferred_element_type=jnp.float32).astype(jnp.bfloat16)
+    parts, _, share, width = out_refs[0].shape
+    for half, out_ref in enumerate(out_refs):
+        for part in range(parts):
+            out_ref[part, 0] = first[part * share:(part + 1) * share, half * width:(half + 1) * width]
+
+
+def first_factor(ids, length, occupancy, tile_tokens, block_mix, parts, halves):
+    blocks, blk_size, _ = block_mix.shape
+    feat_width = tile_tokens.shape[2]
+    share, width = blk_size // parts, feat_width // halves
+    return pl.pallas_call(
+        first_kernel,
+        grid=(blocks,),
+        in_specs=[
+            SMEM,
+            SMEM,
+            SMEM,
+            pl.BlockSpec((1, blk_size, feat_width), lambda b: (0, b, 0)),
+            pl.BlockSpec((1, blk_size, blk_size), lambda b: (b, 0, 0)),
+        ],
+        out_specs=[pl.BlockSpec((parts, 1, share, width), lambda b: (0, b, 0, 0))] * halves,
+        out_shape=[jax.ShapeDtypeStruct((parts, blocks, share, width), jnp.bfloat16)] * halves,
+        compiler_params=params(),
+        name="first_factor",
+    )(ids, length, occupancy, tile_tokens, block_mix)
+
+
+GROUP = 16
+SUB = 8
+
+
+def spread_kernel(stride_ref, out_ref):
+    spots, outs, ins = stride_ref.shape
+    rows, cols = GROUP * outs, GROUP * ins
+    picks = lax.broadcasted_iota(jnp.int32, (ins, cols), 1) // GROUP
+    picks = picks == lax.broadcasted_iota(jnp.int32, (ins, cols), 0)
+    picks = picks.astype(jnp.float32).astype(jnp.bfloat16)
+    spot_row = lax.broadcasted_iota(jnp.int32, (rows, cols), 0) // outs
+    spot_col = lax.broadcasted_iota(jnp.int32, (rows, cols), 1) % GROUP
+    for group in range(spots // GROUP):
+        flat = stride_ref[group * GROUP:(group + 1) * GROUP].reshape(rows, ins)
+        wide = jnp.dot(flat, picks, preferred_element_type=jnp.float32)
+        out_ref[group] = jnp.where(spot_row == spot_col, wide, 0.0).astype(jnp.bfloat16)
+
+
+def spread_stride(stride_mix):
+    spots, outs, ins = stride_mix.shape
+    return pl.pallas_call(
+        spread_kernel,
+        in_specs=[VMEM],
+        out_specs=VMEM,
+        out_shape=jax.ShapeDtypeStruct((spots // GROUP, GROUP * outs, GROUP * ins), jnp.bfloat16),
+        compiler_params=params(),
+        name="spread_stride",
+    )(stride_mix)
+
+
+def kept_of(length, lane, rows):
+    return jnp.clip(length - lane * rows, 0, rows)
+
+
+def offset_of(lengths_ref, page, lane, rows):
+    total = jnp.int32(0)
+    for earlier in range(lengths_ref.shape[0]):
+        total += jnp.where(earlier < page, kept_of(lengths_ref[earlier], lane, rows), 0)
+    return total
+
+
+def second_kernel(ids_ref, lengths_ref, occ_ref, spread_ref, first_ref, tile_ref, *refs):
+    out_refs, twice_ref = refs[:-1], refs[-1]
+    rows, width = tile_ref.shape[1:]
+    page, lane = ids_ref[0], ids_ref[1]
+    length = lengths_ref[page]
+    groups, group_rows, depth = spread_ref.shape
+    blocks = occ_ref.shape[1]
+    blk_size = rows // blocks
+    for group in range(groups):
+        values = first_ref[:, group * GROUP:(group + 1) * GROUP, :].reshape(depth, width)
+        second = jnp.dot(spread_ref[group], values, preferred_element_type=jnp.float32)
+        for part in range(group_rows // blk_size):
+            at = group * group_rows + part * blk_size
+            live = live_rows(lane * rows + at, blk_size, length, occ_ref[0, at // blk_size])
+            masked = jnp.where(live, tile_ref[0, at:at + blk_size, :].astype(jnp.float32), 0.0)
+            mixed = masked + second[part * blk_size:(part + 1) * blk_size]
+            mixed = mixed.astype(jnp.bfloat16).astype(jnp.float32)
+            twice_ref[at:at + blk_size, :] = mixed
+            twice_ref[rows + at:rows + at + blk_size, :] = mixed
+    shift = offset_of(lengths_ref, page, lane, rows) % rows
+    start = rows - shift
+    extra = start % SUB
+    base = pl.multiple_of(start - extra, SUB)
+    tall = twice_ref[pl.ds(base, rows + SUB), :].reshape(rows // SUB + 1, SUB, width)
+    tall = pltpu.roll(tall, (SUB - extra) % SUB, 1)
+    inside = lax.broadcasted_iota(jnp.int32, (1, SUB, 1), 1) + extra < SUB
+    turned = jnp.where(inside, tall[:-1], tall[1:]).reshape(rows, width).astype(jnp.bfloat16)
+    for part, out_ref in enumerate(out_refs):
+        span = out_ref.shape[1]
+        out_ref[...] = turned[:, part * span:(part + 1) * span]
+
+
+def second_factor(half, pieces, ids, lengths, occupancy, spread, first, tile_tokens):
+    rows = tile_tokens.shape[1]
+    width = first.shape[2]
+    return pl.pallas_call(
+        second_kernel,
+        grid=(1,),
+        in_specs=[
+            SMEM,
+            SMEM,
+            SMEM,
+            VMEM,
+            VMEM,
+            pl.BlockSpec((1, rows, width), lambda i: (0, 0, half)),
+        ],
+        out_specs=[VMEM] * pieces,
+        out_shape=[jax.ShapeDtypeStruct((rows, width // pieces), jnp.bfloat16)] * pieces,
+        scratch_shapes=[pltpu.VMEM((2 * rows + SUB, width), jnp.float32)],
+        compiler_params=params(),
+        name="second_factor",
+    )(ids, lengths, occupancy, spread, first, tile_tokens)
+
+
+def parity_kernel(ids_ref, lengths_ref, own_ref, got_ref, out_ref):
+    rows = own_ref.shape[0]
+    page, lane = ids_ref[0], ids_ref[1]
+    offset = offset_of(lengths_ref, page, lane, rows)
+    kept = kept_of(lengths_ref[page], lane, rows)
+    slot = lax.broadcasted_iota(jnp.int32, (rows, 1), 0)
+    base = offset // rows
+    shift = offset % rows
+    late = slot < shift
+    row = jnp.where(late, slot + rows, slot) - shift
+    target = jnp.where(late, base + 1, base)
+    mine = (row < kept) & (target % 2 == page % 2)
+    out_ref[...] = jnp.where(mine, own_ref[...], got_ref[...])
+
+
+def join_parity(ids, lengths, own, got):
+    return pl.pallas_call(
+        parity_kernel,
+        in_specs=[SMEM, SMEM, VMEM, VMEM],
+        out_specs=VMEM,
+        out_shape=jax.ShapeDtypeStruct(own.shape, own.dtype),
+        compiler_params=params(),
+        name="join_parity",
+    )(ids, lengths, own, got)
+
+
+def forward_kernel(ids_ref, lengths_ref, own_ref, one_ref, two_ref, out_ref):
+    rows = own_ref.shape[0]
+    page, lane = ids_ref[0], ids_ref[1]
+    level = page // 2
+    slot = (page % 2) * rows + lax.broadcasted_iota(jnp.int32, (rows, 1), 0)
+    after_one = offset_of(lengths_ref, 2 * level + 2, lane, rows)
+    after_two = offset_of(lengths_ref, 2 * level + 4, lane, rows)
+    value = jnp.where(slot < after_two, one_ref[...], two_ref[...])
+    out_ref[...] = jnp.where(slot < after_one, own_ref[...], value)
+
+
+def forward_merge(ids, lengths, own, one, two):
+    return pl.pallas_call(
+        forward_kernel,
+        in_specs=[SMEM, SMEM, VMEM, VMEM, VMEM],
+        out_specs=VMEM,
+        out_shape=jax.ShapeDtypeStruct(own.shape, own.dtype),
+        compiler_params=params(),
+        name="forward_merge",
+    )(ids, lengths, own, one, two)
+
+
+def mlp_kernel(pieces, ids_ref, lengths_ref, *refs):
+    sources, refs = refs[:4 * pieces], refs[4 * pieces:]
+    weights, out_ref, refs = refs[:4], refs[4], refs[5:]
+    gate_ref, up_ref, low_ref, high_ref, sems = refs
+    step = pl.program_id(0)
+    rows = out_ref.shape[1]
+    page, lane = ids_ref[0], ids_ref[1]
+    core = lane % 2
+
+    @pl.when(step == 0)
+    def _():
+        copies = []
+        for side, main_ref, down_ref in ((0, gate_ref, low_ref), (1, up_ref, high_ref)):
+            for other in range(2):
+                src = weights[2 * side + other]
+                where = core if other == 0 else 1 - core
+                half = src.shape[0]
+                wide = main_ref.shape[0] // (2 * half)
+                thin = down_ref.shape[0] // (2 * half)
+                main = main_ref.reshape(half, 2, wide, main_ref.shape[1])
+                down = down_ref.reshape(half, 2, thin, down_ref.shape[1])
+                copies.append(pltpu.make_async_copy(src.at[:, :wide], main.at[:, where], sems.at[4 * side + 2 * other]))
+                copies.append(pltpu.make_async_copy(src.at[:, wide:], down.at[:, where], sems.at[4 * side + 2 * other + 1]))
+        for copy in copies:
+            copy.start()
+        for copy in copies:
+            copy.wait()
+
+    lane_rows = rows * pl.num_programs(0)
+    slot = page * lane_rows + step * rows + lax.broadcasted_iota(jnp.int32, (rows, 1), 0)
+    level = page // 2
+    ends = [offset_of(lengths_ref, 2 * (level + ahead), lane, lane_rows) for ahead in (1, 2)]
+    total = offset_of(lengths_ref, lengths_ref.shape[0], lane, lane_rows)
+    last_level = level == 0
+    chunks = []
+    for piece in range(pieces):
+        own, one, two, last = (ref[...].astype(jnp.float32) for ref in sources[4 * piece:4 * piece + 4])
+        far = jnp.where(last_level, last, jnp.where(slot < ends[1], one, two))
+        value = jnp.where(slot < ends[0], own, far)
+        chunks.append(jnp.where(slot < total, value, 0.0))
+    mixed = jnp.concatenate(chunks, axis=1)
+    normed = rms_round(mixed)
+    contract = (((1,), (1,)), ((), ()))
+    depth = low_ref.shape[1]
+    count = 4
+    span = gate_ref.shape[0] // count
+    result = mixed
+    for part in range(count):
+        at = part * span
+        gate = lax.dot_general(normed, gate_ref[at:at + span, :], contract, preferred_element_type=jnp.float32)
+        up = lax.dot_general(normed, up_ref[at:at + span, :], contract, preferred_element_type=jnp.float32)
+        hidden = (gate / (1.0 + jnp.exp(-gate)) * up).astype(jnp.bfloat16)
+        down_ref = low_ref if at < depth else high_ref
+        inner = at % depth
+        result += lax.dot_general(hidden, down_ref[:, inner:inner + span], contract, preferred_element_type=jnp.float32)
+    out_ref[0] = result.astype(out_ref.dtype)
+
+
+def packed_mlp(ids, lengths, sources, weights, feat_width, hidden_width):
+    rows, span = sources[0].shape
+    pieces = len(sources) // 4
+    steps = 4
+    block = rows // steps
+    depth = weights[0].shape[2]
+    return pl.pallas_call(
+        functools.partial(mlp_kernel, pieces),
+        grid=(steps,),
+        in_specs=[SMEM, SMEM] + [pl.BlockSpec((block, span), lambda i: (i, 0))] * len(sources) + [ANY] * 4,
+        out_specs=pl.BlockSpec((1, block, feat_width), lambda i: (0, i, 0)),
+        out_shape=jax.ShapeDtypeStruct((1, rows, feat_width), jnp.bfloat16),
+        scratch_shapes=[
+            pltpu.VMEM((hidden_width, feat_width), jnp.bfloat16),
+            pltpu.VMEM((hidden_width, feat_width), jnp.bfloat16),
+            pltpu.VMEM((feat_width, depth), jnp.bfloat16),
+            pltpu.VMEM((feat_width, depth), jnp.bfloat16),
+            pltpu.SemaphoreType.DMA((8,)),
+        ],
+        compiler_params=params(),
+        name="packed_mlp",
+    )(ids, lengths, *sources, *weights)
+
+
+def swap(value, axis, bit):
+    return lax.ppermute(value, axis, [(i, i ^ bit) for i in range(lax.axis_size(axis))])
+
+
+def both_orders(value, got, bit, place):
+    low = jnp.stack([value, got], place)
+    high = jnp.stack([got, value], place)
+    return jnp.where(bit == 0, low, high)
+
+
+def gather_weights(w_gate_up, w_down):
+    page, tok = lax.axis_index("page"), lax.axis_index("tok")
+    pages = lax.axis_size("page")
+    gate_up = jnp.swapaxes(w_gate_up, 1, 2)
+    down = jnp.swapaxes(w_down, 0, 1)
+    depth = gate_up.shape[2]
+    own = jnp.concatenate([gate_up[0], down[:, :depth], gate_up[1], down[:, depth:]], 0)
+    up_pairs = [(i, i + 2) for i in range(pages - 2)]
+    down_pairs = [(i + 2, i) for i in range(pages - 2)]
+    below, above = [own], [own]
+    for _ in range(pages // 2 - 1):
+        below.append(lax.ppermute(below[-1], "page", up_pairs))
+        above.append(lax.ppermute(above[-1], "page", down_pairs))
+    line = jnp.stack(below[:0:-1] + [own] + above[1:], 0)
+    level = page // 2
+    column = lax.dynamic_slice_in_dim(line, pages // 2 - 1 - level, pages // 2, 0)
+    half = own.shape[0] // 2
+    one, two = column[:, :half], column[:, half:]
+    one = both_orders(one, swap(one, "page", 1), page % 2, 1)
+    two = both_orders(two, swap(two, "tok", 2), tok // 2, 1)
+    one = both_orders(one, swap(one, "tok", 2), tok // 2, 2)
+    two = both_orders(two, swap(two, "page", 1), page % 2, 1)
+    one = one.reshape((-1,) + one.shape[3:])
+    two = two.reshape((-1,) + two.shape[3:])
+    return [one, swap(one, "tok", 1), two, swap(two, "tok", 1)]
+
+
+def all_lengths(length):
+    pages = lax.axis_size("page")
+    lengths = jnp.where(jnp.arange(pages) == lax.axis_index("page"), length, 0)
+    bit = 1
+    while bit < pages:
+        lengths = lengths + swap(lengths, "page", bit)
+        bit *= 2
+    return lengths
+
+
+def packed_device(tile_tokens, page_lengths, occupancy, block_mix, stride_mix, w_gate_up, w_down):
+    ids = jnp.stack([lax.axis_index("page"), lax.axis_index("tok")]).astype(jnp.int32)
+    parts = lax.axis_size("tok")
+    pages = lax.axis_size("page")
+    feat_width = tile_tokens.shape[2]
+    weights = gather_weights(w_gate_up, w_down)
+    halves, pieces = 2, 2
+    firsts = first_factor(ids, page_lengths, occupancy, tile_tokens, block_mix, parts, halves)
+    lengths = all_lengths(page_lengths[0])
+    spread = spread_stride(stride_mix)
+    sources = []
+    for half, first in enumerate(firsts):
+        got = lax.all_to_all(first, "tok", split_axis=0, concat_axis=0)
+        got = got.reshape((-1,) + got.shape[2:])
+        turned = second_factor(half, pieces, ids, lengths, occupancy, spread, got, tile_tokens)
+        for own in turned:
+            current = join_parity(ids, lengths, own, swap(own, "page", 1))
+            one = lax.ppermute(current, "page", [(i, i - 2) for i in range(pages // 2, pages)])
+            two = lax.ppermute(current, "page", [(i, i - 4) for i in range(pages - 2, pages)])
+            merged = forward_merge(ids, lengths, current, one, two)
+            last = lax.ppermute(merged, "page", [(i, i - 2) for i in range(2, 4)])
+            sources += [current, one, two, last]
+    hidden_width = w_down.shape[0]
+    return packed_mlp(ids, lengths, sources, weights, feat_width, hidden_width)
+
+
 def solution(mesh):
+    pages, parts = mesh.shape["page"], mesh.shape["tok"]
     return jax.shard_map(
-        per_device,
+        packed_device if (pages, parts) == (8, 4) else per_device,
         mesh=mesh,
         in_specs=(
             P("page", "tok", None),

time: 437 us -> 292 us (0.67)
  waiting for transfers between devices: 324 us -> 163 us
  Pallas kernels: 0 us -> 60.6 us
  starting transfers between devices: 14.8 us -> 50.5 us
  matrix products: 33 us -> 0 us
  between operations: 14.3 us -> 1.36 us
  blocking collectives: 12.7 us -> 0 us
  local copies, waits for them, and re-layouts: 17.6 us -> 6.03 us
  other arithmetic: 15.7 us -> 9.3 us
  loops' own time: 4.86 us -> 0 us
    all_gather x2 -> x0, waiting for transfers between devices: 83 us -> none  [the longest x1 54.6 us: channel_mlp(): lax.all_gather(w_down, ('page', 'tok'), axis=1, tiled=True)]
    ppermute x8 -> x31, waiting for transfers between devices: 234 us -> 157 us  [the longest x4 76.2 us: packed_device(): last = lax.ppermute(merged, 'page', [(i, i - 2) for i in range(2, 4)])]
    pallas_call x0 -> x13, Pallas kernels: none -> 60.6 us  [the longest x1 24.5 us: packed_mlp(): pl.pallas_call(functools.partial(mlp_kernel, pieces), grid=(steps,), in_s...]
    dot_general x4 -> x0, matrix products: 33 us -> none  [the longest x1 16.6 us: channel_mlp(): jnp.dot(hidden, lax.all_gather(w_down, ('page', 'tok'), axis=1, tiled=Tru...]
    ppermute x8 -> x31, starting transfers between devices: 10.3 us -> 42.8 us  [the longest x13 14.3 us: swap(): lax.ppermute(value, axis, [(i, i ^ bit) for i in range(lax.axis_size(axis...]
    unnamed x1 -> x0, blocking collectives: 12.7 us -> none
    convert_element_type x2 -> x0, local copies, waits for them, and re-layouts: 8.37 us -> none  [the longest x1 5.46 us: per_device(): tile_tokens[0].astype(jnp.float32)]
    dynamic_slice x9 -> x0, local copies, waits for them, and re-layouts: 7.56 us -> none  [the longest x7 4.53 us: hop(): longer = join(so_far, pieces[position])]
  transfers between devices with their start and end apart: 11 -> 33, of which waited for: 8 -> 17; matrix products, arithmetic and copies ran while one was open for 8% -> 4% of each run, Pallas kernels for 0% -> 12%
where the time goes in v1:
time: 292 us; the launch traced here: 291 us
  waiting for transfers between devices  163 us (56%)
  Pallas kernels  60.6 us (21%)
  starting transfers between devices  50.5 us (17%)
  other arithmetic  9.3 us (3%)
  local copies, waits for them, and re-layouts  6.03 us (2%)
    ppermute x4, waiting for transfers between devices, packed_device(): last = lax.ppermute(merged, 'page', [(i, i - 2) for i in range(2, 4)])  76.2 us
    ppermute x13, waiting for transfers between devices, swap(): lax.ppermute(value, axis, [(i, i ^ bit) for i in range(lax.axis_size(axis...  58.7 us
    pallas_call x1, Pallas kernels, packed_mlp(): pl.pallas_call(functools.partial(mlp_kernel, pieces), grid=(steps,), in_s...  24.5 us
    ppermute x3, waiting for transfers between devices, gather_weights(): below.append(lax.ppermute(below[-1], 'page', up_pairs))  18.4 us
    ppermute x13, starting transfers between devices, swap(): lax.ppermute(value, axis, [(i, i ^ bit) for i in range(lax.axis_size(axis...  14.3 us
    ppermute x3, starting transfers between devices, gather_weights(): below.append(lax.ppermute(below[-1], 'page', up_pairs))  13.7 us
    pallas_call x4, Pallas kernels, join_parity(): pl.pallas_call(parity_kernel, in_specs=[SMEM, SMEM, VMEM, VMEM], out_spec...  9.74 us
    pallas_call x4, Pallas kernels, forward_merge(): pl.pallas_call(forward_kernel, in_specs=[SMEM, SMEM, VMEM, VMEM, VMEM], o...  9.37 us
  transfers between devices with their start and end apart: 33, of which 17 were waited for; matrix products, arithmetic and copies ran while one was open for 4% of the time, Pallas kernels for 12%

profile of v1, /device:TPU:0, one launch (start us, length us, event | category | flops | bytes accessed | tf_op | source)
XLA Modules:
  0.0 290.7 jit_solution(5237095335138361074)
XLA Ops:
  1.9 5.0 %collective-permute-start.19 = (bf16[192,1024]{1,0:T(8,128)(2,1)S(1)}, bf16[192,1024]{1,0:T(8,128)(2,1)S(1)}, u32[]{:S(2)}, u32[]{:S(2)}) collective-permute-start(bf16[192,1024]{1,0:T(8,128)(2,1)S(1)} %pad_maximum_fusion), channel_id=1, source_target_pairs={{0,8},{4,12},{8,16},{12,20},{16,24},{20,28},{1,9},{5,13},{9,17},{1... | collective-permute-start | bytes 1179656 | tf_op jit(solution)/shard_map/ppermute | solution.py:423
  8.2 7.0 %collective-permute-done.19 = bf16[192,1024]{1,0:T(8,128)(2,1)S(1)} collective-permute-done((bf16[192,1024]{1,0:T(8,128)(2,1)S(1)}, bf16[192,1024]{1,0:T(8,128)(2,1)S(1)}, u32[]{:S(2)}, u32[]{:S(2)}) %collective-permute-start.19) | collective-permute-done | bytes 393248 | tf_op jit(solution)/shard_map/ppermute | solution.py:423
  15.2 4.4 %collective-permute-start.20 = (bf16[192,1024]{1,0:T(8,128)(2,1)S(1)}, bf16[192,1024]{1,0:T(8,128)(2,1)S(1)}, u32[]{:S(2)}, u32[]{:S(2)}) collective-permute-start(bf16[192,1024]{1,0:T(8,128)(2,1)S(1)} %collective-permute-done.19), channel_id=1, source_target_pairs={{0,8},{4,12},{8,16},{12,20},{16,24},{20,28},{1,9},{5,13},{9,17},{1... | collective-permute-start | bytes 1179656 | tf_op jit(solution)/shard_map/ppermute | solution.py:423
  20.9 6.1 %collective-permute-done.20 = bf16[192,1024]{1,0:T(8,128)(2,1)S(1)} collective-permute-done((bf16[192,1024]{1,0:T(8,128)(2,1)S(1)}, bf16[192,1024]{1,0:T(8,128)(2,1)S(1)}, u32[]{:S(2)}, u32[]{:S(2)}) %collective-permute-start.20) | collective-permute-done | bytes 393248 | tf_op jit(solution)/shard_map/ppermute | solution.py:423
  27.1 4.4 %collective-permute-start.21 = (bf16[192,1024]{1,0:T(8,128)(2,1)S(1)}, bf16[192,1024]{1,0:T(8,128)(2,1)S(1)}, u32[]{:S(2)}, u32[]{:S(2)}) collective-permute-start(bf16[192,1024]{1,0:T(8,128)(2,1)S(1)} %collective-permute-done.20), channel_id=1, source_target_pairs={{0,8},{4,12},{8,16},{12,20},{16,24},{20,28},{1,9},{5,13},{9,17},{1... | collective-permute-start | bytes 1179656 | tf_op jit(solution)/shard_map/ppermute | solution.py:423
  32.8 5.2 %collective-permute-done.21 = bf16[192,1024]{1,0:T(8,128)(2,1)S(1)} collective-permute-done((bf16[192,1024]{1,0:T(8,128)(2,1)S(1)}, bf16[192,1024]{1,0:T(8,128)(2,1)S(1)}, u32[]{:S(2)}, u32[]{:S(2)}) %collective-permute-start.21) | collective-permute-done | bytes 393248 | tf_op jit(solution)/shard_map/ppermute | solution.py:423
  38.2 4.0 %collective-permute-done.24 = bf16[192,1024]{1,0:T(8,128)(2,1)S(1)} collective-permute-done((bf16[192,1024]{1,0:T(8,128)(2,1)S(1)}, bf16[192,1024]{1,0:T(8,128)(2,1)S(1)}, u32[]{:S(2)}, u32[]{:S(2)}) %collective-permute-start.24) | collective-permute-done | bytes 393248 | tf_op jit(solution)/shard_map/ppermute | solution.py:424
  45.5 13.3 %collective-permute-done.28 = bf16[4,96,1024]{2,1,0:T(8,128)(2,1)S(1)} collective-permute-done((bf16[4,96,1024]{2,1,0:T(8,128)(2,1)S(1)}, bf16[4,96,1024]{2,1,0:T(8,128)(2,1)S(1)}, u32[]{:S(2)}, u32[]{:S(2)}) %collective-permute-start.28) | collective-permute-done | bytes 786464 | tf_op jit(solution)/shard_map/ppermute | solution.py:403
  65.9 7.0 %first_factor.1 = (bf16[4,8,32,512]{3,2,1,0:T(8,128)(2,1)}, bf16[4,8,32,512]{3,2,1,0:T(8,128)(2,1)}) custom-call(s32[2]{0:T(128)} %pad_add_fusion.ids_ref, s32[1]{0:T(128)} %copy.16.length_ref, s32[1,8]{1,0:T(1,128)} %occ_ref.5, bf16[1,1024,1024]{2,1,0:T(8,128)(2,1)} %tile_ref.5, bf16[8,128,128]{2,1,0:T(8,128)(2,1)} %mix_ref.1), custom_call_target="tpu_custom_call" | custom-call | tf_op jit(solution)/shard_map/first_factor/pallas_call | solution.py:160
  72.9 3.5 %all-to-all-start.1 = ((bf16[4,8,32,512]{3,2,1,0:T(8,128)(2,1)}), bf16[4,8,32,512]{3,2,1,0:T(8,128)(2,1)S(1)}, u32[]{:S(2)}, u32[]{:S(2)}) async-start(bf16[4,8,32,512]{3,2,1,0:T(8,128)(2,1)} %get-tuple-element.14), calls=%async_computation.1 | async-start | bytes 2097152 | tf_op jit(solution)/shard_map/all_to_all | solution.py:461
  79.4 14.4 %collective-permute-done = s32[8]{0:T(128)S(1)} collective-permute-done((s32[8]{0:T(128)S(1)}, s32[8]{0:T(128)S(1)}, u32[]{:S(2)}, u32[]{:S(2)}) %collective-permute-start) | collective-permute-done | bytes 64 | tf_op jit(solution)/shard_map/ppermute | solution.py:403
  97.4 2.6 collective-permute-start.2
  102.3 4.1 %all-to-all-done.1 = bf16[4,8,32,512]{3,2,1,0:T(8,128)(2,1)S(1)} async-done(((bf16[4,8,32,512]{3,2,1,0:T(8,128)(2,1)}), bf16[4,8,32,512]{3,2,1,0:T(8,128)(2,1)S(1)}, u32[]{:S(2)}, u32[]{:S(2)}) %all-to-all-start.1) | async-done | bytes 1048608 | tf_op jit(solution)/shard_map/all_to_all | solution.py:461
  106.5 4.3 %all-to-all-start = ((bf16[4,8,32,512]{3,2,1,0:T(8,128)(2,1)}), bf16[4,8,32,512]{3,2,1,0:T(8,128)(2,1)}, u32[]{:S(2)}, u32[]{:S(2)}) async-start(bf16[4,8,32,512]{3,2,1,0:T(8,128)(2,1)} %get-tuple-element.11), calls=%async_computation | async-start | bytes 2097152 | tf_op jit(solution)/shard_map/all_to_all | solution.py:461
  110.7 3.9 %second_factor.3 = (bf16[1024,256]{1,0:T(8,128)(2,1)}, bf16[1024,256]{1,0:T(8,128)(2,1)}) custom-call(s32[2]{0:T(128)} %pad_add_fusion.ids_ref, s32[8]{0:T(128)} %add.22.lengths_ref, s32[1,8]{1,0:T(1,128)} %occ_ref.5, bf16[2,512,512]{2,1,0:T(8,128)(2,1)} %spread_stride.1.spread_ref, bf16[32,32,512]{2,1,0:T(8,128)(2,1)} %bitcast.46, ...), custom_call_target="tpu_custom_call" | custom-call | tf_op jit(solution)/shard_map/second_factor/pallas_call | solution.py:253
  115.7 2.4 maximum_select_fusion.1
  118.1 2.4 maximum_select_fusion
  121.0 2.4 copy.8
  125.3 3.8 %second_factor.2 = (bf16[1024,256]{1,0:T(8,128)(2,1)}, bf16[1024,256]{1,0:T(8,128)(2,1)}) custom-call(s32[2]{0:T(128)} %pad_add_fusion.ids_ref, s32[8]{0:T(128)} %add.22.lengths_ref, s32[1,8]{1,0:T(1,128)} %occ_ref.5, bf16[2,512,512]{2,1,0:T(8,128)(2,1)} %spread_stride.1.spread_ref, bf16[32,32,512]{2,1,0:T(8,128)(2,1)} %bitcast.3.first_ref, ...), custom_call_target="tpu_custom_call" | custom-call | tf_op jit(solution)/shard_map/second_factor/pallas_call | solution.py:253
  131.6 2.4 join_parity.6.own_ref.refs_8_
  134.1 9.8 %collective-permute-done.15.got_ref = bf16[1024,256]{1,0:T(8,128)(2,1)S(1)} collective-permute-done((bf16[1024,256]{1,0:T(8,128)(2,1)S(1)}, bf16[1024,256]{1,0:T(8,128)(2,1)S(1)}, u32[]{:S(2)}, u32[]{:S(2)}) %collective-permute-start.15) | collective-permute-done | bytes 524320 | tf_op jit(solution)/shard_map/ppermute | solution.py:403
  144.6 10.5 %collective-permute-done.3.got_ref = bf16[1024,256]{1,0:T(8,128)(2,1)S(1)} collective-permute-done((bf16[1024,256]{1,0:T(8,128)(2,1)}, bf16[1024,256]{1,0:T(8,128)(2,1)S(1)}, u32[]{:S(2)}, u32[]{:S(2)}) %collective-permute-start.3) | collective-permute-done | bytes 524320 | tf_op jit(solution)/shard_map/ppermute | solution.py:403
  155.9 2.4 join_parity.7.own_ref.refs_12_
  158.3 6.7 %collective-permute-done.7.got_ref = bf16[1024,256]{1,0:T(8,128)(2,1)S(1)} collective-permute-done((bf16[1024,256]{1,0:T(8,128)(2,1)}, bf16[1024,256]{1,0:T(8,128)(2,1)S(1)}, u32[]{:S(2)}, u32[]{:S(2)}) %collective-permute-start.7) | collective-permute-done | bytes 524320 | tf_op jit(solution)/shard_map/ppermute | solution.py:403
  165.7 2.4 join_parity.4.own_ref.refs_0_
  170.3 2.4 join_parity.5.own_ref.refs_4_
  185.2 2.4 forward_merge.5
  187.5 45.0 %collective-permute-done.14.refs_11_ = bf16[1024,256]{1,0:T(8,128)(2,1)S(1)} collective-permute-done((bf16[1024,256]{1,0:T(8,128)(2,1)}, bf16[1024,256]{1,0:T(8,128)(2,1)S(1)}, u32[]{:S(2)}, u32[]{:S(2)}) %collective-permute-start.14) | collective-permute-done | bytes 524320 | tf_op jit(solution)/shard_map/ppermute | solution.py:469
  233.9 9.9 %collective-permute-done.18.refs_15_ = bf16[1024,256]{1,0:T(8,128)(2,1)S(1)} collective-permute-done((bf16[1024,256]{1,0:T(8,128)(2,1)}, bf16[1024,256]{1,0:T(8,128)(2,1)S(1)}, u32[]{:S(2)}, u32[]{:S(2)}) %collective-permute-start.18) | collective-permute-done | bytes 524320 | tf_op jit(solution)/shard_map/ppermute | solution.py:469
  243.8 11.2 %collective-permute-done.6.refs_3_ = bf16[1024,256]{1,0:T(8,128)(2,1)S(1)} collective-permute-done((bf16[1024,256]{1,0:T(8,128)(2,1)}, bf16[1024,256]{1,0:T(8,128)(2,1)S(1)}, u32[]{:S(2)}, u32[]{:S(2)}) %collective-permute-start.6) | collective-permute-done | bytes 524320 | tf_op jit(solution)/shard_map/ppermute | solution.py:469
  255.0 10.2 %collective-permute-done.10.refs_7_ = bf16[1024,256]{1,0:T(8,128)(2,1)S(1)} collective-permute-done((bf16[1024,256]{1,0:T(8,128)(2,1)}, bf16[1024,256]{1,0:T(8,128)(2,1)S(1)}, u32[]{:S(2)}, u32[]{:S(2)}) %collective-permute-start.10) | collective-permute-done | bytes 524320 | tf_op jit(solution)/shard_map/ppermute | solution.py:469
  266.0 24.5 %packed_mlp.1 = bf16[1,1024,1024]{2,1,0:T(8,128)(2,1)} custom-call(s32[2]{0:T(128)} %pad_add_fusion.ids_ref, s32[8]{0:T(128)} %add.22.lengths_ref, bf16[1024,256]{1,0:T(8,128)(2,1)} %join_parity.4.own_ref.refs_0_, bf16[1024,256]{1,0:T(8,128)(2,1)} %copy-done.9, bf16[1024,256]{1,0:T(8,128)(2,1)} %copy-done.8, bf16[1024,256]{1,0:T(8,128)(2,1)} %copy-done.14, ...), custom_call_target="tpu_custom_call" | custom-call | tf_op jit(solution)/shard_map/packed_mlp/pallas_call | solution.py:384
  (111 shorter events, 49.2 us)
Async XLA Ops:
  1.9 13.3 %collective-permute-start.19 = (bf16[192,1024]{1,0:T(8,128)(2,1)S(1)}, bf16[192,1024]{1,0:T(8,128)(2,1)S(1)}, u32[]{:S(2)}, u32[]{:S(2)}) collective-permute-start(bf16[192,1024]{1,0:T(8,128)(2,1)S(1)} %pad_maximum_fusion), channel_id=1, source_target_pairs={{0,8},{4,12},{8,16},{12,20},{16,24},{20,28},{1,9},{5,13},{9,17},{1... | collective-permute-start | bytes 1179656 | tf_op jit(solution)/shard_map/ppermute | solution.py:423
  6.9 12.7 %collective-permute-start.22 = (bf16[192,1024]{1,0:T(8,128)(2,1)S(1)}, bf16[192,1024]{1,0:T(8,128)(2,1)S(1)}, u32[]{:S(2)}, u32[]{:S(2)}) collective-permute-start(bf16[192,1024]{1,0:T(8,128)(2,1)S(1)} %pad_maximum_fusion), channel_id=1, source_target_pairs={{8,0},{12,4},{16,8},{20,12},{24,16},{28,20},{9,1},{13,5},{17,9},{2... | collective-permute-start | bytes 1179656 | tf_op jit(solution)/shard_map/ppermute | solution.py:424
  15.2 11.9 %collective-permute-start.20 = (bf16[192,1024]{1,0:T(8,128)(2,1)S(1)}, bf16[192,1024]{1,0:T(8,128)(2,1)S(1)}, u32[]{:S(2)}, u32[]{:S(2)}) collective-permute-start(bf16[192,1024]{1,0:T(8,128)(2,1)S(1)} %collective-permute-done.19), channel_id=1, source_target_pairs={{0,8},{4,12},{8,16},{12,20},{16,24},{20,28},{1,9},{5,13},{9,17},{1... | collective-permute-start | bytes 1179656 | tf_op jit(solution)/shard_map/ppermute | solution.py:423
  19.6 11.9 %collective-permute-start.23 = (bf16[192,1024]{1,0:T(8,128)(2,1)S(1)}, bf16[192,1024]{1,0:T(8,128)(2,1)S(1)}, u32[]{:S(2)}, u32[]{:S(2)}) collective-permute-start(bf16[192,1024]{1,0:T(8,128)(2,1)S(1)} %collective-permute-done.22), channel_id=1, source_target_pairs={{8,0},{12,4},{16,8},{20,12},{24,16},{28,20},{9,1},{13,5},{17,9},{2... | collective-permute-start | bytes 1179656 | tf_op jit(solution)/shard_map/ppermute | solution.py:424
  27.1 10.9 %collective-permute-start.21 = (bf16[192,1024]{1,0:T(8,128)(2,1)S(1)}, bf16[192,1024]{1,0:T(8,128)(2,1)S(1)}, u32[]{:S(2)}, u32[]{:S(2)}) collective-permute-start(bf16[192,1024]{1,0:T(8,128)(2,1)S(1)} %collective-permute-done.20), channel_id=1, source_target_pairs={{0,8},{4,12},{8,16},{12,20},{16,24},{20,28},{1,9},{5,13},{9,17},{1... | collective-permute-start | bytes 1179656 | tf_op jit(solution)/shard_map/ppermute | solution.py:423
  31.5 10.7 %collective-permute-start.24 = (bf16[192,1024]{1,0:T(8,128)(2,1)S(1)}, bf16[192,1024]{1,0:T(8,128)(2,1)S(1)}, u32[]{:S(2)}, u32[]{:S(2)}) collective-permute-start(bf16[192,1024]{1,0:T(8,128)(2,1)S(1)} %collective-permute-done.23), channel_id=1, source_target_pairs={{8,0},{12,4},{16,8},{20,12},{24,16},{28,20},{9,1},{13,5},{17,9},{2... | collective-permute-start | bytes 1179656 | tf_op jit(solution)/shard_map/ppermute | solution.py:424
  42.4 16.4 %collective-permute-start.28 = (bf16[4,96,1024]{2,1,0:T(8,128)(2,1)S(1)}, bf16[4,96,1024]{2,1,0:T(8,128)(2,1)S(1)}, u32[]{:S(2)}, u32[]{:S(2)}) collective-permute-start(bf16[4,96,1024]{2,1,0:T(8,128)(2,1)S(1)} %get-tuple-element.17), channel_id=1, source_target_pairs={{0,2},{1,3},{2,0},{3,1},{4,6},{5,7},{6,4},{7,5},{8,10},{9,11},{10,... | collective-permute-start | bytes 2359304 | tf_op jit(solution)/shard_map/ppermute | solution.py:403
  44.0 17.7 %collective-permute-start.25 = (bf16[4,96,1024]{2,1,0:T(8,128)(2,1)S(1)}, bf16[4,96,1024]{2,1,0:T(8,128)(2,1)S(1)}, u32[]{:S(2)}, u32[]{:S(2)}) collective-permute-start(bf16[4,96,1024]{2,1,0:T(8,128)(2,1)S(1)} %get-tuple-element.18), channel_id=1, source_target_pairs={{0,4},{4,0},{8,12},{12,8},{16,20},{20,16},{24,28},{28,24},{1,5},{5... | collective-permute-start | bytes 2359304 | tf_op jit(solution)/shard_map/ppermute | solution.py:403
  60.2 55.5 %collective-permute-start.29 = (bf16[4,2,96,1024]{3,2,0,1:T(8,128)(2,1)}, bf16[4,2,96,1024]{3,2,0,1:T(8,128)(2,1)}, u32[]{:S(2)}, u32[]{:S(2)}) collective-permute-start(bf16[4,2,96,1024]{3,2,0,1:T(8,128)(2,1)} %maximum_select_fusion.5), channel_id=1, source_target_pairs={{0,4},{4,0},{8,12},{12,8},{16,20},{20,16},{24,28},{28,24},{1,5},{5... | collective-permute-start | bytes 4718600 | tf_op jit(solution)/shard_map/ppermute | solution.py:403
  63.1 55.0 %collective-permute-start.26 = (bf16[4,2,96,1024]{3,2,0,1:T(8,128)(2,1)}, bf16[4,2,96,1024]{3,2,0,1:T(8,128)(2,1)}, u32[]{:S(2)}, u32[]{:S(2)}) collective-permute-start(bf16[4,2,96,1024]{3,2,0,1:T(8,128)(2,1)} %maximum_select_fusion.3), channel_id=1, source_target_pairs={{0,2},{1,3},{2,0},{3,1},{4,6},{5,7},{6,4},{7,5},{8,10},{9,11},{10,... | collective-permute-start | bytes 4718600 | tf_op jit(solution)/shard_map/ppermute | solution.py:403
  72.9 33.6 %all-to-all-start.1 = ((bf16[4,8,32,512]{3,2,1,0:T(8,128)(2,1)}), bf16[4,8,32,512]{3,2,1,0:T(8,128)(2,1)S(1)}, u32[]{:S(2)}, u32[]{:S(2)}) async-start(bf16[4,8,32,512]{3,2,1,0:T(8,128)(2,1)} %get-tuple-element.14), calls=%async_computation.1 | async-start | bytes 2097152 | tf_op jit(solution)/shard_map/all_to_all | solution.py:461
  76.4 17.4 %collective-permute-start = (s32[8]{0:T(128)S(1)}, s32[8]{0:T(128)S(1)}, u32[]{:S(2)}, u32[]{:S(2)}) collective-permute-start(s32[8]{0:T(128)S(1)} %compare_select_fusion), channel_id=1, source_target_pairs={{0,4},{4,0},{8,12},{12,8},{16,20},{20,16},{24,28},{28,24},{1,5},{5... | collective-permute-start | bytes 104 | tf_op jit(solution)/shard_map/ppermute | solution.py:403
  97.4 4.4 %collective-permute-start.2 = (s32[8]{0:T(128)S(1)}, s32[8]{0:T(128)S(1)}, u32[]{:S(2)}, u32[]{:S(2)}) collective-permute-start(s32[8]{0:T(128)S(1)} %fusion.2), channel_id=1, source_target_pairs={{0,16},{4,20},{8,24},{12,28},{16,0},{20,4},{24,8},{28,12},{1,17},{... | collective-permute-start | bytes 104 | tf_op jit(solution)/shard_map/ppermute | solution.py:403
  106.5 18.8 %all-to-all-start = ((bf16[4,8,32,512]{3,2,1,0:T(8,128)(2,1)}), bf16[4,8,32,512]{3,2,1,0:T(8,128)(2,1)}, u32[]{:S(2)}, u32[]{:S(2)}) async-start(bf16[4,8,32,512]{3,2,1,0:T(8,128)(2,1)} %get-tuple-element.11), calls=%async_computation | async-start | bytes 2097152 | tf_op jit(solution)/shard_map/all_to_all | solution.py:461
  114.6 16.5 %collective-permute-start.11 = (bf16[1024,256]{1,0:T(8,128)(2,1)}, bf16[1024,256]{1,0:T(8,128)(2,1)}, u32[]{:S(2)}, u32[]{:S(2)}) collective-permute-start(bf16[1024,256]{1,0:T(8,128)(2,1)} %get-tuple-element.15.own_ref), channel_id=1, source_target_pairs={{0,4},{4,0},{8,12},{12,8},{16,20},{20,16},{24,28},{28,24},{1,5},{5... | collective-permute-start | bytes 1572872 | tf_op jit(solution)/shard_map/ppermute | solution.py:403
  123.4 141.9 %collective-permute-start.27 = (bf16[16,96,1024]{2,1,0:T(8,128)(2,1)}, bf16[16,96,1024]{2,1,0:T(8,128)(2,1)}, u32[]{:S(2)}, u32[]{:S(2)}) collective-permute-start(bf16[16,96,1024]{2,1,0:T(8,128)(2,1)} %bitcast.21.refs_16_), channel_id=1, source_target_pairs={{0,1},{1,0},{2,3},{3,2},{4,5},{5,4},{6,7},{7,6},{8,9},{9,8},{10,11... | collective-permute-start | bytes 9437192 | tf_op jit(solution)/shard_map/ppermute | solution.py:403
  123.6 141.6 %collective-permute-start.30 = (bf16[16,96,1024]{2,1,0:T(8,128)(2,1)S(1)}, bf16[16,96,1024]{2,1,0:T(8,128)(2,1)}, u32[]{:S(2)}, u32[]{:S(2)}) collective-permute-start(bf16[16,96,1024]{2,1,0:T(8,128)(2,1)S(1)} %bitcast.40), channel_id=1, source_target_pairs={{0,1},{1,0},{2,3},{3,2},{4,5},{5,4},{6,7},{7,6},{8,9},{9,8},{10,11... | collective-permute-start | bytes 9437192 | tf_op jit(solution)/shard_map/ppermute | solution.py:403
  129.1 14.8 %collective-permute-start.15 = (bf16[1024,256]{1,0:T(8,128)(2,1)S(1)}, bf16[1024,256]{1,0:T(8,128)(2,1)S(1)}, u32[]{:S(2)}, u32[]{:S(2)}) collective-permute-start(bf16[1024,256]{1,0:T(8,128)(2,1)S(1)} %copy-done.16), channel_id=1, source_target_pairs={{0,4},{4,0},{8,12},{12,8},{16,20},{20,16},{24,28},{28,24},{1,5},{5... | collective-permute-start | bytes 1572872 | tf_op jit(solution)/shard_map/ppermute | solution.py:403
  129.6 25.5 %collective-permute-start.3 = (bf16[1024,256]{1,0:T(8,128)(2,1)}, bf16[1024,256]{1,0:T(8,128)(2,1)S(1)}, u32[]{:S(2)}, u32[]{:S(2)}) collective-permute-start(bf16[1024,256]{1,0:T(8,128)(2,1)} %get-tuple-element.12.own_ref), channel_id=1, source_target_pairs={{0,4},{4,0},{8,12},{12,8},{16,20},{20,16},{24,28},{28,24},{1,5},{5... | collective-permute-start | bytes 1572872 | tf_op jit(solution)/shard_map/ppermute | solution.py:403
  131.1 33.9 %collective-permute-start.7 = (bf16[1024,256]{1,0:T(8,128)(2,1)}, bf16[1024,256]{1,0:T(8,128)(2,1)S(1)}, u32[]{:S(2)}, u32[]{:S(2)}) collective-permute-start(bf16[1024,256]{1,0:T(8,128)(2,1)} %get-tuple-element.13.own_ref), channel_id=1, source_target_pairs={{0,4},{4,0},{8,12},{12,8},{16,20},{20,16},{24,28},{28,24},{1,5},{5... | collective-permute-start | bytes 1572872 | tf_op jit(solution)/shard_map/ppermute | solution.py:403
  143.9 24.2 %collective-permute-start.13 = (bf16[1024,256]{1,0:T(8,128)(2,1)}, bf16[1024,256]{1,0:T(8,128)(2,1)S(1)}, u32[]{:S(2)}, u32[]{:S(2)}) collective-permute-start(bf16[1024,256]{1,0:T(8,128)(2,1)} %join_parity.6.own_ref.refs_8_), channel_id=1, source_target_pairs={{24,8},{28,12},{25,9},{29,13},{26,10},{30,14},{27,11},{31,15}} | collective-permute-start | bytes 1572872 | tf_op jit(solution)/shard_map/ppermute | solution.py:467
  155.2 13.7 %collective-permute-start.12 = (bf16[1024,256]{1,0:T(8,128)(2,1)}, bf16[1024,256]{1,0:T(8,128)(2,1)S(1)}, u32[]{:S(2)}, u32[]{:S(2)}) collective-permute-start(bf16[1024,256]{1,0:T(8,128)(2,1)} %join_parity.6.own_ref.refs_8_), channel_id=1, source_target_pairs={{16,8},{20,12},{24,16},{28,20},{17,9},{21,13},{25,17},{29,21},{18,... | collective-permute-start | bytes 1572872 | tf_op jit(solution)/shard_map/ppermute | solution.py:466
  165.0 4.6 %collective-permute-start.17 = (bf16[1024,256]{1,0:T(8,128)(2,1)}, bf16[1024,256]{1,0:T(8,128)(2,1)S(1)}, u32[]{:S(2)}, u32[]{:S(2)}) collective-permute-start(bf16[1024,256]{1,0:T(8,128)(2,1)} %join_parity.7.own_ref.refs_12_), channel_id=1, source_target_pairs={{24,8},{28,12},{25,9},{29,13},{26,10},{30,14},{27,11},{31,15}} | collective-permute-start | bytes 1572872 | tf_op jit(solution)/shard_map/ppermute | solution.py:467
  168.2 4.6 %collective-permute-start.16 = (bf16[1024,256]{1,0:T(8,128)(2,1)}, bf16[1024,256]{1,0:T(8,128)(2,1)S(1)}, u32[]{:S(2)}, u32[]{:S(2)}) collective-permute-start(bf16[1024,256]{1,0:T(8,128)(2,1)} %join_parity.7.own_ref.refs_12_), channel_id=1, source_target_pairs={{16,8},{20,12},{24,16},{28,20},{17,9},{21,13},{25,17},{29,21},{18,... | collective-permute-start | bytes 1572872 | tf_op jit(solution)/shard_map/ppermute | solution.py:466
  168.9 4.6 %collective-permute-start.5 = (bf16[1024,256]{1,0:T(8,128)(2,1)}, bf16[1024,256]{1,0:T(8,128)(2,1)S(1)}, u32[]{:S(2)}, u32[]{:S(2)}) collective-permute-start(bf16[1024,256]{1,0:T(8,128)(2,1)} %join_parity.4.own_ref.refs_0_), channel_id=1, source_target_pairs={{24,8},{28,12},{25,9},{29,13},{26,10},{30,14},{27,11},{31,15}} | collective-permute-start | bytes 1572872 | tf_op jit(solution)/shard_map/ppermute | solution.py:467
  169.6 6.9 %collective-permute-start.4 = (bf16[1024,256]{1,0:T(8,128)(2,1)}, bf16[1024,256]{1,0:T(8,128)(2,1)S(1)}, u32[]{:S(2)}, u32[]{:S(2)}) collective-permute-start(bf16[1024,256]{1,0:T(8,128)(2,1)} %join_parity.4.own_ref.refs_0_), channel_id=1, source_target_pairs={{16,8},{20,12},{24,16},{28,20},{17,9},{21,13},{25,17},{29,21},{18,... | collective-permute-start | bytes 1572872 | tf_op jit(solution)/shard_map/ppermute | solution.py:466
  172.8 9.8 %collective-permute-start.9 = (bf16[1024,256]{1,0:T(8,128)(2,1)}, bf16[1024,256]{1,0:T(8,128)(2,1)S(1)}, u32[]{:S(2)}, u32[]{:S(2)}) collective-permute-start(bf16[1024,256]{1,0:T(8,128)(2,1)} %join_parity.5.own_ref.refs_4_), channel_id=1, source_target_pairs={{24,8},{28,12},{25,9},{29,13},{26,10},{30,14},{27,11},{31,15}} | collective-permute-start | bytes 1572872 | tf_op jit(solution)/shard_map/ppermute | solution.py:467
  173.5 10.4 %collective-permute-start.8 = (bf16[1024,256]{1,0:T(8,128)(2,1)}, bf16[1024,256]{1,0:T(8,128)(2,1)S(1)}, u32[]{:S(2)}, u32[]{:S(2)}) collective-permute-start(bf16[1024,256]{1,0:T(8,128)(2,1)} %join_parity.5.own_ref.refs_4_), channel_id=1, source_target_pairs={{16,8},{20,12},{24,16},{28,20},{17,9},{21,13},{25,17},{29,21},{18,... | collective-permute-start | bytes 1572872 | tf_op jit(solution)/shard_map/ppermute | solution.py:466
  176.5 55.9 %collective-permute-start.14 = (bf16[1024,256]{1,0:T(8,128)(2,1)}, bf16[1024,256]{1,0:T(8,128)(2,1)S(1)}, u32[]{:S(2)}, u32[]{:S(2)}) collective-permute-start(bf16[1024,256]{1,0:T(8,128)(2,1)} %forward_merge.6), channel_id=1, source_target_pairs={{8,0},{12,4},{9,1},{13,5},{10,2},{14,6},{11,3},{15,7}} | collective-permute-start | bytes 1572872 | tf_op jit(solution)/shard_map/ppermute | solution.py:469
  182.5 61.3 %collective-permute-start.18 = (bf16[1024,256]{1,0:T(8,128)(2,1)}, bf16[1024,256]{1,0:T(8,128)(2,1)S(1)}, u32[]{:S(2)}, u32[]{:S(2)}) collective-permute-start(bf16[1024,256]{1,0:T(8,128)(2,1)} %forward_merge.7), channel_id=1, source_target_pairs={{8,0},{12,4},{9,1},{13,5},{10,2},{14,6},{11,3},{15,7}} | collective-permute-start | bytes 1572872 | tf_op jit(solution)/shard_map/ppermute | solution.py:469
  183.8 71.2 %collective-permute-start.6 = (bf16[1024,256]{1,0:T(8,128)(2,1)}, bf16[1024,256]{1,0:T(8,128)(2,1)S(1)}, u32[]{:S(2)}, u32[]{:S(2)}) collective-permute-start(bf16[1024,256]{1,0:T(8,128)(2,1)} %forward_merge.4), channel_id=1, source_target_pairs={{8,0},{12,4},{9,1},{13,5},{10,2},{14,6},{11,3},{15,7}} | collective-permute-start | bytes 1572872 | tf_op jit(solution)/shard_map/ppermute | solution.py:469
  232.5 32.7 %collective-permute-start.10 = (bf16[1024,256]{1,0:T(8,128)(2,1)}, bf16[1024,256]{1,0:T(8,128)(2,1)S(1)}, u32[]{:S(2)}, u32[]{:S(2)}) collective-permute-start(bf16[1024,256]{1,0:T(8,128)(2,1)} %forward_merge.5), channel_id=1, source_target_pairs={{8,0},{12,4},{9,1},{13,5},{10,2},{14,6},{11,3},{15,7}} | collective-permute-start | bytes 1572872 | tf_op jit(solution)/shard_map/ppermute | solution.py:469
  (21 other events, 161.9 us)

commit v2 on v0

--- a/solution.py
+++ b/solution.py
@@ -1,6 +1,10 @@
+import functools
+
 import jax
 import jax.numpy as jnp
 from jax import lax
+from jax.experimental import pallas as pl
+from jax.experimental.pallas import tpu as pltpu
 from jax.sharding import PartitionSpec as P
 
 epsilon = 1e-05
@@ -119,9 +123,451 @@
     return packed.reshape(1, row_count, feat_width)
 
 
+SMEM = pl.BlockSpec(memory_space=pltpu.SMEM)
+VMEM = pl.BlockSpec(memory_space=pltpu.VMEM)
+ANY = pl.BlockSpec(memory_space=pl.ANY)
+MIB = 1024 * 1024
+GROUP = 16
+SUB = 8
+SPANS = (2, 2, 2, 2)
+TOKEN = jax.ShapeDtypeStruct((8, 128), jnp.int32)
+
+
+def local_call(kernel, name, limit, in_specs, out_specs, out_shape, after=(), grid=(), scratch=()):
+    ins, waits, outs = len(in_specs), len(after), len(out_specs)
+
+    def body(*refs):
+        token_ref = refs[ins + waits + outs]
+        kernel(*refs[:ins], *refs[ins + waits:ins + waits + outs], *refs[ins + waits + outs + 1:])
+        token_ref[...] = jnp.zeros(token_ref.shape, token_ref.dtype)
+
+    token_spec = pl.BlockSpec(TOKEN.shape, lambda *_: (0, 0)) if grid else VMEM
+    call = pl.pallas_call(
+        body,
+        grid=grid,
+        in_specs=list(in_specs) + [ANY] * waits,
+        out_specs=list(out_specs) + [token_spec],
+        out_shape=list(out_shape) + [TOKEN],
+        scratch_shapes=list(scratch),
+        compiler_params=pltpu.CompilerParams(vmem_limit_bytes=limit * MIB),
+        cost_estimate=pl.CostEstimate(flops=1, bytes_accessed=1, transcendentals=0),
+        name=name,
+    )
+
+    def run(*operands):
+        *results, token = call(*operands, *after)
+        return results, token
+
+    return run
+
+
+def live_rows(start, shape, length, occupied):
+    ids = start + lax.broadcasted_iota(jnp.int32, shape, 0)
+    return (ids < length) & (occupied > 0)
+
+
+def first_kernel(ids_ref, lengths_ref, occ_ref, tile_ref, mix_ref, *out_refs):
+    step = pl.program_id(0)
+    blocks, blk_size = mix_ref.shape[:2]
+    feat_width = tile_ref.shape[2]
+    lane = ids_ref[1]
+    share = out_refs[0].shape[1]
+    parts = blk_size // share
+    rows_here = pl.num_programs(0) * blocks * blk_size
+    for i in range(blocks):
+        block = step * blocks + i
+        start = lane * rows_here + block * blk_size
+        live = live_rows(start, (blk_size, feat_width), lengths_ref[ids_ref[0]], occ_ref[0, block])
+        tile = tile_ref[0, i * blk_size:(i + 1) * blk_size, :]
+        masked = jnp.where(live, tile.astype(jnp.float32), 0.0)
+        normed = rms_round(masked)
+        picked = [mix_ref[i, pl.ds(pl.multiple_of((lane ^ part) * share, share), share), :] for part in range(parts)]
+        mix = jnp.concatenate(picked, axis=0)
+        first = jnp.dot(mix, normed, preferred_element_type=jnp.float32).astype(jnp.bfloat16)
+        begin = 0
+        for group in range(len(out_refs) // parts):
+            end = begin + out_refs[group * parts].shape[2]
+            for part in range(parts):
+                out_refs[group * parts + part][i] = first[part * share:(part + 1) * share, begin:end]
+            begin = end
+
+
+def first_factor(ids, lengths, occupancy, tile_tokens, block_mix, parts, groups, after):
+    blocks, blk_size, _ = block_mix.shape
+    feat_width = tile_tokens.shape[2]
+    share = blk_size // parts
+    each = 2
+    return local_call(
+        first_kernel,
+        "first_factor",
+        16,
+        [
+            SMEM,
+            SMEM,
+            SMEM,
+            pl.BlockSpec((1, each * blk_size, feat_width), lambda b: (0, b, 0)),
+            pl.BlockSpec((each, blk_size, blk_size), lambda b: (b, 0, 0)),
+        ],
+        [pl.BlockSpec((each, share, width), lambda b: (b, 0, 0)) for width in groups for _ in range(parts)],
+        [jax.ShapeDtypeStruct((blocks, share, width), jnp.bfloat16) for width in groups for _ in range(parts)],
+        after,
+        grid=(blocks // each,),
+    )(ids, lengths, occupancy, tile_tokens, block_mix)
+
+
+def spread_kernel(parts, ids_ref, stride_ref, out_ref):
+    spots, outs, ins = stride_ref.shape
+    rows, cols = GROUP * outs, GROUP * ins
+    column = lax.broadcasted_iota(jnp.int32, (ins, cols), 1) // GROUP
+    here = ins // parts
+    block = ((column // here) ^ ids_ref[1]) * here + column % here
+    picks = block == lax.broadcasted_iota(jnp.int32, (ins, cols), 0)
+    picks = picks.astype(jnp.float32).astype(jnp.bfloat16)
+    spot_row = lax.broadcasted_iota(jnp.int32, (rows, cols), 0) // outs
+    spot_col = lax.broadcasted_iota(jnp.int32, (rows, cols), 1) % GROUP
+    for group in range(spots // GROUP):
+        flat = stride_ref[group * GROUP:(group + 1) * GROUP].reshape(rows, ins)
+        wide = jnp.dot(flat, picks, preferred_element_type=jnp.float32)
+        out_ref[group] = jnp.where(spot_row == spot_col, wide, 0.0).astype(jnp.bfloat16)
+
+
+def spread_stride(ids, stride_mix, parts, after):
+    spots, outs, ins = stride_mix.shape
+    shape = jax.ShapeDtypeStruct((spots // GROUP, GROUP * outs, GROUP * ins), jnp.bfloat16)
+    kernel = functools.partial(spread_kernel, parts)
+    return local_call(kernel, "spread_stride", 12, [SMEM, VMEM], [VMEM], [shape], after)(ids, stride_mix)
+
+
+def kept_of(length, lane, rows):
+    return jnp.clip(length - lane * rows, 0, rows)
+
+
+def offset_of(lengths_ref, page, lane, rows):
+    total = jnp.int32(0)
+    for earlier in range(lengths_ref.shape[0]):
+        total += jnp.where(earlier < page, kept_of(lengths_ref[earlier], lane, rows), 0)
+    return total
+
+
+def second_kernel(parts, begin, ids_ref, lengths_ref, occ_ref, spread_ref, *refs):
+    first_refs, tile_ref, out_refs, twice_ref = refs[:parts], refs[parts], refs[parts + 1:-1], refs[-1]
+    rows, width = tile_ref.shape[1], first_refs[0].shape[2]
+    page, lane = ids_ref[0], ids_ref[1]
+    length = lengths_ref[page]
+    groups, group_rows, depth = spread_ref.shape
+    blk_size = rows // occ_ref.shape[1]
+    for group in range(groups):
+        values = [ref[:, group * GROUP:(group + 1) * GROUP, :].reshape(depth // parts, width) for ref in first_refs]
+        second = jnp.dot(spread_ref[group], jnp.concatenate(values, axis=0), preferred_element_type=jnp.float32)
+        for part in range(group_rows // blk_size):
+            at = group * group_rows + part * blk_size
+            live = live_rows(lane * rows + at, (blk_size, width), length, occ_ref[0, at // blk_size])
+            tile = tile_ref[0, at:at + blk_size, begin:begin + width]
+            masked = jnp.where(live, tile.astype(jnp.float32), 0.0)
+            mixed = masked + second[part * blk_size:(part + 1) * blk_size]
+            mixed = mixed.astype(jnp.bfloat16).astype(jnp.float32)
+            twice_ref[at:at + blk_size, :] = mixed
+            twice_ref[rows + at:rows + at + blk_size, :] = mixed
+    twice_ref[2 * rows:, :] = jnp.zeros((SUB, width), jnp.float32)
+    start = rows - offset_of(lengths_ref, page, lane, rows) % rows
+    extra = start % SUB
+    base = pl.multiple_of(start - extra, SUB)
+    tall = twice_ref[pl.ds(base, rows + SUB), :].reshape(rows // SUB + 1, SUB, width)
+    tall = pltpu.roll(tall, (SUB - extra) % SUB, 1)
+    inside = lax.broadcasted_iota(jnp.int32, (1, SUB, width), 1) + extra < SUB
+    turned = jnp.where(inside, tall[:-1], tall[1:]).reshape(rows, width).astype(jnp.bfloat16)
+    begin = 0
+    for out_ref in out_refs:
+        end = begin + out_ref.shape[1]
+        out_ref[...] = turned[:, begin:end]
+        begin = end
+
+
+def second_factor(begin, spans, ids, lengths, occupancy, spread, firsts, tile_tokens, after):
+    rows = tile_tokens.shape[1]
+    width = firsts[0].shape[2]
+    parts = len(firsts)
+    return local_call(
+        functools.partial(second_kernel, parts, begin),
+        "second_factor",
+        24,
+        [SMEM, SMEM, SMEM, VMEM] + [VMEM] * parts + [VMEM],
+        [VMEM] * len(spans),
+        [jax.ShapeDtypeStruct((rows, span), jnp.bfloat16) for span in spans],
+        after,
+        scratch=[pltpu.VMEM((2 * rows + SUB, width), jnp.float32)],
+    )(ids, lengths, occupancy, spread, *firsts, tile_tokens)
+
+
+def pick(mask, yes_ref, no_ref):
+    return jnp.where(mask, yes_ref[...].astype(jnp.float32), no_ref[...].astype(jnp.float32))
+
+
+def parity_kernel(ids_ref, lengths_ref, own_ref, got_ref, out_ref):
+    rows = own_ref.shape[0]
+    page, lane = ids_ref[0], ids_ref[1]
+    offset = offset_of(lengths_ref, page, lane, rows)
+    kept = kept_of(lengths_ref[page], lane, rows)
+    slot = lax.broadcasted_iota(jnp.int32, own_ref.shape, 0)
+    base, shift = offset // rows, offset % rows
+    early = (base % 2 == page % 2).astype(jnp.int32)
+    low = jnp.where(early == 1, shift, 0)
+    high = jnp.where(early == 1, jnp.minimum(shift + kept, rows), shift + kept - rows)
+    out_ref[...] = pick((slot >= low) & (slot < high), own_ref, got_ref).astype(out_ref.dtype)
+
+
+def join_parity(ids, lengths, own, got, after):
+    shape = jax.ShapeDtypeStruct(own.shape, own.dtype)
+    return local_call(parity_kernel, "join_parity", 6, [SMEM, SMEM, VMEM, VMEM], [VMEM], [shape], after)(ids, lengths, own, got)
+
+
+def forward_kernel(ids_ref, lengths_ref, own_ref, one_ref, two_ref, out_ref):
+    rows = own_ref.shape[0]
+    page, lane = ids_ref[0], ids_ref[1]
+    level = page // 2
+    slot = (page % 2) * rows + lax.broadcasted_iota(jnp.int32, own_ref.shape, 0)
+    after_one = offset_of(lengths_ref, 2 * level + 2, lane, rows)
+    after_two = offset_of(lengths_ref, 2 * level + 4, lane, rows)
+    value = pick(slot < after_two, one_ref, two_ref)
+    out_ref[...] = jnp.where(slot < after_one, own_ref[...].astype(jnp.float32), value).astype(out_ref.dtype)
+
+
+def forward_merge(ids, lengths, own, one, two, after):
+    shape = jax.ShapeDtypeStruct(own.shape, own.dtype)
+    specs = [SMEM, SMEM, VMEM, VMEM, VMEM]
+    return local_call(forward_kernel, "forward_merge", 6, specs, [VMEM], [shape], after)(ids, lengths, own, one, two)
+
+
+def final_kernel(ids_ref, lengths_ref, own_ref, one_ref, two_ref, last_ref, out_ref):
+    rows = own_ref.shape[0]
+    page, lane = ids_ref[0], ids_ref[1]
+    level = page // 2
+    slot = page * rows + lax.broadcasted_iota(jnp.int32, own_ref.shape, 0)
+    ends = [offset_of(lengths_ref, 2 * (level + ahead), lane, rows) for ahead in (1, 2)]
+    total = offset_of(lengths_ref, lengths_ref.shape[0], lane, rows)
+
+    @pl.when(level == 0)
+    def _():
+        value = pick(slot < ends[0], own_ref, last_ref)
+        out_ref[...] = jnp.where(slot < total, value, 0.0).astype(out_ref.dtype)
+
+    @pl.when(level > 0)
+    def _():
+        value = pick(slot < ends[1], one_ref, two_ref)
+        value = jnp.where(slot < ends[0], own_ref[...].astype(jnp.float32), value)
+        out_ref[...] = jnp.where(slot < total, value, 0.0).astype(out_ref.dtype)
+
+
+def final_merge(ids, lengths, own, one, two, last, after):
+    shape = jax.ShapeDtypeStruct(own.shape, own.dtype)
+    specs = [SMEM, SMEM, VMEM, VMEM, VMEM, VMEM]
+    return local_call(final_kernel, "final_merge", 8, specs, [VMEM], [shape], after)(ids, lengths, own, one, two, last)
+
+
+def mlp_kernel(pieces, *refs):
+    sources, refs = refs[:pieces], refs[pieces:]
+    main_ref, out_ref, gate_ref, up_ref, down_ref, sems = refs
+    step = pl.program_id(0)
+    here, levels = main_ref.shape[:2]
+    hidden_width, feat_width = gate_ref.shape
+    wide, thin = hidden_width // (here * levels), feat_width // (here * levels)
+    parts = levels
+    span = hidden_width // parts
+    gates = gate_ref.reshape(levels, here, wide, feat_width)
+    ups = up_ref.reshape(levels, here, wide, feat_width)
+    downs = down_ref.reshape(levels, here, thin, hidden_width)
+
+    def copies(part):
+        begin = part * span
+        at, cols = 2 * wide + begin // feat_width * thin, pl.ds(begin % feat_width, span)
+        found = [(main_ref.at[:, part, :wide], gates.at[part]), (main_ref.at[:, part, wide:2 * wide], ups.at[part])]
+        for level in range(levels):
+            found.append((main_ref.at[:, level, at:at + thin, cols], downs.at[level, :, :, begin:begin + span]))
+        return [pltpu.make_async_copy(src, dst, sems.at[part, i]) for i, (src, dst) in enumerate(found)]
+
+    @pl.when(step == 0)
+    def _():
+        for part in range(parts):
+            for copy in copies(part):
+                copy.start()
+
+    mixed = jnp.concatenate([ref[...] for ref in sources], axis=1).astype(jnp.float32)
+    normed = rms_round(mixed)
+    contract = (((1,), (1,)), ((), ()))
+    result = mixed
+    for part in range(parts):
+        @pl.when(step == 0)
+        def _():
+            for copy in copies(part):
+                copy.wait()
+
+        at = part * span
+        gate = lax.dot_general(normed, gate_ref[at:at + span, :], contract, preferred_element_type=jnp.float32)
+        up = lax.dot_general(normed, up_ref[at:at + span, :], contract, preferred_element_type=jnp.float32)
+        hidden = (gate / (1.0 + jnp.exp(-gate)) * up).astype(jnp.bfloat16)
+        down = down_ref[:, at:at + span]
+        result += lax.dot_general(hidden, down, contract, preferred_element_type=jnp.float32)
+    out_ref[0] = result.astype(out_ref.dtype)
+
+
+def packed_mlp(sources, weights):
+    rows = sources[0].shape[0]
+    pieces = len(sources)
+    here, levels, each, feat_width = weights.shape
+    hidden_width = here * levels * (each - feat_width // (here * levels) * 2) // 2
+    steps = 2
+    block = rows // steps
+    return pl.pallas_call(
+        functools.partial(mlp_kernel, pieces),
+        grid=(steps,),
+        in_specs=[pl.BlockSpec((block, source.shape[1]), lambda i: (i, 0)) for source in sources] + [ANY],
+        out_specs=pl.BlockSpec((1, block, feat_width), lambda i: (0, i, 0)),
+        out_shape=jax.ShapeDtypeStruct((1, rows, feat_width), jnp.bfloat16),
+        scratch_shapes=[
+            pltpu.VMEM((hidden_width, feat_width), jnp.bfloat16),
+            pltpu.VMEM((hidden_width, feat_width), jnp.bfloat16),
+            pltpu.VMEM((feat_width, hidden_width), jnp.bfloat16),
+            pltpu.SemaphoreType.DMA((levels, 2 + levels)),
+        ],
+        compiler_params=pltpu.CompilerParams(vmem_limit_bytes=40 * MIB),
+        name="packed_mlp",
+    )(*sources, weights)
+
+
+def swap(value, axis, bit):
+    return lax.ppermute(value, axis, [(i, i ^ bit) for i in range(lax.axis_size(axis))])
+
+
+def pack_kernel(main_ref, down_ref, out_ref):
+    wide, feat_width = main_ref.shape[1:]
+    thin = down_ref.shape[0]
+    out_ref[:wide] = main_ref[0]
+    out_ref[wide:2 * wide] = main_ref[1]
+    for part in range(down_ref.shape[1] // feat_width):
+        at = 2 * wide + part * thin
+        out_ref[at:at + thin] = down_ref[:, part * feat_width:(part + 1) * feat_width]
+
+
+def pack_weights(main, down, after):
+    _, wide, feat_width = main.shape
+    rows = 2 * wide + down.size // feat_width
+    shape = jax.ShapeDtypeStruct((rows, feat_width), main.dtype)
+    return local_call(pack_kernel, "pack_weights", 6, [VMEM, VMEM], [VMEM], [shape], after)(main, down)
+
+
+def pair_kernel(which, place, ids_ref, own_ref, got_ref, out_ref, both_ref, sems):
+    axis, shift = which
+    bit = (ids_ref[axis] // shift) % 2
+    lead = (slice(None),) * place
+    copies = [
+        pltpu.make_async_copy(own_ref, both_ref.at[lead + (bit,)], sems.at[0]),
+        pltpu.make_async_copy(got_ref, both_ref.at[lead + (1 - bit,)], sems.at[1]),
+    ]
+    for copy in copies:
+        copy.start()
+    for copy in copies:
+        copy.wait()
+    whole = pltpu.make_async_copy(both_ref, out_ref, sems.at[2])
+    whole.start()
+    whole.wait()
+
+
+def pair_up(ids, own, got, which, place, after):
+    shape = own.shape[:place] + (2,) + own.shape[place:]
+    return local_call(
+        functools.partial(pair_kernel, which, place),
+        "pair_up",
+        8,
+        [SMEM, ANY, ANY],
+        [ANY],
+        [jax.ShapeDtypeStruct(shape, own.dtype)],
+        after,
+        scratch=[pltpu.VMEM(shape, own.dtype), pltpu.SemaphoreType.DMA((3,))],
+    )(ids, own, got)
+
+
+AXES = ("page", "tok")
+
+
+def some_lengths(length, bit, least):
+    pages = lax.axis_size("page")
+    lengths = jnp.where(jnp.arange(pages) == lax.axis_index("page"), length, 0)
+    while bit > least:
+        lengths = lengths + swap(lengths, "page", bit)
+        bit //= 2
+    return lengths
+
+
+def packed_device(tile_tokens, page_lengths, occupancy, block_mix, stride_mix, w_gate_up, w_down):
+    ids = jnp.stack([lax.axis_index("page"), lax.axis_index("tok")]).astype(jnp.int32)
+    pages, parts = lax.axis_size("page"), lax.axis_size("tok")
+    feat_width = tile_tokens.shape[2]
+    spans = [feat_width * eighths // 8 for eighths in SPANS]
+    groups = (spans[0], feat_width - spans[0])
+    z_far, z_near = (0, 4), (0, 2)
+    tokens = []
+
+    def chained(step, *operands):
+        results, token = step(*operands, tokens[-1:])
+        tokens.append(token)
+        return results
+
+    def paired(value, which, place):
+        axis, shift = which
+        return chained(pair_up, ids, value, swap(value, AXES[axis], shift), which, place)[0]
+
+    def plane(value):
+        here = 2 * parts
+        groups = [[level * here + i for i in range(here)] for level in range(pages // 2)]
+        return lax.all_gather(value.reshape((-1,) + value.shape[2:]), AXES, axis_index_groups=groups)
+
+    def across(firsts):
+        return firsts[:1] + [swap(firsts[part], "tok", part) for part in range(1, parts)]
+
+    far_lengths = some_lengths(page_lengths[0], pages // 2, 1)
+    tokens.append(far_lengths)
+    weights = chained(pack_weights, jnp.swapaxes(w_gate_up, 1, 2), jnp.swapaxes(w_down, 0, 1))[0]
+    lengths = far_lengths + swap(far_lengths, "page", 1)
+    firsts = chained(first_factor, ids, lengths, occupancy, tile_tokens, block_mix, parts, groups)
+    found = [across(firsts[:parts]), across(firsts[parts:])]
+    spread = chained(spread_stride, ids, stride_mix, parts)[0]
+    turned = chained(second_factor, 0, spans[:1], ids, lengths, occupancy, spread, found[0], tile_tokens)
+    weights = paired(weights, z_far, 0)
+    swapped = [swap(own, "page", 1) for own in turned]
+    current, one, two, last, sources = {}, {}, {}, {}, []
+
+    def join(k):
+        current[k] = chained(join_parity, ids, lengths, turned[k], swapped[k])[0]
+        one[k] = lax.ppermute(current[k], "page", [(4, 2), (5, 3), (6, 4), (7, 5), (2, 6), (3, 7)])
+        two[k] = lax.ppermute(current[k], "page", [(6, 2), (7, 3), (2, 6), (3, 7)])
+
+    def forward(k):
+        merged = chained(forward_merge, ids, lengths, current[k], one[k], two[k])[0]
+        last[k] = lax.ppermute(merged, "page", [(2, 0), (3, 1), (0, 2), (1, 3)])
+
+    def finish(k):
+        sources.extend(chained(final_merge, ids, lengths, current[k], one[k], two[k], last[k]))
+
+    join(0)
+    turned += chained(second_factor, spans[0], spans[1:], ids, lengths, occupancy, spread, found[1], tile_tokens)
+    swapped += [swap(own, "page", 1) for own in turned[1:]]
+    weights = plane(paired(weights, z_near, 1))
+    join(1)
+    count = len(spans)
+    for k in range(count):
+        forward(k)
+        if k + 2 < count:
+            join(k + 2)
+        if k:
+            finish(k - 1)
+    finish(count - 1)
+    return packed_mlp(sources, weights)
+
+
 def solution(mesh):
+    pages, parts = mesh.shape["page"], mesh.shape["tok"]
     return jax.shard_map(
-        per_device,
+        packed_device if (pages, parts) == (8, 4) else per_device,
         mesh=mesh,
         in_specs=(
             P("page", "tok", None),

time: 437 us -> 204 us (0.47)
  waiting for transfers between devices: 324 us -> 69.9 us
  starting transfers between devices: 14.8 us -> 76.2 us
  Pallas kernels: 0 us -> 38.3 us
  matrix products: 33 us -> 0 us
  other arithmetic: 15.7 us -> 0.09 us
  blocking collectives: 12.7 us -> 0 us
  local copies, waits for them, and re-layouts: 17.6 us -> 5.06 us
  loops' own time: 4.86 us -> 0 us
    ppermute x8 -> x27, waiting for transfers between devices: 234 us -> 69.8 us  [the longest x15 59.5 us: swap(): lax.ppermute(value, axis, [(i, i ^ bit) for i in range(lax.axis_size(axis...]
    all_gather x2 -> x1, waiting for transfers between devices: 83 us -> 0.01 us  [plane(): lax.all_gather(value.reshape((-1,) + value.shape[2:]), AXES, axis_index_g...]
    ppermute x8 -> x27, starting transfers between devices: 10.3 us -> 76.2 us  [the longest x4 50.3 us: forward(): last[k] = lax.ppermute(merged, 'page', [(2, 0), (3, 1), (0, 2), (1, 3)])]
    pallas_call x0 -> x20, Pallas kernels: none -> 38.3 us  [the longest x19 19.9 us: run(): *results, token = call(*operands, *after)]
    dot_general x4 -> x0, matrix products: 33 us -> none  [the longest x1 16.6 us: channel_mlp(): jnp.dot(hidden, lax.all_gather(w_down, ('page', 'tok'), axis=1, tiled=Tru...]
    unnamed x1 -> x0, blocking collectives: 12.7 us -> none
    convert_element_type x2 -> x0, local copies, waits for them, and re-layouts: 8.37 us -> none  [the longest x1 5.46 us: per_device(): tile_tokens[0].astype(jnp.float32)]
    select_n x7 -> x1, other arithmetic: 7.6 us -> 0.01 us  [some_lengths(): lengths = jnp.where(jnp.arange(pages) == lax.axis_index('page'), length, 0)]
  transfers between devices with their start and end apart: 11 -> 28, of which waited for: 8 -> 11; matrix products, arithmetic and copies ran while one was open for 8% -> 0% of each run, Pallas kernels for 0% -> 8%
where the time goes in v2:
time: 204 us
  starting transfers between devices  76.2 us (37%)
  waiting for transfers between devices  69.9 us (34%)
  Pallas kernels  38.3 us (19%)
  between operations  14.5 us (7%)
  local copies, waits for them, and re-layouts  5.06 us (2%)
    ppermute x15, waiting for transfers between devices, swap(): lax.ppermute(value, axis, [(i, i ^ bit) for i in range(lax.axis_size(axis...  59.5 us
    ppermute x4, starting transfers between devices, forward(): last[k] = lax.ppermute(merged, 'page', [(2, 0), (3, 1), (0, 2), (1, 3)])  50.3 us
    ppermute x15, starting transfers between devices, swap(): lax.ppermute(value, axis, [(i, i ^ bit) for i in range(lax.axis_size(axis...  20.4 us
    pallas_call x19, Pallas kernels, run(): *results, token = call(*operands, *after)  19.9 us
    pallas_call x1, Pallas kernels, packed_mlp(): pl.pallas_call(functools.partial(mlp_kernel, pieces), grid=(steps,), in_s...  18.4 us
    ppermute x4, waiting for transfers between devices, forward(): last[k] = lax.ppermute(merged, 'page', [(2, 0), (3, 1), (0, 2), (1, 3)])  10.3 us
    unnamed x16, local copies, waits for them, and re-layouts  5.06 us
  transfers between devices with their start and end apart: 28, of which 11 were waited for; matrix products, arithmetic and copies ran while one was open for 0% of the time, Pallas kernels for 8%

profile of v2, /device:TPU:0, one launch (start us, length us, event | category | flops | bytes accessed | tf_op | source)
XLA Modules:
  0.0 203.9 jit_solution(8175657586631742931)
XLA Ops:
  7.2 4.1 %collective-permute-start = (s32[8]{0:T(128)S(1)}, s32[8]{0:T(128)S(1)}, u32[]{:S(2)}, u32[]{:S(2)}) collective-permute-start(s32[8]{0:T(128)S(1)} %compare_select_fusion), channel_id=1, source_target_pairs={{0,16},{4,20},{8,24},{12,28},{16,0},{20,4},{24,8},{28,12},{1,17},{... | collective-permute-start | bytes 104 | tf_op jit(solution)/shard_map/ppermute | solution.py:438
  11.3 1.5 collective-permute-done
  12.8 1.9 collective-permute-start.1
  14.7 1.6 collective-permute-done.1
  18.3 3.0 %collective-permute-start.7 = (bf16[192,1024]{1,0:T(8,128)(2,1)S(1)}, bf16[192,1024]{1,0:T(8,128)(2,1)S(1)}, u32[]{:S(2)}, u32[]{:S(2)}) collective-permute-start(bf16[192,1024]{1,0:T(8,128)(2,1)S(1)} %get-tuple-element.60.refs_1_), channel_id=1, source_target_pairs={{0,16},{4,20},{8,24},{12,28},{16,0},{20,4},{24,8},{28,12},{1,17},{... | collective-permute-start | bytes 1179656 | tf_op jit(solution)/shard_map/ppermute | solution.py:438
  21.3 1.5 collective-permute-start.2
  22.8 2.0 %collective-permute-done.2 = s32[8]{0:T(128)S(1)} collective-permute-done((s32[8]{0:T(128)S(1)}, s32[8]{0:T(128)S(1)}, u32[]{:S(2)}, u32[]{:S(2)}) %collective-permute-start.2) | collective-permute-done | bytes 64 | tf_op jit(solution)/shard_map/ppermute | solution.py:438
  24.9 1.6 copy-done
  28.1 2.4 %first_factor.1 = (bf16[8,32,256]{2,1,0:T(8,128)(2,1)S(1)}, bf16[8,32,256]{2,1,0:T(8,128)(2,1)S(1)}, bf16[8,32,256]{2,1,0:T(8,128)(2,1)S(1)}, bf16[8,32,256]{2,1...) custom-call(s32[2]{0:T(128)S(1)} %pad_add_fusion.refs_0_, ...), custom_call_target="tpu_custom_call" | custom-call | flops 1 | bytes 1 | tf_op jit(solution)/shard_map/first_factor/pallas_call | solution.py:158
  30.6 1.6 collective-permute-start.4
  33.4 3.5 %collective-permute-done.4.refs_6_ = bf16[8,32,256]{2,1,0:T(8,128)(2,1)S(1)} collective-permute-done((bf16[8,32,256]{2,1,0:T(8,128)(2,1)S(1)}, bf16[8,32,256]{2,1,0:T(8,128)(2,1)S(1)}, u32[]{:S(2)}, u32[]{:S(2)}) %collective-permute-start.4) | collective-permute-done | bytes 131104 | tf_op jit(solution)/shard_map/ppermute | solution.py:438
  37.0 1.9 collective-permute-done.5.refs_7_
  38.9 1.2 second_factor.2
  40.1 1.0 pair_up.2
  41.1 1.6 collective-permute-start.14
  42.7 1.5 collective-permute-start.6
  44.2 1.5 collective-permute-start.11
  46.1 10.5 %collective-permute-done.6.refs_3_ = bf16[1024,256]{1,0:T(8,128)(2,1)S(1)} collective-permute-done((bf16[1024,256]{1,0:T(8,128)(2,1)S(1)}, bf16[1024,256]{1,0:T(8,128)(2,1)S(1)}, u32[]{:S(2)}, u32[]{:S(2)}) %collective-permute-start.6) | collective-permute-done | bytes 524320 | tf_op jit(solution)/shard_map/ppermute | solution.py:438
  57.3 6.4 %collective-permute-done.12.refs_7_ = bf16[8,32,768]{2,1,0:T(8,128)(2,1)S(1)} collective-permute-done((bf16[8,32,768]{2,1,0:T(8,128)(2,1)S(1)}, bf16[8,32,768]{2,1,0:T(8,128)(2,1)S(1)}, u32[]{:S(2)}, u32[]{:S(2)}) %collective-permute-start.12) | collective-permute-done | bytes 393248 | tf_op jit(solution)/shard_map/ppermute | solution.py:438
  63.8 2.2 %second_factor.3 = (bf16[1024,256]{1,0:T(8,128)(2,1)S(1)}, bf16[1024,256]{1,0:T(8,128)(2,1)S(1)}, bf16[1024,256]{1,0:T(8,128)(2,1)S(1)}, s32[8,128]{1,0:T(8,128)S(1)}) custom-call(s32[2]{0:T(128)S(1)} %pad_add_fusion.refs_0_, s32[8]{0:T(128)S(1)} %add.11.refs_1_, s32[1,8]{1,0:T(1,128)S(1)} %copy-done.7, bf16[2,512,512]{2,1,0:T(8,128)(2,1)S(1)} %get-tuple-element.53.refs_3_, ...), custom_call_target="tpu_custom_call" | custom-call | flops 1 | bytes 1 | tf_op jit(solution)/shard_map/second_factor/pallas_call | solution.py:158
  66.0 1.8 pair_up.3
  69.9 1.6 collective-permute-start.19
  71.4 17.4 %collective-permute-done.13.refs_3_ = bf16[1024,256]{1,0:T(8,128)(2,1)S(1)} collective-permute-done((bf16[1024,256]{1,0:T(8,128)(2,1)S(1)}, bf16[1024,256]{1,0:T(8,128)(2,1)S(1)}, u32[]{:S(2)}, u32[]{:S(2)}) %collective-permute-start.13) | collective-permute-done | bytes 524320 | tf_op jit(solution)/shard_map/ppermute | solution.py:438
  92.7 6.8 %collective-permute-start.15 = (bf16[1024,256]{1,0:T(8,128)(2,1)S(1)}, bf16[1024,256]{1,0:T(8,128)(2,1)S(1)}, u32[]{:S(2)}, u32[]{:S(2)}) collective-permute-start(bf16[1024,256]{1,0:T(8,128)(2,1)S(1)} %get-tuple-element.74), channel_id=1, source_target_pairs={{8,0},{12,4},{0,8},{4,12},{9,1},{13,5},{1,9},{5,13},{10,2},{14,6},... | collective-permute-start | bytes 1572872 | tf_op jit(solution)/shard_map/ppermute | solution.py:546
  99.5 11.3 %collective-permute-done.19.refs_3_ = bf16[1024,256]{1,0:T(8,128)(2,1)S(1)} collective-permute-done((bf16[1024,256]{1,0:T(8,128)(2,1)S(1)}, bf16[1024,256]{1,0:T(8,128)(2,1)S(1)}, u32[]{:S(2)}, u32[]{:S(2)}) %collective-permute-start.19) | collective-permute-done | bytes 524320 | tf_op jit(solution)/shard_map/ppermute | solution.py:438
  113.8 8.2 %collective-permute-start.20 = (bf16[1024,256]{1,0:T(8,128)(2,1)S(1)}, bf16[1024,256]{1,0:T(8,128)(2,1)S(1)}, u32[]{:S(2)}, u32[]{:S(2)}) collective-permute-start(bf16[1024,256]{1,0:T(8,128)(2,1)S(1)} %get-tuple-element.83), channel_id=1, source_target_pairs={{8,0},{12,4},{0,8},{4,12},{9,1},{13,5},{1,9},{5,13},{10,2},{14,6},... | collective-permute-start | bytes 1572872 | tf_op jit(solution)/shard_map/ppermute | solution.py:546
  122.1 3.2 %collective-permute-done.16.refs_3_ = bf16[1024,256]{1,0:T(8,128)(2,1)S(1)} collective-permute-done((bf16[1024,256]{1,0:T(8,128)(2,1)S(1)}, bf16[1024,256]{1,0:T(8,128)(2,1)S(1)}, u32[]{:S(2)}, u32[]{:S(2)}) %collective-permute-start.16) | collective-permute-done | bytes 524320 | tf_op jit(solution)/shard_map/ppermute | solution.py:438
  129.1 15.5 %collective-permute-start.23 = (bf16[1024,256]{1,0:T(8,128)(2,1)S(1)}, bf16[1024,256]{1,0:T(8,128)(2,1)S(1)}, u32[]{:S(2)}, u32[]{:S(2)}) collective-permute-start(bf16[1024,256]{1,0:T(8,128)(2,1)S(1)} %get-tuple-element.88), channel_id=1, source_target_pairs={{8,0},{12,4},{0,8},{4,12},{9,1},{13,5},{1,9},{5,13},{10,2},{14,6},... | collective-permute-start | bytes 1572872 | tf_op jit(solution)/shard_map/ppermute | solution.py:546
  146.2 19.8 %collective-permute-start.26 = (bf16[1024,256]{1,0:T(8,128)(2,1)S(1)}, bf16[1024,256]{1,0:T(8,128)(2,1)S(1)}, u32[]{:S(2)}, u32[]{:S(2)}) collective-permute-start(bf16[1024,256]{1,0:T(8,128)(2,1)S(1)} %get-tuple-element.93), channel_id=1, source_target_pairs={{8,0},{12,4},{0,8},{4,12},{9,1},{13,5},{1,9},{5,13},{10,2},{14,6},... | collective-permute-start | bytes 1572872 | tf_op jit(solution)/shard_map/ppermute | solution.py:546
  166.8 10.3 %collective-permute-done.26.refs_5_ = bf16[1024,256]{1,0:T(8,128)(2,1)S(1)} collective-permute-done((bf16[1024,256]{1,0:T(8,128)(2,1)S(1)}, bf16[1024,256]{1,0:T(8,128)(2,1)S(1)}, u32[]{:S(2)}, u32[]{:S(2)}) %collective-permute-start.26) | collective-permute-done | bytes 524320 | tf_op jit(solution)/shard_map/ppermute | solution.py:546
  177.1 1.5 final_merge.7
  178.7 18.4 %packed_mlp.1 = bf16[1,1024,1024]{2,1,0:T(8,128)(2,1)} custom-call(bf16[1024,256]{1,0:T(8,128)(2,1)S(1)} %get-tuple-element.82.refs_0_, bf16[1024,256]{1,0:T(8,128)(2,1)S(1)} %get-tuple-element.87.refs_1_, bf16[1024,256]{1,0:T(8,128)(2,1)S(1)} %get-tuple-element.92.refs_2_, bf16[1024,256]{1,0:T(8,128)(2,1)S(1)} %get-tuple-element.95.refs_3_, ...), custom_call_target="tpu_custom_call" | custom-call | tf_op jit(solution)/shard_map/packed_mlp/pallas_call | solution.py:420
  (66 shorter events, 20.9 us)
Async XLA Ops:
  6.5 32.3 %copy-start.7 = (s32[1,8]{1,0:T(1,128)S(1)}, s32[1,8]{1,0:T(1,128)}, u32[]{:S(2)}) copy-start(s32[1,8]{1,0:T(1,128)} %refs_2_.5) | copy-start | bytes 100
  6.5 172.1 %all-gather.2.cloned.1.call-start = ((), (), s32[]{:S(2)}) async-start(), calls=%async_computation | async-start | bytes 14155776 | tf_op jit(solution)/shard_map/all_gather | solution.py:522
  7.2 5.6 %collective-permute-start = (s32[8]{0:T(128)S(1)}, s32[8]{0:T(128)S(1)}, u32[]{:S(2)}, u32[]{:S(2)}) collective-permute-start(s32[8]{0:T(128)S(1)} %compare_select_fusion), channel_id=1, source_target_pairs={{0,16},{4,20},{8,24},{12,28},{16,0},{20,4},{24,8},{28,12},{1,17},{... | collective-permute-start | bytes 104 | tf_op jit(solution)/shard_map/ppermute | solution.py:438
  12.8 3.5 %collective-permute-start.1 = (s32[8]{0:T(128)S(1)}, s32[8]{0:T(128)S(1)}, u32[]{:S(2)}, u32[]{:S(2)}) collective-permute-start(s32[8]{0:T(128)S(1)} %fusion), channel_id=1, source_target_pairs={{0,8},{4,12},{8,0},{12,4},{16,24},{20,28},{24,16},{28,20},{1,9},{5... | collective-permute-start | bytes 104 | tf_op jit(solution)/shard_map/ppermute | solution.py:438
  18.2 14.2 %copy-start.4 = (bf16[32,32,32]{2,1,0:T(8,128)(2,1)S(1)}, bf16[32,32,32]{2,1,0:T(8,128)(2,1)}, u32[]{:S(2)}) copy-start(bf16[32,32,32]{2,1,0:T(8,128)(2,1)} %refs_1_.1) | copy-start | bytes 196612
  18.3 21.8 %collective-permute-start.7 = (bf16[192,1024]{1,0:T(8,128)(2,1)S(1)}, bf16[192,1024]{1,0:T(8,128)(2,1)S(1)}, u32[]{:S(2)}, u32[]{:S(2)}) collective-permute-start(bf16[192,1024]{1,0:T(8,128)(2,1)S(1)} %get-tuple-element.60.refs_1_), channel_id=1, source_target_pairs={{0,16},{4,20},{8,24},{12,28},{16,0},{20,4},{24,8},{28,12},{1,17},{... | collective-permute-start | bytes 1179656 | tf_op jit(solution)/shard_map/ppermute | solution.py:438
  21.3 3.5 %collective-permute-start.2 = (s32[8]{0:T(128)S(1)}, s32[8]{0:T(128)S(1)}, u32[]{:S(2)}, u32[]{:S(2)}) collective-permute-start(s32[8]{0:T(128)S(1)} %fusion.1.refs_2_), channel_id=1, source_target_pairs={{0,4},{4,0},{8,12},{12,8},{16,20},{20,16},{24,28},{28,24},{1,5},{5... | collective-permute-start | bytes 104 | tf_op jit(solution)/shard_map/ppermute | solution.py:438
  24.9 1.6 copy-start
  28.1 10.8 %copy-start.1 = (bf16[1,1024,1024]{2,1,0:T(8,128)(2,1)S(1)}, bf16[1,1024,1024]{2,1,0:T(8,128)(2,1)}, u32[]{:S(2)}) copy-start(bf16[1,1024,1024]{2,1,0:T(8,128)(2,1)} %refs_8_.3) | copy-start | bytes 6291460
  30.5 2.9 %collective-permute-start.3 = (bf16[8,32,256]{2,1,0:T(8,128)(2,1)S(1)}, bf16[8,32,256]{2,1,0:T(8,128)(2,1)S(1)}, u32[]{:S(2)}, u32[]{:S(2)}) collective-permute-start(bf16[8,32,256]{2,1,0:T(8,128)(2,1)S(1)} %get-tuple-element.55), channel_id=1, source_target_pairs={{0,1},{1,0},{2,3},{3,2},{4,5},{5,4},{6,7},{7,6},{8,9},{9,8},{10,11... | collective-permute-start | bytes 393224 | tf_op jit(solution)/shard_map/ppermute | solution.py:438
  30.6 6.4 %collective-permute-start.4 = (bf16[8,32,256]{2,1,0:T(8,128)(2,1)S(1)}, bf16[8,32,256]{2,1,0:T(8,128)(2,1)S(1)}, u32[]{:S(2)}, u32[]{:S(2)}) collective-permute-start(bf16[8,32,256]{2,1,0:T(8,128)(2,1)S(1)} %get-tuple-element.56), channel_id=1, source_target_pairs={{0,2},{1,3},{2,0},{3,1},{4,6},{5,7},{6,4},{7,5},{8,10},{9,11},{10,... | collective-permute-start | bytes 393224 | tf_op jit(solution)/shard_map/ppermute | solution.py:438
  32.2 6.7 %collective-permute-start.5 = (bf16[8,32,256]{2,1,0:T(8,128)(2,1)S(1)}, bf16[8,32,256]{2,1,0:T(8,128)(2,1)S(1)}, u32[]{:S(2)}, u32[]{:S(2)}) collective-permute-start(bf16[8,32,256]{2,1,0:T(8,128)(2,1)S(1)} %get-tuple-element.57), channel_id=1, source_target_pairs={{0,3},{1,2},{2,1},{3,0},{4,7},{5,6},{6,5},{7,4},{8,11},{9,10},{10,... | collective-permute-start | bytes 393224 | tf_op jit(solution)/shard_map/ppermute | solution.py:438
  41.1 24.9 %collective-permute-start.14 = (bf16[2,192,1024]{2,1,0:T(8,128)(2,1)S(1)}, bf16[2,192,1024]{2,1,0:T(8,128)(2,1)S(1)}, u32[]{:S(2)}, u32[]{:S(2)}) collective-permute-start(bf16[2,192,1024]{2,1,0:T(8,128)(2,1)S(1)} %get-tuple-element.70.refs_1_), channel_id=1, source_target_pairs={{0,8},{4,12},{8,0},{12,4},{16,24},{20,28},{24,16},{28,20},{1,9},{5... | collective-permute-start | bytes 2359304 | tf_op jit(solution)/shard_map/ppermute | solution.py:438
  42.7 13.8 %collective-permute-start.6 = (bf16[1024,256]{1,0:T(8,128)(2,1)S(1)}, bf16[1024,256]{1,0:T(8,128)(2,1)S(1)}, u32[]{:S(2)}, u32[]{:S(2)}) collective-permute-start(bf16[1024,256]{1,0:T(8,128)(2,1)S(1)} %get-tuple-element.59.refs_2_), channel_id=1, source_target_pairs={{0,4},{4,0},{8,12},{12,8},{16,20},{20,16},{24,28},{28,24},{1,5},{5... | collective-permute-start | bytes 1572872 | tf_op jit(solution)/shard_map/ppermute | solution.py:438
  44.2 13.1 %collective-permute-start.10 = (bf16[8,32,768]{2,1,0:T(8,128)(2,1)S(1)}, bf16[8,32,768]{2,1,0:T(8,128)(2,1)S(1)}, u32[]{:S(2)}, u32[]{:S(2)}) collective-permute-start(bf16[8,32,768]{2,1,0:T(8,128)(2,1)S(1)} %get-tuple-element.65), channel_id=1, source_target_pairs={{0,1},{1,0},{2,3},{3,2},{4,5},{5,4},{6,7},{7,6},{8,9},{9,8},{10,11... | collective-permute-start | bytes 1179656 | tf_op jit(solution)/shard_map/ppermute | solution.py:438
  44.2 13.1 %collective-permute-start.11 = (bf16[8,32,768]{2,1,0:T(8,128)(2,1)S(1)}, bf16[8,32,768]{2,1,0:T(8,128)(2,1)S(1)}, u32[]{:S(2)}, u32[]{:S(2)}) collective-permute-start(bf16[8,32,768]{2,1,0:T(8,128)(2,1)S(1)} %get-tuple-element.66), channel_id=1, source_target_pairs={{0,2},{1,3},{2,0},{3,1},{4,6},{5,7},{6,4},{7,5},{8,10},{9,11},{10,... | collective-permute-start | bytes 1179656 | tf_op jit(solution)/shard_map/ppermute | solution.py:438
  45.7 18.0 %collective-permute-start.12 = (bf16[8,32,768]{2,1,0:T(8,128)(2,1)S(1)}, bf16[8,32,768]{2,1,0:T(8,128)(2,1)S(1)}, u32[]{:S(2)}, u32[]{:S(2)}) collective-permute-start(bf16[8,32,768]{2,1,0:T(8,128)(2,1)S(1)} %get-tuple-element.67), channel_id=1, source_target_pairs={{0,3},{1,2},{2,1},{3,0},{4,7},{5,6},{6,5},{7,4},{8,11},{9,10},{10,... | collective-permute-start | bytes 1179656 | tf_op jit(solution)/shard_map/ppermute | solution.py:438
  67.9 21.0 %collective-permute-start.13 = (bf16[1024,256]{1,0:T(8,128)(2,1)S(1)}, bf16[1024,256]{1,0:T(8,128)(2,1)S(1)}, u32[]{:S(2)}, u32[]{:S(2)}) collective-permute-start(bf16[1024,256]{1,0:T(8,128)(2,1)S(1)} %get-tuple-element.69.refs_2_), channel_id=1, source_target_pairs={{0,4},{4,0},{8,12},{12,8},{16,20},{20,16},{24,28},{28,24},{1,5},{5... | collective-permute-start | bytes 1572872 | tf_op jit(solution)/shard_map/ppermute | solution.py:438
  68.5 22.6 %collective-permute-start.8 = (bf16[1024,256]{1,0:T(8,128)(2,1)S(1)}, bf16[1024,256]{1,0:T(8,128)(2,1)S(1)}, u32[]{:S(2)}, u32[]{:S(2)}) collective-permute-start(bf16[1024,256]{1,0:T(8,128)(2,1)S(1)} %get-tuple-element.63.refs_2_), channel_id=1, source_target_pairs={{16,8},{20,12},{24,16},{28,20},{8,24},{12,28},{17,9},{21,13},{25,1... | collective-permute-start | bytes 1572872 | tf_op jit(solution)/shard_map/ppermute | solution.py:541
  69.2 22.7 %collective-permute-start.9 = (bf16[1024,256]{1,0:T(8,128)(2,1)S(1)}, bf16[1024,256]{1,0:T(8,128)(2,1)S(1)}, u32[]{:S(2)}, u32[]{:S(2)}) collective-permute-start(bf16[1024,256]{1,0:T(8,128)(2,1)S(1)} %get-tuple-element.63.refs_2_), channel_id=1, source_target_pairs={{24,8},{28,12},{8,24},{12,28},{25,9},{29,13},{9,25},{13,29},{26,10... | collective-permute-start | bytes 1572872 | tf_op jit(solution)/shard_map/ppermute | solution.py:542
  69.9 40.9 %collective-permute-start.19 = (bf16[1024,256]{1,0:T(8,128)(2,1)S(1)}, bf16[1024,256]{1,0:T(8,128)(2,1)S(1)}, u32[]{:S(2)}, u32[]{:S(2)}) collective-permute-start(bf16[1024,256]{1,0:T(8,128)(2,1)S(1)} %get-tuple-element.77.refs_2_), channel_id=1, source_target_pairs={{0,4},{4,0},{8,12},{12,8},{16,20},{20,16},{24,28},{28,24},{1,5},{5... | collective-permute-start | bytes 1572872 | tf_op jit(solution)/shard_map/ppermute | solution.py:438
  89.6 22.6 %collective-permute-start.17 = (bf16[1024,256]{1,0:T(8,128)(2,1)S(1)}, bf16[1024,256]{1,0:T(8,128)(2,1)S(1)}, u32[]{:S(2)}, u32[]{:S(2)}) collective-permute-start(bf16[1024,256]{1,0:T(8,128)(2,1)S(1)} %get-tuple-element.76.refs_2_), channel_id=1, source_target_pairs={{16,8},{20,12},{24,16},{28,20},{8,24},{12,28},{17,9},{21,13},{25,1... | collective-permute-start | bytes 1572872 | tf_op jit(solution)/shard_map/ppermute | solution.py:541
  90.3 22.6 %collective-permute-start.18 = (bf16[1024,256]{1,0:T(8,128)(2,1)S(1)}, bf16[1024,256]{1,0:T(8,128)(2,1)S(1)}, u32[]{:S(2)}, u32[]{:S(2)}) collective-permute-start(bf16[1024,256]{1,0:T(8,128)(2,1)S(1)} %get-tuple-element.76.refs_2_), channel_id=1, source_target_pairs={{24,8},{28,12},{8,24},{12,28},{25,9},{29,13},{9,25},{13,29},{26,10... | collective-permute-start | bytes 1572872 | tf_op jit(solution)/shard_map/ppermute | solution.py:542
  91.0 34.2 %collective-permute-start.16 = (bf16[1024,256]{1,0:T(8,128)(2,1)S(1)}, bf16[1024,256]{1,0:T(8,128)(2,1)S(1)}, u32[]{:S(2)}, u32[]{:S(2)}) collective-permute-start(bf16[1024,256]{1,0:T(8,128)(2,1)S(1)} %get-tuple-element.75.refs_2_), channel_id=1, source_target_pairs={{0,4},{4,0},{8,12},{12,8},{16,20},{20,16},{24,28},{28,24},{1,5},{5... | collective-permute-start | bytes 1572872 | tf_op jit(solution)/shard_map/ppermute | solution.py:438
  92.7 34.0 %collective-permute-start.15 = (bf16[1024,256]{1,0:T(8,128)(2,1)S(1)}, bf16[1024,256]{1,0:T(8,128)(2,1)S(1)}, u32[]{:S(2)}, u32[]{:S(2)}) collective-permute-start(bf16[1024,256]{1,0:T(8,128)(2,1)S(1)} %get-tuple-element.74), channel_id=1, source_target_pairs={{8,0},{12,4},{0,8},{4,12},{9,1},{13,5},{1,9},{5,13},{10,2},{14,6},... | collective-permute-start | bytes 1572872 | tf_op jit(solution)/shard_map/ppermute | solution.py:546
  111.6 16.7 %collective-permute-start.21 = (bf16[1024,256]{1,0:T(8,128)(2,1)S(1)}, bf16[1024,256]{1,0:T(8,128)(2,1)S(1)}, u32[]{:S(2)}, u32[]{:S(2)}) collective-permute-start(bf16[1024,256]{1,0:T(8,128)(2,1)S(1)} %get-tuple-element.84.refs_2_), channel_id=1, source_target_pairs={{16,8},{20,12},{24,16},{28,20},{8,24},{12,28},{17,9},{21,13},{25,1... | collective-permute-start | bytes 1572872 | tf_op jit(solution)/shard_map/ppermute | solution.py:541
  112.3 16.0 %collective-permute-start.22 = (bf16[1024,256]{1,0:T(8,128)(2,1)S(1)}, bf16[1024,256]{1,0:T(8,128)(2,1)S(1)}, u32[]{:S(2)}, u32[]{:S(2)}) collective-permute-start(bf16[1024,256]{1,0:T(8,128)(2,1)S(1)} %get-tuple-element.84.refs_2_), channel_id=1, source_target_pairs={{24,8},{28,12},{8,24},{12,28},{25,9},{29,13},{9,25},{13,29},{26,10... | collective-permute-start | bytes 1572872 | tf_op jit(solution)/shard_map/ppermute | solution.py:542
  113.8 30.7 %collective-permute-start.20 = (bf16[1024,256]{1,0:T(8,128)(2,1)S(1)}, bf16[1024,256]{1,0:T(8,128)(2,1)S(1)}, u32[]{:S(2)}, u32[]{:S(2)}) collective-permute-start(bf16[1024,256]{1,0:T(8,128)(2,1)S(1)} %get-tuple-element.83), channel_id=1, source_target_pairs={{8,0},{12,4},{0,8},{4,12},{9,1},{13,5},{1,9},{5,13},{10,2},{14,6},... | collective-permute-start | bytes 1572872 | tf_op jit(solution)/shard_map/ppermute | solution.py:546
  126.0 19.3 %collective-permute-start.24 = (bf16[1024,256]{1,0:T(8,128)(2,1)S(1)}, bf16[1024,256]{1,0:T(8,128)(2,1)S(1)}, u32[]{:S(2)}, u32[]{:S(2)}) collective-permute-start(bf16[1024,256]{1,0:T(8,128)(2,1)S(1)} %get-tuple-element.89.refs_2_), channel_id=1, source_target_pairs={{16,8},{20,12},{24,16},{28,20},{8,24},{12,28},{17,9},{21,13},{25,1... | collective-permute-start | bytes 1572872 | tf_op jit(solution)/shard_map/ppermute | solution.py:541
  126.8 18.6 %collective-permute-start.25 = (bf16[1024,256]{1,0:T(8,128)(2,1)S(1)}, bf16[1024,256]{1,0:T(8,128)(2,1)S(1)}, u32[]{:S(2)}, u32[]{:S(2)}) collective-permute-start(bf16[1024,256]{1,0:T(8,128)(2,1)S(1)} %get-tuple-element.89.refs_2_), channel_id=1, source_target_pairs={{24,8},{28,12},{8,24},{12,28},{25,9},{29,13},{9,25},{13,29},{26,10... | collective-permute-start | bytes 1572872 | tf_op jit(solution)/shard_map/ppermute | solution.py:542
  129.1 36.9 %collective-permute-start.23 = (bf16[1024,256]{1,0:T(8,128)(2,1)S(1)}, bf16[1024,256]{1,0:T(8,128)(2,1)S(1)}, u32[]{:S(2)}, u32[]{:S(2)}) collective-permute-start(bf16[1024,256]{1,0:T(8,128)(2,1)S(1)} %get-tuple-element.88), channel_id=1, source_target_pairs={{8,0},{12,4},{0,8},{4,12},{9,1},{13,5},{1,9},{5,13},{10,2},{14,6},... | collective-permute-start | bytes 1572872 | tf_op jit(solution)/shard_map/ppermute | solution.py:546
  146.2 30.9 %collective-permute-start.26 = (bf16[1024,256]{1,0:T(8,128)(2,1)S(1)}, bf16[1024,256]{1,0:T(8,128)(2,1)S(1)}, u32[]{:S(2)}, u32[]{:S(2)}) collective-permute-start(bf16[1024,256]{1,0:T(8,128)(2,1)S(1)} %get-tuple-element.93), channel_id=1, source_target_pairs={{8,0},{12,4},{0,8},{4,12},{9,1},{13,5},{1,9},{5,13},{10,2},{14,6},... | collective-permute-start | bytes 1572872 | tf_op jit(solution)/shard_map/ppermute | solution.py:546
  (4 other events, 3.5 us)
Sparse Core Ops, SparseCore 0:
  68.0 88.7 all-gather.1

commit v3 on v2

--- a/solution.py
+++ b/solution.py
@@ -128,12 +128,16 @@
 ANY = pl.BlockSpec(memory_space=pl.ANY)
 MIB = 1024 * 1024
 GROUP = 16
+BLOCKS = 2
+MLP_MIB = 30
 SUB = 8
 SPANS = (2, 2, 2, 2)
+BRIEF = 1
 TOKEN = jax.ShapeDtypeStruct((8, 128), jnp.int32)
 
 
-def local_call(kernel, name, limit, in_specs, out_specs, out_shape, after=(), grid=(), scratch=()):
+def local_call(kernel, name, limit, in_specs, out_specs, out_shape, after, grid=(), scratch=()):
+    after, cost = after
     ins, waits, outs = len(in_specs), len(after), len(out_specs)
 
     def body(*refs):
@@ -150,7 +154,7 @@
         out_shape=list(out_shape) + [TOKEN],
         scratch_shapes=list(scratch),
         compiler_params=pltpu.CompilerParams(vmem_limit_bytes=limit * MIB),
-        cost_estimate=pl.CostEstimate(flops=1, bytes_accessed=1, transcendentals=0),
+        cost_estimate=pl.CostEstimate(flops=cost, bytes_accessed=cost // 1000, transcendentals=0),
         name=name,
     )
 
@@ -166,7 +170,7 @@
     return (ids < length) & (occupied > 0)
 
 
-def first_kernel(ids_ref, lengths_ref, occ_ref, tile_ref, mix_ref, *out_refs):
+def first_kernel(ids_ref, length_ref, occ_ref, tile_ref, mix_ref, *out_refs):
     step = pl.program_id(0)
     blocks, blk_size = mix_ref.shape[:2]
     feat_width = tile_ref.shape[2]
@@ -177,7 +181,7 @@
     for i in range(blocks):
         block = step * blocks + i
         start = lane * rows_here + block * blk_size
-        live = live_rows(start, (blk_size, feat_width), lengths_ref[ids_ref[0]], occ_ref[0, block])
+        live = live_rows(start, (blk_size, feat_width), length_ref[0], occ_ref[0, block])
         tile = tile_ref[0, i * blk_size:(i + 1) * blk_size, :]
         masked = jnp.where(live, tile.astype(jnp.float32), 0.0)
         normed = rms_round(masked)
@@ -192,7 +196,7 @@
             begin = end
 
 
-def first_factor(ids, lengths, occupancy, tile_tokens, block_mix, parts, groups, after):
+def first_factor(ids, length, occupancy, tile_tokens, block_mix, parts, groups, after):
     blocks, blk_size, _ = block_mix.shape
     feat_width = tile_tokens.shape[2]
     share = blk_size // parts
@@ -212,7 +216,7 @@
         [jax.ShapeDtypeStruct((blocks, share, width), jnp.bfloat16) for width in groups for _ in range(parts)],
         after,
         grid=(blocks // each,),
-    )(ids, lengths, occupancy, tile_tokens, block_mix)
+    )(ids, length, occupancy, tile_tokens, block_mix)
 
 
 def spread_kernel(parts, ids_ref, stride_ref, out_ref):
@@ -364,72 +368,50 @@
     return local_call(final_kernel, "final_merge", 8, specs, [VMEM], [shape], after)(ids, lengths, own, one, two, last)
 
 
+NT = (((1,), (1,)), ((), ()))
+
+
 def mlp_kernel(pieces, *refs):
-    sources, refs = refs[:pieces], refs[pieces:]
-    main_ref, out_ref, gate_ref, up_ref, down_ref, sems = refs
-    step = pl.program_id(0)
-    here, levels = main_ref.shape[:2]
-    hidden_width, feat_width = gate_ref.shape
-    wide, thin = hidden_width // (here * levels), feat_width // (here * levels)
-    parts = levels
-    span = hidden_width // parts
-    gates = gate_ref.reshape(levels, here, wide, feat_width)
-    ups = up_ref.reshape(levels, here, wide, feat_width)
-    downs = down_ref.reshape(levels, here, thin, hidden_width)
-
-    def copies(part):
-        begin = part * span
-        at, cols = 2 * wide + begin // feat_width * thin, pl.ds(begin % feat_width, span)
-        found = [(main_ref.at[:, part, :wide], gates.at[part]), (main_ref.at[:, part, wide:2 * wide], ups.at[part])]
+    sources, (main_ref, out_ref) = refs[:pieces], refs[pieces:]
+    here, levels, each, feat_width = main_ref.shape
+    thin = feat_width // (here * levels)
+    wide = (each - 2 * thin) // 2
+    rows = out_ref.shape[1]
+    block = rows // BLOCKS
+
+    def weights(level, begin, count):
+        return main_ref[:, level, begin:begin + count, :].reshape(here * count, feat_width)
+
+    def times(values, matrix):
+        return lax.dot_general(values, matrix, NT, preferred_element_type=jnp.float32)
+
+    for at in range(0, rows, block):
+        mixed = jnp.concatenate([ref[at:at + block, :] for ref in sources], axis=1).astype(jnp.float32)
+        normed = rms_round(mixed)
+        hidden = []
         for level in range(levels):
-            found.append((main_ref.at[:, level, at:at + thin, cols], downs.at[level, :, :, begin:begin + span]))
-        return [pltpu.make_async_copy(src, dst, sems.at[part, i]) for i, (src, dst) in enumerate(found)]
-
-    @pl.when(step == 0)
-    def _():
-        for part in range(parts):
-            for copy in copies(part):
-                copy.start()
-
-    mixed = jnp.concatenate([ref[...] for ref in sources], axis=1).astype(jnp.float32)
-    normed = rms_round(mixed)
-    contract = (((1,), (1,)), ((), ()))
-    result = mixed
-    for part in range(parts):
-        @pl.when(step == 0)
-        def _():
-            for copy in copies(part):
-                copy.wait()
-
-        at = part * span
-        gate = lax.dot_general(normed, gate_ref[at:at + span, :], contract, preferred_element_type=jnp.float32)
-        up = lax.dot_general(normed, up_ref[at:at + span, :], contract, preferred_element_type=jnp.float32)
-        hidden = (gate / (1.0 + jnp.exp(-gate)) * up).astype(jnp.bfloat16)
-        down = down_ref[:, at:at + span]
-        result += lax.dot_general(hidden, down, contract, preferred_element_type=jnp.float32)
-    out_ref[0] = result.astype(out_ref.dtype)
+            gate = times(normed, weights(level, 0, wide))
+            up = times(normed, weights(level, wide, wide))
+            hidden.append((gate / (1.0 + jnp.exp(-gate)) * up).astype(jnp.bfloat16))
+        hidden = jnp.concatenate(hidden, axis=1)
+        halves = hidden.shape[1] // feat_width
+        for level in range(levels):
+            cols = slice(level * here * thin, (level + 1) * here * thin)
+            result = mixed[:, cols]
+            for part in range(halves):
+                inner = hidden[:, part * feat_width:(part + 1) * feat_width]
+                result += times(inner, weights(level, 2 * wide + part * thin, thin))
+            out_ref[0, at:at + block, cols] = result.astype(out_ref.dtype)
 
 
 def packed_mlp(sources, weights):
-    rows = sources[0].shape[0]
-    pieces = len(sources)
-    here, levels, each, feat_width = weights.shape
-    hidden_width = here * levels * (each - feat_width // (here * levels) * 2) // 2
-    steps = 2
-    block = rows // steps
+    rows, feat_width = sources[0].shape[0], weights.shape[3]
     return pl.pallas_call(
-        functools.partial(mlp_kernel, pieces),
-        grid=(steps,),
-        in_specs=[pl.BlockSpec((block, source.shape[1]), lambda i: (i, 0)) for source in sources] + [ANY],
-        out_specs=pl.BlockSpec((1, block, feat_width), lambda i: (0, i, 0)),
+        functools.partial(mlp_kernel, len(sources)),
+        in_specs=[VMEM] * (len(sources) + 1),
+        out_specs=VMEM,
         out_shape=jax.ShapeDtypeStruct((1, rows, feat_width), jnp.bfloat16),
-        scratch_shapes=[
-            pltpu.VMEM((hidden_width, feat_width), jnp.bfloat16),
-            pltpu.VMEM((hidden_width, feat_width), jnp.bfloat16),
-            pltpu.VMEM((feat_width, hidden_width), jnp.bfloat16),
-            pltpu.SemaphoreType.DMA((levels, 2 + levels)),
-        ],
-        compiler_params=pltpu.CompilerParams(vmem_limit_bytes=40 * MIB),
+        compiler_params=pltpu.CompilerParams(vmem_limit_bytes=MLP_MIB * MIB),
         name="packed_mlp",
     )(*sources, weights)
 
@@ -498,70 +480,114 @@
     return lengths
 
 
+ORDER = (
+    ("first",),
+    ("lengths",),
+    ("pack",),
+    ("spread",),
+    ("second", 0),
+    ("wide", 0),
+    ("second", 1),
+    ("join", 0),
+    ("after_two", 0),
+    ("join", 1),
+    ("wide", 1),
+    ("forward", 0),
+    ("join", 2),
+    ("forward", 1),
+    ("finish", 0),
+    ("join", 3),
+    ("forward", 2),
+    ("finish", 1),
+    ("forward", 3),
+    ("after_weights",),
+    ("finish", 2),
+    ("finish", 3),
+)
+
+
 def packed_device(tile_tokens, page_lengths, occupancy, block_mix, stride_mix, w_gate_up, w_down):
     ids = jnp.stack([lax.axis_index("page"), lax.axis_index("tok")]).astype(jnp.int32)
     pages, parts = lax.axis_size("page"), lax.axis_size("tok")
     feat_width = tile_tokens.shape[2]
     spans = [feat_width * eighths // 8 for eighths in SPANS]
-    groups = (spans[0], feat_width - spans[0])
-    z_far, z_near = (0, 4), (0, 2)
-    tokens = []
-
-    def chained(step, *operands):
-        results, token = step(*operands, tokens[-1:])
-        tokens.append(token)
+    tokens, held = [], {}
+
+    def chained(name, step, *operands):
+        results, token = step(*operands, (list(tokens), BRIEF))
+        tokens[:] = [token]
         return results
-
-    def paired(value, which, place):
-        axis, shift = which
-        return chained(pair_up, ids, value, swap(value, AXES[axis], shift), which, place)[0]
 
     def plane(value):
         here = 2 * parts
         groups = [[level * here + i for i in range(here)] for level in range(pages // 2)]
         return lax.all_gather(value.reshape((-1,) + value.shape[2:]), AXES, axis_index_groups=groups)
 
-    def across(firsts):
-        return firsts[:1] + [swap(firsts[part], "tok", part) for part in range(1, parts)]
-
     far_lengths = some_lengths(page_lengths[0], pages // 2, 1)
-    tokens.append(far_lengths)
-    weights = chained(pack_weights, jnp.swapaxes(w_gate_up, 1, 2), jnp.swapaxes(w_down, 0, 1))[0]
     lengths = far_lengths + swap(far_lengths, "page", 1)
-    firsts = chained(first_factor, ids, lengths, occupancy, tile_tokens, block_mix, parts, groups)
-    found = [across(firsts[:parts]), across(firsts[parts:])]
-    spread = chained(spread_stride, ids, stride_mix, parts)[0]
-    turned = chained(second_factor, 0, spans[:1], ids, lengths, occupancy, spread, found[0], tile_tokens)
-    weights = paired(weights, z_far, 0)
-    swapped = [swap(own, "page", 1) for own in turned]
-    current, one, two, last, sources = {}, {}, {}, {}, []
+    place = [ids, lengths]
+
+    def swap_pages(k, own):
+        held["own", k], held["got", k] = own, swap(own, "page", 1)
+
+    def pack():
+        value = chained("pack", pack_weights, jnp.swapaxes(w_gate_up, 1, 2), jnp.swapaxes(w_down, 0, 1))[0]
+        held["weights"], held["across"] = value, swap(value, "page", 4)
+
+    def first():
+        groups = (spans[0], sum(spans[1:]))
+        found = chained("first", first_factor, ids, page_lengths, occupancy, tile_tokens, block_mix, parts, groups)
+        for k in range(2):
+            mine = found[k * parts:(k + 1) * parts]
+            held["first", k] = mine[:1] + [swap(mine[other], "tok", other) for other in range(1, parts)]
+
+    def spread():
+        held["spread"] = chained("spread", spread_stride, ids, stride_mix, parts)[0]
+
+    def second(k):
+        begin, here = (spans[0], spans[1:]) if k else (0, spans[:1])
+        operands = (begin, here, *place, occupancy, held["spread"], held["first", k], tile_tokens)
+        for i, own in enumerate(chained("second", second_factor, *operands)):
+            swap_pages(k + i, own)
+
+    def wide(k):
+        value = chained("wide", pair_up, ids, held["weights"], held["across"], (0, 4 - 2 * k), k)[0]
+        if k:
+            held["weights"] = plane(value)
+        else:
+            held["weights"], held["across"] = value, swap(value, "page", 2)
 
     def join(k):
-        current[k] = chained(join_parity, ids, lengths, turned[k], swapped[k])[0]
-        one[k] = lax.ppermute(current[k], "page", [(4, 2), (5, 3), (6, 4), (7, 5), (2, 6), (3, 7)])
-        two[k] = lax.ppermute(current[k], "page", [(6, 2), (7, 3), (2, 6), (3, 7)])
+        value = chained("join", join_parity, *place, held["own", k], held["got", k])[0]
+        held["one", k] = lax.ppermute(value, "page", [(4, 2), (5, 3), (6, 4), (7, 5), (2, 6), (3, 7)])
+        held["two", k] = lax.ppermute(value, "page", [(6, 2), (7, 3), (2, 6), (3, 7)])
+        held["own", k] = value
 
     def forward(k):
-        merged = chained(forward_merge, ids, lengths, current[k], one[k], two[k])[0]
-        last[k] = lax.ppermute(merged, "page", [(2, 0), (3, 1), (0, 2), (1, 3)])
+        value = chained("forward", forward_merge, *place, held["own", k], held["one", k], held["two", k])[0]
+        held["last", k] = lax.ppermute(value, "page", [(2, 0), (3, 1), (0, 2), (1, 3)])
 
     def finish(k):
-        sources.extend(chained(final_merge, ids, lengths, current[k], one[k], two[k], last[k]))
-
-    join(0)
-    turned += chained(second_factor, spans[0], spans[1:], ids, lengths, occupancy, spread, found[1], tile_tokens)
-    swapped += [swap(own, "page", 1) for own in turned[1:]]
-    weights = plane(paired(weights, z_near, 1))
-    join(1)
-    count = len(spans)
-    for k in range(count):
-        forward(k)
-        if k + 2 < count:
-            join(k + 2)
-        if k:
-            finish(k - 1)
-    finish(count - 1)
-    return packed_mlp(sources, weights)
+        found = [held[kind, k] for kind in ("own", "one", "two", "last")]
+        held["source", k] = chained("finish", final_merge, *place, *found)[0]
+
+    def lengths_first():
+        tokens.append(far_lengths)
+
+    def after_one(k):
+        tokens.append(held["one", k])
+
+    def after_two(k):
+        tokens.append(held["two", k])
+
+    def after_weights():
+        tokens.append(held["weights"])
+
+    steps = dict(pack=pack, first=first, spread=spread, second=second, wide=wide, join=join, forward=forward, finish=finish)
+    steps.update(lengths=lengths_first, after_one=after_one, after_two=after_two, after_weights=after_weights)
+    for name, *which in ORDER:
+        steps[name](*which)
+    return packed_mlp([held["source", k] for k in range(len(spans))], held["weights"])
 
 
 def solution(mesh):

time: 204 us -> 200 us (0.980)
  waiting for transfers between devices: 69.9 us -> 34.7 us
  starting transfers between devices: 76.2 us -> 100 us
  local copies, waits for them, and re-layouts: 5.06 us -> 11.4 us
    ppermute x12, starting transfers between devices: 55.8 us -> 84.7 us  [the longest x4 79.2 us: forward(): lax.ppermute(value, 'page', [(2, 0), (3, 1), (0, 2), (1, 3)])]
    ppermute x15, waiting for transfers between devices: 59.5 us -> 32 us  [swap(): lax.ppermute(value, axis, [(i, i ^ bit) for i in range(lax.axis_size(axis...]
    ppermute x12, waiting for transfers between devices: 10.4 us -> 2.72 us  [the longest x4 2.7 us: forward(): lax.ppermute(value, 'page', [(2, 0), (3, 1), (0, 2), (1, 3)])]
    unnamed x16 -> x36, local copies, waits for them, and re-layouts: 5.06 us -> 11.4 us
    ppermute x15, starting transfers between devices: 20.4 us -> 15.6 us  [swap(): lax.ppermute(value, axis, [(i, i ^ bit) for i in range(lax.axis_size(axis...]
    pallas_call x1, Pallas kernels: 18.4 us -> 15.1 us  [packed_mlp(): pl.pallas_call(functools.partial(mlp_kernel, len(sources)), in_specs=[VME...]
    pallas_call x19, Pallas kernels: 19.9 us -> 23.2 us  [run(): *results, token = call(*operands, *after)]
  transfers between devices with their start and end apart: 28 -> 28, of which waited for: 11 -> 6; matrix products, arithmetic and copies ran while one was open for 0% -> 0% of each run, Pallas kernels for 8% -> 9%
where the time goes in v3:
time: 200 us; the launch traced here: 199 us
  starting transfers between devices  100 us (50%)
  Pallas kernels  38.3 us (19%)
  waiting for transfers between devices  34.7 us (17%)
  between operations  14.5 us (7%)
  local copies, waits for them, and re-layouts  11.4 us (6%)
    ppermute x4, starting transfers between devices, forward(): lax.ppermute(value, 'page', [(2, 0), (3, 1), (0, 2), (1, 3)])  79.2 us
    ppermute x15, waiting for transfers between devices, swap(): lax.ppermute(value, axis, [(i, i ^ bit) for i in range(lax.axis_size(axis...  32 us
    pallas_call x19, Pallas kernels, run(): *results, token = call(*operands, *after)  23.2 us
    ppermute x15, starting transfers between devices, swap(): lax.ppermute(value, axis, [(i, i ^ bit) for i in range(lax.axis_size(axis...  15.6 us
    pallas_call x1, Pallas kernels, packed_mlp(): pl.pallas_call(functools.partial(mlp_kernel, len(sources)), in_specs=[VME...  15.1 us
    unnamed x36, local copies, waits for them, and re-layouts  11.4 us
  transfers between devices with their start and end apart: 28, of which 6 were waited for; matrix products, arithmetic and copies ran while one was open for 0% of the time, Pallas kernels for 9%

profile of v3, /device:TPU:0, one launch (start us, length us, event | category | flops | bytes accessed | tf_op | source)
XLA Modules:
  0.0 199.2 jit_solution(1367301964205297137)
XLA Ops:
  7.2 4.1 %collective-permute-start = (s32[8]{0:T(128)S(1)}, s32[8]{0:T(128)S(1)}, u32[]{:S(2)}, u32[]{:S(2)}) collective-permute-start(s32[8]{0:T(128)S(1)} %compare_select_fusion), channel_id=1, source_target_pairs={{0,16},{4,20},{8,24},{12,28},{16,0},{20,4},{24,8},{28,12},{1,17},{... | collective-permute-start | bytes 104 | tf_op jit(solution)/shard_map/ppermute | solution.py:420
  11.4 1.6 copy-done.2
  13.0 0.9 copy-done.12
  14.6 2.4 %first_factor.1 = (bf16[8,32,256]{2,1,0:T(8,128)(2,1)S(1)}, bf16[8,32,256]{2,1,0:T(8,128)(2,1)S(1)}, bf16[8,32,256]{2,1,0:T(8,128)(2,1)S(1)}, bf16[8,32,256]{2,1...) custom-call(s32[2]{0:T(128)S(1)} %pad_add_fusion.refs_0_, ...), custom_call_target="tpu_custom_call" | custom-call | flops 1 | tf_op jit(solution)/shard_map/first_factor/pallas_call | solution.py:162
  17.1 1.6 collective-permute-start.4
  19.0 1.6 collective-permute-start.1
  20.5 2.0 collective-permute-done.1
  22.5 0.9 copy-done.15
  23.7 1.7 collective-permute-start.2
  25.3 1.0 spread_stride.1
  26.3 0.9 collective-permute-done.2
  27.3 1.2 second_factor.2
  28.5 1.7 collective-permute-start.6
  30.2 1.5 collective-permute-start.8
  32.0 11.3 %collective-permute-done.10.refs_2_ = bf16[192,1024]{1,0:T(8,128)(2,1)S(1)} collective-permute-done((bf16[192,1024]{1,0:T(8,128)(2,1)S(1)}, bf16[192,1024]{1,0:T(8,128)(2,1)S(1)}, u32[]{:S(2)}, u32[]{:S(2)}) %collective-permute-start.10) | collective-permute-done | bytes 393248 | tf_op jit(solution)/shard_map/ppermute | solution.py:420
  43.3 1.0 pair_up.2
  44.5 5.3 %collective-permute-done.9.refs_7_ = bf16[8,32,768]{2,1,0:T(8,128)(2,1)S(1)} collective-permute-done((bf16[8,32,768]{2,1,0:T(8,128)(2,1)S(1)}, bf16[8,32,768]{2,1,0:T(8,128)(2,1)S(1)}, u32[]{:S(2)}, u32[]{:S(2)}) %collective-permute-start.9) | collective-permute-done | bytes 393248 | tf_op jit(solution)/shard_map/ppermute | solution.py:420
  49.8 3.0 %second_factor.3 = (bf16[1024,256]{1,0:T(8,128)(2,1)S(1)}, bf16[1024,256]{1,0:T(8,128)(2,1)S(1)}, bf16[1024,256]{1,0:T(8,128)(2,1)}, s32[8,128]{1,0:T(8,128)S(1)}) custom-call(s32[2]{0:T(128)S(1)} %pad_add_fusion.refs_0_, s32[8]{0:T(128)S(1)} %add.11.refs_1_, s32[1,8]{1,0:T(1,128)S(1)} %copy-done.17, bf16[2,512,512]{2,1,0:T(8,128)(2,1)S(1)} %get-tuple-element.53.refs_3_, ...), custom_call_target="tpu_custom_call" | custom-call | flops 1 | tf_op jit(solution)/shard_map/second_factor/pallas_call | solution.py:162
  54.6 12.5 %collective-permute-done.14.refs_3_ = bf16[1024,256]{1,0:T(8,128)(2,1)S(1)} collective-permute-done((bf16[1024,256]{1,0:T(8,128)(2,1)S(1)}, bf16[1024,256]{1,0:T(8,128)(2,1)S(1)}, u32[]{:S(2)}, u32[]{:S(2)}) %collective-permute-start.14) | collective-permute-done | bytes 524320 | tf_op jit(solution)/shard_map/ppermute | solution.py:420
  67.9 1.8 pair_up.3
  73.1 24.2 %collective-permute-start.15 = (bf16[1024,256]{1,0:T(8,128)(2,1)S(1)}, bf16[1024,256]{1,0:T(8,128)(2,1)S(1)}, u32[]{:S(2)}, u32[]{:S(2)}) collective-permute-start(bf16[1024,256]{1,0:T(8,128)(2,1)S(1)} %get-tuple-element.74), channel_id=1, source_target_pairs={{8,0},{12,4},{0,8},{4,12},{9,1},{13,5},{1,9},{5,13},{10,2},{14,6},... | collective-permute-start | bytes 1572872 | tf_op jit(solution)/shard_map/ppermute | solution.py:568
  97.3 1.6 collective-permute-start.22
  101.9 19.8 %collective-permute-start.19 = (bf16[1024,256]{1,0:T(8,128)(2,1)S(1)}, bf16[1024,256]{1,0:T(8,128)(2,1)S(1)}, u32[]{:S(2)}, u32[]{:S(2)}) collective-permute-start(bf16[1024,256]{1,0:T(8,128)(2,1)S(1)} %get-tuple-element.81), channel_id=1, source_target_pairs={{8,0},{12,4},{0,8},{4,12},{9,1},{13,5},{1,9},{5,13},{10,2},{14,6},... | collective-permute-start | bytes 1572872 | tf_op jit(solution)/shard_map/ppermute | solution.py:568
  122.5 1.5 join_parity.7
  126.2 16.0 %collective-permute-start.23 = (bf16[1024,256]{1,0:T(8,128)(2,1)S(1)}, bf16[1024,256]{1,0:T(8,128)(2,1)S(1)}, u32[]{:S(2)}, u32[]{:S(2)}) collective-permute-start(bf16[1024,256]{1,0:T(8,128)(2,1)S(1)} %get-tuple-element.88), channel_id=1, source_target_pairs={{8,0},{12,4},{0,8},{4,12},{9,1},{13,5},{1,9},{5,13},{10,2},{14,6},... | collective-permute-start | bytes 1572872 | tf_op jit(solution)/shard_map/ppermute | solution.py:568
  143.1 1.6 forward_merge.7
  145.5 19.2 %collective-permute-start.26 = (bf16[1024,256]{1,0:T(8,128)(2,1)}, bf16[1024,256]{1,0:T(8,128)(2,1)}, u32[]{:S(2)}, u32[]{:S(2)}) collective-permute-start(bf16[1024,256]{1,0:T(8,128)(2,1)} %get-tuple-element.94), channel_id=1, source_target_pairs={{8,0},{12,4},{0,8},{4,12},{9,1},{13,5},{1,9},{5,13},{10,2},{14,6},... | collective-permute-start | bytes 1572872 | tf_op jit(solution)/shard_map/ppermute | solution.py:568
  165.6 4.6 %copy-done = bf16[8,4,192,1024]{3,2,1,0:T(8,128)(2,1)S(1)} copy-done((bf16[8,4,192,1024]{3,2,1,0:T(8,128)(2,1)S(1)}, bf16[8,4,192,1024]{3,2,1,0:T(8,128)(2,1)}, u32[]{:S(2)}) %copy-start) | copy-done | bytes 12582936
  170.2 1.0 copy-done.11
  172.0 2.7 %collective-permute-done.26.refs_5_ = bf16[1024,256]{1,0:T(8,128)(2,1)} collective-permute-done((bf16[1024,256]{1,0:T(8,128)(2,1)}, bf16[1024,256]{1,0:T(8,128)(2,1)}, u32[]{:S(2)}, u32[]{:S(2)}) %collective-permute-start.26) | collective-permute-done | bytes 524320 | tf_op jit(solution)/shard_map/ppermute | solution.py:568
  174.7 2.6 %final_merge.7 = (bf16[1024,256]{1,0:T(8,128)(2,1)S(1)}, s32[8,128]{1,0:T(8,128)}) custom-call(s32[2]{0:T(128)S(1)} %pad_add_fusion.refs_0_, s32[8]{0:T(128)S(1)} %add.11.refs_1_, bf16[1024,256]{1,0:T(8,128)(2,1)S(1)} %get-tuple-element.89.refs_2_, bf16[1024,256]{1,0:T(8,128)(2,1)S(1)} %collective-permute-done.24.refs_3_, bf16[1024,256]{1,0:T(8,128)(2,1)S(1)} %copy-done.5, ...), custom_call_target="tpu_custom_call" | custom-call | flops 1 | tf_op jit(solution)/shard_map/final_merge/pallas_call | solution.py:162
  177.3 15.1 %packed_mlp.1 = bf16[1,1024,1024]{2,1,0:T(8,128)(2,1)} custom-call(bf16[1024,256]{1,0:T(8,128)(2,1)S(1)} %copy-done.7, bf16[1024,256]{1,0:T(8,128)(2,1)S(1)} %copy-done.9, bf16[1024,256]{1,0:T(8,128)(2,1)S(1)} %get-tuple-element.93.refs_2_, bf16[1024,256]{1,0:T(8,128)(2,1)S(1)} %get-tuple-element.96.refs_3_, bf16[8,4,192,1024]{3,2,1,0:T(8,128)(2,1)S(1)} %copy-done.1), custom_call_target="tpu_custom_call" | custom-call | tf_op jit(solution)/shard_map/packed_mlp/pallas_call | solution.py:409
  (86 shorter events, 17.0 us)
Async XLA Ops:
  6.5 159.1 %all-gather.2.cloned.1.call-start = ((), (), s32[]{:S(2)}) async-start(), calls=%async_computation | async-start | bytes 14155776 | tf_op jit(solution)/shard_map/all_gather | solution.py:524
  7.2 11.7 %collective-permute-start = (s32[8]{0:T(128)S(1)}, s32[8]{0:T(128)S(1)}, u32[]{:S(2)}, u32[]{:S(2)}) collective-permute-start(s32[8]{0:T(128)S(1)} %compare_select_fusion), channel_id=1, source_target_pairs={{0,16},{4,20},{8,24},{12,28},{16,0},{20,4},{24,8},{28,12},{1,17},{... | collective-permute-start | bytes 104 | tf_op jit(solution)/shard_map/ppermute | solution.py:420
  14.6 7.9 %copy-start.13 = (bf16[2,1024,64]{1,2,0:T(8,128)(2,1)S(1)}, bf16[2,1024,64]{1,2,0:T(8,128)(2,1)}, u32[]{:S(2)}) copy-start(bf16[2,1024,64]{1,2,0:T(8,128)(2,1)} %param.12) | copy-start | bytes 786436
  14.6 10.8 %copy-start.14 = (bf16[32,32,32]{2,1,0:T(8,128)(2,1)S(1)}, bf16[32,32,32]{2,1,0:T(8,128)(2,1)}, u32[]{:S(2)}) copy-start(bf16[32,32,32]{2,1,0:T(8,128)(2,1)} %refs_1_.2) | copy-start | bytes 196612
  14.6 12.7 %copy-start.3 = (bf16[1,1024,1024]{2,1,0:T(8,128)(2,1)S(1)}, bf16[1,1024,1024]{2,1,0:T(8,128)(2,1)}, u32[]{:S(2)}) copy-start(bf16[1,1024,1024]{2,1,0:T(8,128)(2,1)} %refs_8_.3) | copy-start | bytes 6291460
  17.0 10.2 %collective-permute-start.3 = (bf16[8,32,256]{2,1,0:T(8,128)(2,1)S(1)}, bf16[8,32,256]{2,1,0:T(8,128)(2,1)S(1)}, u32[]{:S(2)}, u32[]{:S(2)}) collective-permute-start(bf16[8,32,256]{2,1,0:T(8,128)(2,1)S(1)} %get-tuple-element.55), channel_id=1, source_target_pairs={{0,1},{1,0},{2,3},{3,2},{4,5},{5,4},{6,7},{7,6},{8,9},{9,8},{10,11... | collective-permute-start | bytes 393224 | tf_op jit(solution)/shard_map/ppermute | solution.py:420
  17.1 10.1 %collective-permute-start.4 = (bf16[8,32,256]{2,1,0:T(8,128)(2,1)S(1)}, bf16[8,32,256]{2,1,0:T(8,128)(2,1)S(1)}, u32[]{:S(2)}, u32[]{:S(2)}) collective-permute-start(bf16[8,32,256]{2,1,0:T(8,128)(2,1)S(1)} %get-tuple-element.56), channel_id=1, source_target_pairs={{0,2},{1,3},{2,0},{3,1},{4,6},{5,7},{6,4},{7,5},{8,10},{9,11},{10,... | collective-permute-start | bytes 393224 | tf_op jit(solution)/shard_map/ppermute | solution.py:420
  18.7 8.6 %collective-permute-start.5 = (bf16[8,32,256]{2,1,0:T(8,128)(2,1)S(1)}, bf16[8,32,256]{2,1,0:T(8,128)(2,1)S(1)}, u32[]{:S(2)}, u32[]{:S(2)}) collective-permute-start(bf16[8,32,256]{2,1,0:T(8,128)(2,1)S(1)} %get-tuple-element.57), channel_id=1, source_target_pairs={{0,3},{1,2},{2,1},{3,0},{4,7},{5,6},{6,5},{7,4},{8,11},{9,10},{10,... | collective-permute-start | bytes 393224 | tf_op jit(solution)/shard_map/ppermute | solution.py:420
  19.0 3.5 %collective-permute-start.1 = (s32[8]{0:T(128)S(1)}, s32[8]{0:T(128)S(1)}, u32[]{:S(2)}, u32[]{:S(2)}) collective-permute-start(s32[8]{0:T(128)S(1)} %fusion), channel_id=1, source_target_pairs={{0,8},{4,12},{8,0},{12,4},{16,24},{20,28},{24,16},{28,20},{1,9},{5... | collective-permute-start | bytes 104 | tf_op jit(solution)/shard_map/ppermute | solution.py:420
  23.4 19.9 %collective-permute-start.10 = (bf16[192,1024]{1,0:T(8,128)(2,1)S(1)}, bf16[192,1024]{1,0:T(8,128)(2,1)S(1)}, u32[]{:S(2)}, u32[]{:S(2)}) collective-permute-start(bf16[192,1024]{1,0:T(8,128)(2,1)S(1)} %get-tuple-element.64.refs_1_), channel_id=1, source_target_pairs={{0,16},{4,20},{8,24},{12,28},{16,0},{20,4},{24,8},{28,12},{1,17},{... | collective-permute-start | bytes 1179656 | tf_op jit(solution)/shard_map/ppermute | solution.py:420
  23.7 3.5 %collective-permute-start.2 = (s32[8]{0:T(128)S(1)}, s32[8]{0:T(128)S(1)}, u32[]{:S(2)}, u32[]{:S(2)}) collective-permute-start(s32[8]{0:T(128)S(1)} %fusion.1.refs_3_), channel_id=1, source_target_pairs={{0,4},{4,0},{8,12},{12,8},{16,20},{20,16},{24,28},{28,24},{1,5},{5... | collective-permute-start | bytes 104 | tf_op jit(solution)/shard_map/ppermute | solution.py:420
  27.3 22.5 %copy-start.17 = (s32[1,8]{1,0:T(1,128)S(1)}, s32[1,8]{1,0:T(1,128)}, u32[]{:S(2)}) copy-start(s32[1,8]{1,0:T(1,128)} %refs_2_.5) | copy-start | bytes 100
  28.5 24.7 %collective-permute-start.6 = (bf16[1024,256]{1,0:T(8,128)(2,1)S(1)}, bf16[1024,256]{1,0:T(8,128)(2,1)S(1)}, u32[]{:S(2)}, u32[]{:S(2)}) collective-permute-start(bf16[1024,256]{1,0:T(8,128)(2,1)S(1)} %get-tuple-element.59.refs_2_), channel_id=1, source_target_pairs={{0,4},{4,0},{8,12},{12,8},{16,20},{20,16},{24,28},{28,24},{1,5},{5... | collective-permute-start | bytes 1572872 | tf_op jit(solution)/shard_map/ppermute | solution.py:420
  30.2 14.3 %collective-permute-start.7 = (bf16[8,32,768]{2,1,0:T(8,128)(2,1)S(1)}, bf16[8,32,768]{2,1,0:T(8,128)(2,1)S(1)}, u32[]{:S(2)}, u32[]{:S(2)}) collective-permute-start(bf16[8,32,768]{2,1,0:T(8,128)(2,1)S(1)} %get-tuple-element.61), channel_id=1, source_target_pairs={{0,1},{1,0},{2,3},{3,2},{4,5},{5,4},{6,7},{7,6},{8,9},{9,8},{10,11... | collective-permute-start | bytes 1179656 | tf_op jit(solution)/shard_map/ppermute | solution.py:420
  30.2 14.3 %collective-permute-start.8 = (bf16[8,32,768]{2,1,0:T(8,128)(2,1)S(1)}, bf16[8,32,768]{2,1,0:T(8,128)(2,1)S(1)}, u32[]{:S(2)}, u32[]{:S(2)}) collective-permute-start(bf16[8,32,768]{2,1,0:T(8,128)(2,1)S(1)} %get-tuple-element.62), channel_id=1, source_target_pairs={{0,2},{1,3},{2,0},{3,1},{4,6},{5,7},{6,4},{7,5},{8,10},{9,11},{10,... | collective-permute-start | bytes 1179656 | tf_op jit(solution)/shard_map/ppermute | solution.py:420
  31.7 18.0 %collective-permute-start.9 = (bf16[8,32,768]{2,1,0:T(8,128)(2,1)S(1)}, bf16[8,32,768]{2,1,0:T(8,128)(2,1)S(1)}, u32[]{:S(2)}, u32[]{:S(2)}) collective-permute-start(bf16[8,32,768]{2,1,0:T(8,128)(2,1)S(1)} %get-tuple-element.63), channel_id=1, source_target_pairs={{0,3},{1,2},{2,1},{3,0},{4,7},{5,6},{6,5},{7,4},{8,11},{9,10},{10,... | collective-permute-start | bytes 1179656 | tf_op jit(solution)/shard_map/ppermute | solution.py:420
  44.4 23.5 %collective-permute-start.13 = (bf16[2,192,1024]{2,1,0:T(8,128)(2,1)S(1)}, bf16[2,192,1024]{2,1,0:T(8,128)(2,1)S(1)}, u32[]{:S(2)}, u32[]{:S(2)}) collective-permute-start(bf16[2,192,1024]{2,1,0:T(8,128)(2,1)S(1)} %get-tuple-element.69.refs_1_), channel_id=1, source_target_pairs={{0,8},{4,12},{8,0},{12,4},{16,24},{20,28},{24,16},{28,20},{1,9},{5... | collective-permute-start | bytes 2359304 | tf_op jit(solution)/shard_map/ppermute | solution.py:420
  52.7 14.3 %collective-permute-start.14 = (bf16[1024,256]{1,0:T(8,128)(2,1)S(1)}, bf16[1024,256]{1,0:T(8,128)(2,1)S(1)}, u32[]{:S(2)}, u32[]{:S(2)}) collective-permute-start(bf16[1024,256]{1,0:T(8,128)(2,1)S(1)} %get-tuple-element.70.refs_2_), channel_id=1, source_target_pairs={{0,4},{4,0},{8,12},{12,8},{16,20},{20,16},{24,28},{28,24},{1,5},{5... | collective-permute-start | bytes 1572872 | tf_op jit(solution)/shard_map/ppermute | solution.py:420
  53.9 13.2 %collective-permute-start.12 = (bf16[1024,256]{1,0:T(8,128)(2,1)S(1)}, bf16[1024,256]{1,0:T(8,128)(2,1)S(1)}, u32[]{:S(2)}, u32[]{:S(2)}) collective-permute-start(bf16[1024,256]{1,0:T(8,128)(2,1)S(1)} %get-tuple-element.68.refs_2_), channel_id=1, source_target_pairs={{24,8},{28,12},{8,24},{12,28},{25,9},{29,13},{9,25},{13,29},{26,10... | collective-permute-start | bytes 1572872 | tf_op jit(solution)/shard_map/ppermute | solution.py:563
  69.7 2.5 %collective-permute-start.11 = (bf16[1024,256]{1,0:T(8,128)(2,1)S(1)}, bf16[1024,256]{1,0:T(8,128)(2,1)S(1)}, u32[]{:S(2)}, u32[]{:S(2)}) collective-permute-start(bf16[1024,256]{1,0:T(8,128)(2,1)S(1)} %get-tuple-element.68.refs_2_), channel_id=1, source_target_pairs={{16,8},{20,12},{24,16},{28,20},{8,24},{12,28},{17,9},{21,13},{25,1... | collective-permute-start | bytes 1572872 | tf_op jit(solution)/shard_map/ppermute | solution.py:562
  70.4 28.5 %collective-permute-start.18 = (bf16[1024,256]{1,0:T(8,128)(2,1)S(1)}, bf16[1024,256]{1,0:T(8,128)(2,1)S(1)}, u32[]{:S(2)}, u32[]{:S(2)}) collective-permute-start(bf16[1024,256]{1,0:T(8,128)(2,1)S(1)} %get-tuple-element.76.refs_2_), channel_id=1, source_target_pairs={{0,4},{4,0},{8,12},{12,8},{16,20},{20,16},{24,28},{28,24},{1,5},{5... | collective-permute-start | bytes 1572872 | tf_op jit(solution)/shard_map/ppermute | solution.py:420
  70.9 29.5 %collective-permute-start.16 = (bf16[1024,256]{1,0:T(8,128)(2,1)S(1)}, bf16[1024,256]{1,0:T(8,128)(2,1)S(1)}, u32[]{:S(2)}, u32[]{:S(2)}) collective-permute-start(bf16[1024,256]{1,0:T(8,128)(2,1)S(1)} %get-tuple-element.75.refs_2_), channel_id=1, source_target_pairs={{16,8},{20,12},{24,16},{28,20},{8,24},{12,28},{17,9},{21,13},{25,1... | collective-permute-start | bytes 1572872 | tf_op jit(solution)/shard_map/ppermute | solution.py:562
  71.6 29.5 %collective-permute-start.17 = (bf16[1024,256]{1,0:T(8,128)(2,1)S(1)}, bf16[1024,256]{1,0:T(8,128)(2,1)S(1)}, u32[]{:S(2)}, u32[]{:S(2)}) collective-permute-start(bf16[1024,256]{1,0:T(8,128)(2,1)S(1)} %get-tuple-element.75.refs_2_), channel_id=1, source_target_pairs={{24,8},{28,12},{8,24},{12,28},{25,9},{29,13},{9,25},{13,29},{26,10... | collective-permute-start | bytes 1572872 | tf_op jit(solution)/shard_map/ppermute | solution.py:563
  73.1 48.6 %collective-permute-start.15 = (bf16[1024,256]{1,0:T(8,128)(2,1)S(1)}, bf16[1024,256]{1,0:T(8,128)(2,1)S(1)}, u32[]{:S(2)}, u32[]{:S(2)}) collective-permute-start(bf16[1024,256]{1,0:T(8,128)(2,1)S(1)} %get-tuple-element.74), channel_id=1, source_target_pairs={{8,0},{12,4},{0,8},{4,12},{9,1},{13,5},{1,9},{5,13},{10,2},{14,6},... | collective-permute-start | bytes 1572872 | tf_op jit(solution)/shard_map/ppermute | solution.py:568
  97.3 25.2 %collective-permute-start.22 = (bf16[1024,256]{1,0:T(8,128)(2,1)}, bf16[1024,256]{1,0:T(8,128)(2,1)S(1)}, u32[]{:S(2)}, u32[]{:S(2)}) collective-permute-start(bf16[1024,256]{1,0:T(8,128)(2,1)} %get-tuple-element.83.refs_2_), channel_id=1, source_target_pairs={{0,4},{4,0},{8,12},{12,8},{16,20},{20,16},{24,28},{28,24},{1,5},{5... | collective-permute-start | bytes 1572872 | tf_op jit(solution)/shard_map/ppermute | solution.py:420
  99.7 25.7 %collective-permute-start.20 = (bf16[1024,256]{1,0:T(8,128)(2,1)S(1)}, bf16[1024,256]{1,0:T(8,128)(2,1)S(1)}, u32[]{:S(2)}, u32[]{:S(2)}) collective-permute-start(bf16[1024,256]{1,0:T(8,128)(2,1)S(1)} %get-tuple-element.82.refs_2_), channel_id=1, source_target_pairs={{16,8},{20,12},{24,16},{28,20},{8,24},{12,28},{17,9},{21,13},{25,1... | collective-permute-start | bytes 1572872 | tf_op jit(solution)/shard_map/ppermute | solution.py:562
  100.4 25.0 %collective-permute-start.21 = (bf16[1024,256]{1,0:T(8,128)(2,1)S(1)}, bf16[1024,256]{1,0:T(8,128)(2,1)S(1)}, u32[]{:S(2)}, u32[]{:S(2)}) collective-permute-start(bf16[1024,256]{1,0:T(8,128)(2,1)S(1)} %get-tuple-element.82.refs_2_), channel_id=1, source_target_pairs={{24,8},{28,12},{8,24},{12,28},{25,9},{29,13},{9,25},{13,29},{26,10... | collective-permute-start | bytes 1572872 | tf_op jit(solution)/shard_map/ppermute | solution.py:563
  101.9 40.3 %collective-permute-start.19 = (bf16[1024,256]{1,0:T(8,128)(2,1)S(1)}, bf16[1024,256]{1,0:T(8,128)(2,1)S(1)}, u32[]{:S(2)}, u32[]{:S(2)}) collective-permute-start(bf16[1024,256]{1,0:T(8,128)(2,1)S(1)} %get-tuple-element.81), channel_id=1, source_target_pairs={{8,0},{12,4},{0,8},{4,12},{9,1},{13,5},{1,9},{5,13},{10,2},{14,6},... | collective-permute-start | bytes 1572872 | tf_op jit(solution)/shard_map/ppermute | solution.py:568
  124.0 19.1 %collective-permute-start.24 = (bf16[1024,256]{1,0:T(8,128)(2,1)S(1)}, bf16[1024,256]{1,0:T(8,128)(2,1)S(1)}, u32[]{:S(2)}, u32[]{:S(2)}) collective-permute-start(bf16[1024,256]{1,0:T(8,128)(2,1)S(1)} %get-tuple-element.89.refs_2_), channel_id=1, source_target_pairs={{16,8},{20,12},{24,16},{28,20},{8,24},{12,28},{17,9},{21,13},{25,1... | collective-permute-start | bytes 1572872 | tf_op jit(solution)/shard_map/ppermute | solution.py:562
  124.7 18.4 %collective-permute-start.25 = (bf16[1024,256]{1,0:T(8,128)(2,1)S(1)}, bf16[1024,256]{1,0:T(8,128)(2,1)S(1)}, u32[]{:S(2)}, u32[]{:S(2)}) collective-permute-start(bf16[1024,256]{1,0:T(8,128)(2,1)S(1)} %get-tuple-element.89.refs_2_), channel_id=1, source_target_pairs={{24,8},{28,12},{8,24},{12,28},{25,9},{29,13},{9,25},{13,29},{26,10... | collective-permute-start | bytes 1572872 | tf_op jit(solution)/shard_map/ppermute | solution.py:563
  126.2 38.5 %collective-permute-start.23 = (bf16[1024,256]{1,0:T(8,128)(2,1)S(1)}, bf16[1024,256]{1,0:T(8,128)(2,1)S(1)}, u32[]{:S(2)}, u32[]{:S(2)}) collective-permute-start(bf16[1024,256]{1,0:T(8,128)(2,1)S(1)} %get-tuple-element.88), channel_id=1, source_target_pairs={{8,0},{12,4},{0,8},{4,12},{9,1},{13,5},{1,9},{5,13},{10,2},{14,6},... | collective-permute-start | bytes 1572872 | tf_op jit(solution)/shard_map/ppermute | solution.py:568
  145.5 29.2 %collective-permute-start.26 = (bf16[1024,256]{1,0:T(8,128)(2,1)}, bf16[1024,256]{1,0:T(8,128)(2,1)}, u32[]{:S(2)}, u32[]{:S(2)}) collective-permute-start(bf16[1024,256]{1,0:T(8,128)(2,1)} %get-tuple-element.94), channel_id=1, source_target_pairs={{8,0},{12,4},{0,8},{4,12},{9,1},{13,5},{1,9},{5,13},{10,2},{14,6},... | collective-permute-start | bytes 1572872 | tf_op jit(solution)/shard_map/ppermute | solution.py:568
  (14 other events, 36.2 us)
Sparse Core Ops, SparseCore 0:
  69.8 92.9 all-gather.1

commit v4 on v3

--- a/solution.py
+++ b/solution.py
@@ -371,16 +371,29 @@
 NT = (((1,), (1,)), ((), ()))
 
 
-def mlp_kernel(pieces, *refs):
-    sources, (main_ref, out_ref) = refs[:pieces], refs[pieces:]
-    here, levels, each, feat_width = main_ref.shape
-    thin = feat_width // (here * levels)
-    wide = (each - 2 * thin) // 2
+def mlp_kernel(pieces, ids_ref, *refs):
+    sources, refs = refs[:pieces], refs[pieces:]
+    own_gate, got_gate, own_up, got_up, out_ref = refs
+    core = ids_ref[1] % 2
+
+    @pl.when(core == 0)
+    def _():
+        mlp_rows(sources, (own_gate, got_gate), (own_up, got_up), out_ref)
+
+    @pl.when(core == 1)
+    def _():
+        mlp_rows(sources, (got_gate, own_gate), (got_up, own_up), out_ref)
+
+
+def mlp_rows(sources, gate_refs, up_refs, out_ref):
+    here, levels, each, feat_width = gate_refs[0].shape
+    thin = feat_width // (2 * here * levels)
+    wide = each - thin
     rows = out_ref.shape[1]
     block = rows // BLOCKS
 
-    def weights(level, begin, count):
-        return main_ref[:, level, begin:begin + count, :].reshape(here * count, feat_width)
+    def weights(refs, level, rows):
+        return jnp.concatenate([ref[i, level, rows, :] for i in range(here) for ref in refs], axis=0)
 
     def times(values, matrix):
         return lax.dot_general(values, matrix, NT, preferred_element_type=jnp.float32)
@@ -390,51 +403,52 @@
         normed = rms_round(mixed)
         hidden = []
         for level in range(levels):
-            gate = times(normed, weights(level, 0, wide))
-            up = times(normed, weights(level, wide, wide))
+            gate = times(normed, weights(gate_refs, level, slice(0, wide)))
+            up = times(normed, weights(up_refs, level, slice(0, wide)))
             hidden.append((gate / (1.0 + jnp.exp(-gate)) * up).astype(jnp.bfloat16))
         hidden = jnp.concatenate(hidden, axis=1)
-        halves = hidden.shape[1] // feat_width
         for level in range(levels):
-            cols = slice(level * here * thin, (level + 1) * here * thin)
+            cols = slice(level * 2 * here * thin, (level + 1) * 2 * here * thin)
             result = mixed[:, cols]
-            for part in range(halves):
+            for part, found in enumerate((gate_refs, up_refs)):
                 inner = hidden[:, part * feat_width:(part + 1) * feat_width]
-                result += times(inner, weights(level, 2 * wide + part * thin, thin))
+                result += times(inner, weights(found, level, slice(wide, each)))
             out_ref[0, at:at + block, cols] = result.astype(out_ref.dtype)
 
 
-def packed_mlp(sources, weights):
-    rows, feat_width = sources[0].shape[0], weights.shape[3]
+def packed_mlp(ids, sources, weights):
+    rows, feat_width = sources[0].shape[0], weights[0].shape[3]
     return pl.pallas_call(
         functools.partial(mlp_kernel, len(sources)),
-        in_specs=[VMEM] * (len(sources) + 1),
+        in_specs=[SMEM] + [VMEM] * (len(sources) + 4),
         out_specs=VMEM,
         out_shape=jax.ShapeDtypeStruct((1, rows, feat_width), jnp.bfloat16),
         compiler_params=pltpu.CompilerParams(vmem_limit_bytes=MLP_MIB * MIB),
         name="packed_mlp",
-    )(*sources, weights)
+    )(ids, *sources, *weights)
 
 
 def swap(value, axis, bit):
     return lax.ppermute(value, axis, [(i, i ^ bit) for i in range(lax.axis_size(axis))])
 
 
-def pack_kernel(main_ref, down_ref, out_ref):
+def pack_kernel(main_ref, down_ref, *out_refs):
     wide, feat_width = main_ref.shape[1:]
-    thin = down_ref.shape[0]
-    out_ref[:wide] = main_ref[0]
-    out_ref[wide:2 * wide] = main_ref[1]
-    for part in range(down_ref.shape[1] // feat_width):
-        at = 2 * wide + part * thin
-        out_ref[at:at + thin] = down_ref[:, part * feat_width:(part + 1) * feat_width]
+    for part, out_ref in enumerate(out_refs):
+        out_ref[:wide] = main_ref[part]
+        out_ref[wide:] = down_ref[:, part * feat_width:(part + 1) * feat_width]
 
 
 def pack_weights(main, down, after):
     _, wide, feat_width = main.shape
-    rows = 2 * wide + down.size // feat_width
-    shape = jax.ShapeDtypeStruct((rows, feat_width), main.dtype)
-    return local_call(pack_kernel, "pack_weights", 6, [VMEM, VMEM], [VMEM], [shape], after)(main, down)
+    thin = down.shape[0]
+    shape = jax.ShapeDtypeStruct((2 * (wide + thin), feat_width), main.dtype)
+    return local_call(pack_both, "pack_weights", 6, [VMEM, VMEM], [VMEM], [shape], after)(main, down)
+
+
+def pack_both(main_ref, down_ref, out_ref):
+    rows = out_ref.shape[0] // 2
+    pack_kernel(main_ref, down_ref, out_ref.at[:rows], out_ref.at[rows:])
 
 
 def pair_kernel(which, place, ids_ref, own_ref, got_ref, out_ref, both_ref, sems):
@@ -492,15 +506,19 @@
     ("after_two", 0),
     ("join", 1),
     ("wide", 1),
+    ("join", 2),
+    ("join", 3),
     ("forward", 0),
-    ("join", 2),
     ("forward", 1),
+    ("broad", "gate", 0),
+    ("broad", "up", 0),
     ("finish", 0),
-    ("join", 3),
     ("forward", 2),
     ("finish", 1),
+    ("after_last", 2),
     ("forward", 3),
-    ("after_weights",),
+    ("broad", "gate", 1),
+    ("broad", "up", 1),
     ("finish", 2),
     ("finish", 3),
 )
@@ -550,12 +568,31 @@
         for i, own in enumerate(chained("second", second_factor, *operands)):
             swap_pages(k + i, own)
 
+    def paired(value, got, which, place):
+        return chained("wide", pair_up, ids, value, got, which, place)[0]
+
     def wide(k):
-        value = chained("wide", pair_up, ids, held["weights"], held["across"], (0, 4 - 2 * k), k)[0]
-        if k:
-            held["weights"] = plane(value)
+        value = paired(held["weights"], held["across"], (0, 4 - 2 * k), k)
+        held["weights"] = value
+        if k == 0:
+            held["across"] = swap(value, "page", 2)
         else:
-            held["weights"], held["across"] = value, swap(value, "page", 2)
+            value = value.reshape((-1,) + value.shape[2:])
+            cut = value.shape[1] // 2
+            held["gate"], held["up"] = value[:, :cut], value[:, cut:]
+            held["gate_got"], held["up_got"] = swap(held["gate"], "tok", 2), swap(held["up"], "page", 1)
+
+    def broad(kind, k):
+        bits = ((1, 2), (0, 1))
+        y_first = kind == "gate"
+        which = bits[k] if y_first else bits[1 - k]
+        value = paired(held[kind], held[kind + "_got"], which, 0 if y_first or k == 0 else 1)
+        if k == 0:
+            next_axis = ("page", 1) if y_first else ("tok", 2)
+            held[kind], held[kind + "_got"] = value, swap(value, *next_axis)
+        else:
+            value = value.reshape((-1,) + value.shape[2:])
+            held[kind], held[kind + "_got"] = value, swap(value, "tok", 1)
 
     def join(k):
         value = chained("join", join_parity, *place, held["own", k], held["got", k])[0]
@@ -580,14 +617,16 @@
     def after_two(k):
         tokens.append(held["two", k])
 
-    def after_weights():
-        tokens.append(held["weights"])
-
-    steps = dict(pack=pack, first=first, spread=spread, second=second, wide=wide, join=join, forward=forward, finish=finish)
-    steps.update(lengths=lengths_first, after_one=after_one, after_two=after_two, after_weights=after_weights)
+    def after_last(k):
+        tokens.append(held["last", k])
+
+    steps = dict(pack=pack, first=first, spread=spread, second=second, wide=wide, broad=broad)
+    steps.update(join=join, forward=forward, finish=finish, lengths=lengths_first)
+    steps.update(after_one=after_one, after_two=after_two, after_last=after_last)
     for name, *which in ORDER:
         steps[name](*which)
-    return packed_mlp([held["source", k] for k in range(len(spans))], held["weights"])
+    weights = [held[kind] for kind in ("gate", "gate_got", "up", "up_got")]
+    return packed_mlp(ids, [held["source", k] for k in range(len(spans))], weights)
 
 
 def solution(mesh):

time: 200 us -> 199 us (level)
  waiting for transfers between devices: 34.7 us -> 78.1 us
  starting transfers between devices: 100 us -> 76.1 us
  between operations: 14.5 us -> 1.13 us
  local copies, waits for them, and re-layouts: 11.4 us -> 4.23 us
    ppermute x4, waiting for transfers between devices: 2.7 us -> 30.5 us  [forward(): lax.ppermute(value, 'page', [(2, 0), (3, 1), (0, 2), (1, 3)])]
    ppermute x4, starting transfers between devices: 79.2 us -> 51.5 us  [forward(): lax.ppermute(value, 'page', [(2, 0), (3, 1), (0, 2), (1, 3)])]
    ppermute x15 -> x21, waiting for transfers between devices: 32 us -> 47.5 us  [swap(): lax.ppermute(value, axis, [(i, i ^ bit) for i in range(lax.axis_size(axis...]
    unnamed x36 -> x16, local copies, waits for them, and re-layouts: 11.4 us -> 4.11 us
    ppermute x15 -> x21, starting transfers between devices: 15.6 us -> 19 us  [swap(): lax.ppermute(value, axis, [(i, i ^ bit) for i in range(lax.axis_size(axis...]
    pallas_call x19 -> x23, Pallas kernels: 23.2 us -> 22.3 us  [run(): *results, token = call(*operands, *after)]
  transfers between devices with their start and end apart: 28 -> 33, of which waited for: 6 -> 11; matrix products, arithmetic and copies ran while one was open for 0% -> 0% of each run, Pallas kernels for 9% -> 11%
where the time goes in v4:
time: 199 us; the launch traced here: 198 us
  waiting for transfers between devices  78.1 us (39%)
  starting transfers between devices  76.1 us (38%)
  Pallas kernels  38.5 us (19%)
  local copies, waits for them, and re-layouts  4.23 us (2%)
    ppermute x4, starting transfers between devices, forward(): lax.ppermute(value, 'page', [(2, 0), (3, 1), (0, 2), (1, 3)])  51.5 us
    ppermute x21, waiting for transfers between devices, swap(): lax.ppermute(value, axis, [(i, i ^ bit) for i in range(lax.axis_size(axis...  47.5 us
    ppermute x4, waiting for transfers between devices, forward(): lax.ppermute(value, 'page', [(2, 0), (3, 1), (0, 2), (1, 3)])  30.5 us
    pallas_call x23, Pallas kernels, run(): *results, token = call(*operands, *after)  22.3 us
    ppermute x21, starting transfers between devices, swap(): lax.ppermute(value, axis, [(i, i ^ bit) for i in range(lax.axis_size(axis...  19 us
    pallas_call x1, Pallas kernels, packed_mlp(): pl.pallas_call(functools.partial(mlp_kernel, len(sources)), in_specs=[SME...  16.2 us
    unnamed x16, local copies, waits for them, and re-layouts  4.11 us
  transfers between devices with their start and end apart: 33, of which 11 were waited for; matrix products, arithmetic and copies ran while one was open for 0% of the time, Pallas kernels for 11%

profile of v4, /device:TPU:0, one launch (start us, length us, event | category | flops | bytes accessed | tf_op | source)
XLA Modules:
  0.0 198.1 jit_solution(1888818843066956436)
XLA Ops:
  0.7 4.1 %collective-permute-start = (s32[8]{0:T(128)S(1)}, s32[8]{0:T(128)S(1)}, u32[]{:S(2)}, u32[]{:S(2)}) collective-permute-start(s32[8]{0:T(128)S(1)} %compare_select_fusion), channel_id=1, source_target_pairs={{0,16},{4,20},{8,24},{12,28},{16,0},{20,4},{24,8},{28,12},{1,17},{... | collective-permute-start | bytes 104 | tf_op jit(solution)/shard_map/ppermute | solution.py:432
  4.9 1.6 copy-done
  8.1 2.4 %first_factor.1 = (bf16[8,32,256]{2,1,0:T(8,128)(2,1)S(1)}, bf16[8,32,256]{2,1,0:T(8,128)(2,1)S(1)}, bf16[8,32,256]{2,1,0:T(8,128)(2,1)S(1)}, bf16[8,32,256]{2,1...) custom-call(s32[2]{0:T(128)S(1)} %pad_add_fusion.refs_0_.ids_ref, ...), custom_call_target="tpu_custom_call" | custom-call | flops 1 | tf_op jit(solution)/shard_map/first_factor/pallas_call | solution.py:162
  10.6 1.6 collective-permute-start.4
  12.4 1.6 collective-permute-start.1
  14.0 2.0 collective-permute-done.1
  17.2 1.7 collective-permute-start.2
  18.8 1.0 spread_stride.1
  20.7 1.2 second_factor.2
  21.9 1.7 collective-permute-start.6
  23.7 1.5 collective-permute-start.8
  25.5 11.3 %collective-permute-done.10.refs_2_ = bf16[192,1024]{1,0:T(8,128)(2,1)S(1)} collective-permute-done((bf16[192,1024]{1,0:T(8,128)(2,1)S(1)}, bf16[192,1024]{1,0:T(8,128)(2,1)S(1)}, u32[]{:S(2)}, u32[]{:S(2)}) %collective-permute-start.10) | collective-permute-done | bytes 393248 | tf_op jit(solution)/shard_map/ppermute | solution.py:432
  36.8 1.0 pair_up.6
  37.9 5.3 %collective-permute-done.9.refs_7_ = bf16[8,32,768]{2,1,0:T(8,128)(2,1)S(1)} collective-permute-done((bf16[8,32,768]{2,1,0:T(8,128)(2,1)S(1)}, bf16[8,32,768]{2,1,0:T(8,128)(2,1)S(1)}, u32[]{:S(2)}, u32[]{:S(2)}) %collective-permute-start.9) | collective-permute-done | bytes 393248 | tf_op jit(solution)/shard_map/ppermute | solution.py:432
  43.2 2.2 %second_factor.3 = (bf16[1024,256]{1,0:T(8,128)(2,1)S(1)}, bf16[1024,256]{1,0:T(8,128)(2,1)S(1)}, bf16[1024,256]{1,0:T(8,128)(2,1)S(1)}, s32[8,128]{1,0:T(8,128)S(1)}) custom-call(s32[2]{0:T(128)S(1)} %pad_add_fusion.refs_0_.ids_ref, s32[8]{0:T(128)S(1)} %add.11.refs_1_, s32[1,8]{1,0:T(1,128)S(1)} %copy-done.7, ...), custom_call_target="tpu_custom_call" | custom-call | flops 1 | tf_op jit(solution)/shard_map/second_factor/pallas_call | solution.py:162
  47.3 1.7 collective-permute-start.13
  49.4 10.8 %collective-permute-done.16.refs_3_ = bf16[1024,256]{1,0:T(8,128)(2,1)S(1)} collective-permute-done((bf16[1024,256]{1,0:T(8,128)(2,1)S(1)}, bf16[1024,256]{1,0:T(8,128)(2,1)S(1)}, u32[]{:S(2)}, u32[]{:S(2)}) %collective-permute-start.16) | collective-permute-done | bytes 524320 | tf_op jit(solution)/shard_map/ppermute | solution.py:432
  61.9 1.6 collective-permute-start.19
  64.8 6.7 %collective-permute-done.13.refs_3_ = bf16[1024,256]{1,0:T(8,128)(2,1)S(1)} collective-permute-done((bf16[1024,256]{1,0:T(8,128)(2,1)S(1)}, bf16[1024,256]{1,0:T(8,128)(2,1)S(1)}, u32[]{:S(2)}, u32[]{:S(2)}) %collective-permute-start.13) | collective-permute-done | bytes 524320 | tf_op jit(solution)/shard_map/ppermute | solution.py:432
  72.2 10.5 %collective-permute-done.14.refs_3_ = bf16[1024,256]{1,0:T(8,128)(2,1)S(1)} collective-permute-done((bf16[1024,256]{1,0:T(8,128)(2,1)S(1)}, bf16[1024,256]{1,0:T(8,128)(2,1)S(1)}, u32[]{:S(2)}, u32[]{:S(2)}) %collective-permute-start.14) | collective-permute-done | bytes 524320 | tf_op jit(solution)/shard_map/ppermute | solution.py:432
  85.8 17.9 %collective-permute-start.17 = (bf16[1024,256]{1,0:T(8,128)(2,1)S(1)}, bf16[1024,256]{1,0:T(8,128)(2,1)S(1)}, u32[]{:S(2)}, u32[]{:S(2)}) collective-permute-start(bf16[1024,256]{1,0:T(8,128)(2,1)S(1)} %get-tuple-element.86), channel_id=1, source_target_pairs={{8,0},{12,4},{0,8},{4,12},{9,1},{13,5},{1,9},{5,13},{10,2},{14,6},... | collective-permute-start | bytes 1572872 | tf_op jit(solution)/shard_map/ppermute | solution.py:605
  108.2 2.6 %collective-permute-done.17.refs_5_ = bf16[1024,256]{1,0:T(8,128)(2,1)S(1)} collective-permute-done((bf16[1024,256]{1,0:T(8,128)(2,1)S(1)}, bf16[1024,256]{1,0:T(8,128)(2,1)S(1)}, u32[]{:S(2)}, u32[]{:S(2)}) %collective-permute-start.17) | collective-permute-done | bytes 524320 | tf_op jit(solution)/shard_map/ppermute | solution.py:605
  110.8 12.0 %collective-permute-start.22 = (bf16[1024,256]{1,0:T(8,128)(2,1)S(1)}, bf16[1024,256]{1,0:T(8,128)(2,1)S(1)}, u32[]{:S(2)}, u32[]{:S(2)}) collective-permute-start(bf16[1024,256]{1,0:T(8,128)(2,1)S(1)} %get-tuple-element.94), channel_id=1, source_target_pairs={{8,0},{12,4},{0,8},{4,12},{9,1},{13,5},{1,9},{5,13},{10,2},{14,6},... | collective-permute-start | bytes 1572872 | tf_op jit(solution)/shard_map/ppermute | solution.py:605
  125.9 7.0 %collective-permute-done.22.refs_5_ = bf16[1024,256]{1,0:T(8,128)(2,1)S(1)} collective-permute-done((bf16[1024,256]{1,0:T(8,128)(2,1)S(1)}, bf16[1024,256]{1,0:T(8,128)(2,1)S(1)}, u32[]{:S(2)}, u32[]{:S(2)}) %collective-permute-start.22) | collective-permute-done | bytes 524320 | tf_op jit(solution)/shard_map/ppermute | solution.py:605
  132.9 16.4 %collective-permute-start.25 = (bf16[1024,256]{1,0:T(8,128)(2,1)S(1)}, bf16[1024,256]{1,0:T(8,128)(2,1)S(1)}, u32[]{:S(2)}, u32[]{:S(2)}) collective-permute-start(bf16[1024,256]{1,0:T(8,128)(2,1)S(1)} %get-tuple-element.99), channel_id=1, source_target_pairs={{8,0},{12,4},{0,8},{4,12},{9,1},{13,5},{1,9},{5,13},{10,2},{14,6},... | collective-permute-start | bytes 1572872 | tf_op jit(solution)/shard_map/ppermute | solution.py:605
  150.0 9.6 %collective-permute-done.25.refs_6_.refs_5_ = bf16[1024,256]{1,0:T(8,128)(2,1)S(1)} collective-permute-done((bf16[1024,256]{1,0:T(8,128)(2,1)S(1)}, bf16[1024,256]{1,0:T(8,128)(2,1)S(1)}, u32[]{:S(2)}, u32[]{:S(2)}) %collective-permute-start.25) | collective-permute-done | bytes 524320 | tf_op jit(solution)/shard_map/ppermute | solution.py:605
  160.5 1.0 pair_up.10
  161.5 1.0 pair_up.11
  163.1 5.3 %collective-permute-start.30 = (bf16[1024,256]{1,0:T(8,128)(2,1)S(1)}, bf16[1024,256]{1,0:T(8,128)(2,1)S(1)}, u32[]{:S(2)}, u32[]{:S(2)}) collective-permute-start(bf16[1024,256]{1,0:T(8,128)(2,1)S(1)} %get-tuple-element.108), channel_id=1, source_target_pairs={{8,0},{12,4},{0,8},{4,12},{9,1},{13,5},{1,9},{5,13},{10,2},{14,6},... | collective-permute-start | bytes 1572872 | tf_op jit(solution)/shard_map/ppermute | solution.py:605
  169.2 11.4 %collective-permute-done.30.refs_5_ = bf16[1024,256]{1,0:T(8,128)(2,1)S(1)} collective-permute-done((bf16[1024,256]{1,0:T(8,128)(2,1)S(1)}, bf16[1024,256]{1,0:T(8,128)(2,1)S(1)}, u32[]{:S(2)}, u32[]{:S(2)}) %collective-permute-start.30) | collective-permute-done | bytes 524320 | tf_op jit(solution)/shard_map/ppermute | solution.py:605
  180.5 1.4 final_merge.7
  181.9 16.2 %packed_mlp.1 = bf16[1,1024,1024]{2,1,0:T(8,128)(2,1)} custom-call(s32[2]{0:T(128)S(1)} %pad_add_fusion.refs_0_.ids_ref, bf16[1024,256]{1,0:T(8,128)(2,1)S(1)} %get-tuple-element.93.refs_0_, bf16[1024,256]{1,0:T(8,128)(2,1)S(1)} %get-tuple-element.98.refs_1_, bf16[1024,256]{1,0:T(8,128)(2,1)S(1)} %get-tuple-element.107.refs_2_, ...), custom_call_target="tpu_custom_call" | custom-call | tf_op jit(solution)/shard_map/packed_mlp/pallas_call | solution.py:421
  (80 shorter events, 23.9 us)
Async XLA Ops:
  0.7 11.7 %collective-permute-start = (s32[8]{0:T(128)S(1)}, s32[8]{0:T(128)S(1)}, u32[]{:S(2)}, u32[]{:S(2)}) collective-permute-start(s32[8]{0:T(128)S(1)} %compare_select_fusion), channel_id=1, source_target_pairs={{0,16},{4,20},{8,24},{12,28},{16,0},{20,4},{24,8},{28,12},{1,17},{... | collective-permute-start | bytes 104 | tf_op jit(solution)/shard_map/ppermute | solution.py:432
  10.5 10.2 %collective-permute-start.3 = (bf16[8,32,256]{2,1,0:T(8,128)(2,1)S(1)}, bf16[8,32,256]{2,1,0:T(8,128)(2,1)S(1)}, u32[]{:S(2)}, u32[]{:S(2)}) collective-permute-start(bf16[8,32,256]{2,1,0:T(8,128)(2,1)S(1)} %get-tuple-element.63), channel_id=1, source_target_pairs={{0,1},{1,0},{2,3},{3,2},{4,5},{5,4},{6,7},{7,6},{8,9},{9,8},{10,11... | collective-permute-start | bytes 393224 | tf_op jit(solution)/shard_map/ppermute | solution.py:432
  10.6 10.1 %collective-permute-start.4 = (bf16[8,32,256]{2,1,0:T(8,128)(2,1)S(1)}, bf16[8,32,256]{2,1,0:T(8,128)(2,1)S(1)}, u32[]{:S(2)}, u32[]{:S(2)}) collective-permute-start(bf16[8,32,256]{2,1,0:T(8,128)(2,1)S(1)} %get-tuple-element.64), channel_id=1, source_target_pairs={{0,2},{1,3},{2,0},{3,1},{4,6},{5,7},{6,4},{7,5},{8,10},{9,11},{10,... | collective-permute-start | bytes 393224 | tf_op jit(solution)/shard_map/ppermute | solution.py:432
  12.2 8.6 %collective-permute-start.5 = (bf16[8,32,256]{2,1,0:T(8,128)(2,1)S(1)}, bf16[8,32,256]{2,1,0:T(8,128)(2,1)S(1)}, u32[]{:S(2)}, u32[]{:S(2)}) collective-permute-start(bf16[8,32,256]{2,1,0:T(8,128)(2,1)S(1)} %get-tuple-element.65), channel_id=1, source_target_pairs={{0,3},{1,2},{2,1},{3,0},{4,7},{5,6},{6,5},{7,4},{8,11},{9,10},{10,... | collective-permute-start | bytes 393224 | tf_op jit(solution)/shard_map/ppermute | solution.py:432
  12.4 3.5 %collective-permute-start.1 = (s32[8]{0:T(128)S(1)}, s32[8]{0:T(128)S(1)}, u32[]{:S(2)}, u32[]{:S(2)}) collective-permute-start(s32[8]{0:T(128)S(1)} %fusion.1), channel_id=1, source_target_pairs={{0,8},{4,12},{8,0},{12,4},{16,24},{20,28},{24,16},{28,20},{1,9},{5... | collective-permute-start | bytes 104 | tf_op jit(solution)/shard_map/ppermute | solution.py:432
  16.9 19.9 %collective-permute-start.10 = (bf16[192,1024]{1,0:T(8,128)(2,1)S(1)}, bf16[192,1024]{1,0:T(8,128)(2,1)S(1)}, u32[]{:S(2)}, u32[]{:S(2)}) collective-permute-start(bf16[192,1024]{1,0:T(8,128)(2,1)S(1)} %get-tuple-element.72.refs_1_), channel_id=1, source_target_pairs={{0,16},{4,20},{8,24},{12,28},{16,0},{20,4},{24,8},{28,12},{1,17},{... | collective-permute-start | bytes 1179656 | tf_op jit(solution)/shard_map/ppermute | solution.py:432
  21.9 23.9 %collective-permute-start.6 = (bf16[1024,256]{1,0:T(8,128)(2,1)S(1)}, bf16[1024,256]{1,0:T(8,128)(2,1)S(1)}, u32[]{:S(2)}, u32[]{:S(2)}) collective-permute-start(bf16[1024,256]{1,0:T(8,128)(2,1)S(1)} %get-tuple-element.67.refs_2_), channel_id=1, source_target_pairs={{0,4},{4,0},{8,12},{12,8},{16,20},{20,16},{24,28},{28,24},{1,5},{5... | collective-permute-start | bytes 1572872 | tf_op jit(solution)/shard_map/ppermute | solution.py:432
  23.7 14.3 %collective-permute-start.7 = (bf16[8,32,768]{2,1,0:T(8,128)(2,1)S(1)}, bf16[8,32,768]{2,1,0:T(8,128)(2,1)S(1)}, u32[]{:S(2)}, u32[]{:S(2)}) collective-permute-start(bf16[8,32,768]{2,1,0:T(8,128)(2,1)S(1)} %get-tuple-element.69), channel_id=1, source_target_pairs={{0,1},{1,0},{2,3},{3,2},{4,5},{5,4},{6,7},{7,6},{8,9},{9,8},{10,11... | collective-permute-start | bytes 1179656 | tf_op jit(solution)/shard_map/ppermute | solution.py:432
  23.7 14.3 %collective-permute-start.8 = (bf16[8,32,768]{2,1,0:T(8,128)(2,1)S(1)}, bf16[8,32,768]{2,1,0:T(8,128)(2,1)S(1)}, u32[]{:S(2)}, u32[]{:S(2)}) collective-permute-start(bf16[8,32,768]{2,1,0:T(8,128)(2,1)S(1)} %get-tuple-element.70), channel_id=1, source_target_pairs={{0,2},{1,3},{2,0},{3,1},{4,6},{5,7},{6,4},{7,5},{8,10},{9,11},{10,... | collective-permute-start | bytes 1179656 | tf_op jit(solution)/shard_map/ppermute | solution.py:432
  25.2 18.0 %collective-permute-start.9 = (bf16[8,32,768]{2,1,0:T(8,128)(2,1)S(1)}, bf16[8,32,768]{2,1,0:T(8,128)(2,1)S(1)}, u32[]{:S(2)}, u32[]{:S(2)}) collective-permute-start(bf16[8,32,768]{2,1,0:T(8,128)(2,1)S(1)} %get-tuple-element.71), channel_id=1, source_target_pairs={{0,3},{1,2},{2,1},{3,0},{4,7},{5,6},{6,5},{7,4},{8,11},{9,10},{10,... | collective-permute-start | bytes 1179656 | tf_op jit(solution)/shard_map/ppermute | solution.py:432
  37.8 23.2 %collective-permute-start.15 = (bf16[2,192,1024]{2,1,0:T(8,128)(2,1)S(1)}, bf16[2,192,1024]{2,1,0:T(8,128)(2,1)S(1)}, u32[]{:S(2)}, u32[]{:S(2)}) collective-permute-start(bf16[2,192,1024]{2,1,0:T(8,128)(2,1)S(1)} %get-tuple-element.79.refs_1_), channel_id=1, source_target_pairs={{0,8},{4,12},{8,0},{12,4},{16,24},{20,28},{24,16},{28,20},{1,9},{5... | collective-permute-start | bytes 2359304 | tf_op jit(solution)/shard_map/ppermute | solution.py:432
  45.4 14.8 %collective-permute-start.16 = (bf16[1024,256]{1,0:T(8,128)(2,1)S(1)}, bf16[1024,256]{1,0:T(8,128)(2,1)S(1)}, u32[]{:S(2)}, u32[]{:S(2)}) collective-permute-start(bf16[1024,256]{1,0:T(8,128)(2,1)S(1)} %get-tuple-element.80.refs_2_), channel_id=1, source_target_pairs={{0,4},{4,0},{8,12},{12,8},{16,20},{20,16},{24,28},{28,24},{1,5},{5... | collective-permute-start | bytes 1572872 | tf_op jit(solution)/shard_map/ppermute | solution.py:432
  46.6 13.6 %collective-permute-start.12 = (bf16[1024,256]{1,0:T(8,128)(2,1)S(1)}, bf16[1024,256]{1,0:T(8,128)(2,1)S(1)}, u32[]{:S(2)}, u32[]{:S(2)}) collective-permute-start(bf16[1024,256]{1,0:T(8,128)(2,1)S(1)} %get-tuple-element.76.refs_2_), channel_id=1, source_target_pairs={{24,8},{28,12},{8,24},{12,28},{25,9},{29,13},{9,25},{13,29},{26,10... | collective-permute-start | bytes 1572872 | tf_op jit(solution)/shard_map/ppermute | solution.py:600
  47.3 24.1 %collective-permute-start.13 = (bf16[1024,256]{1,0:T(8,128)(2,1)S(1)}, bf16[1024,256]{1,0:T(8,128)(2,1)S(1)}, u32[]{:S(2)}, u32[]{:S(2)}) collective-permute-start(bf16[1024,256]{1,0:T(8,128)(2,1)S(1)} %get-tuple-element.77.refs_2_), channel_id=1, source_target_pairs={{0,4},{4,0},{8,12},{12,8},{16,20},{20,16},{24,28},{28,24},{1,5},{5... | collective-permute-start | bytes 1572872 | tf_op jit(solution)/shard_map/ppermute | solution.py:432
  49.1 33.6 %collective-permute-start.14 = (bf16[1024,256]{1,0:T(8,128)(2,1)S(1)}, bf16[1024,256]{1,0:T(8,128)(2,1)S(1)}, u32[]{:S(2)}, u32[]{:S(2)}) collective-permute-start(bf16[1024,256]{1,0:T(8,128)(2,1)S(1)} %get-tuple-element.78.refs_2_), channel_id=1, source_target_pairs={{0,4},{4,0},{8,12},{12,8},{16,20},{20,16},{24,28},{28,24},{1,5},{5... | collective-permute-start | bytes 1572872 | tf_op jit(solution)/shard_map/ppermute | solution.py:432
  61.9 42.5 %collective-permute-start.19 = (bf16[4,96,1024]{2,1,0:T(8,128)(2,1)S(1)}, bf16[4,96,1024]{2,1,0:T(8,128)(2,1)S(1)}, u32[]{:S(2)}, u32[]{:S(2)}) collective-permute-start(bf16[4,96,1024]{2,1,0:T(8,128)(2,1)S(1)} %get-tuple-element.113.refs_1_), channel_id=1, source_target_pairs={{0,2},{1,3},{2,0},{3,1},{4,6},{5,7},{6,4},{7,5},{8,10},{9,11},{10,... | collective-permute-start | bytes 2359304 | tf_op jit(solution)/shard_map/ppermute | solution.py:432
  63.5 42.4 %collective-permute-start.18 = (bf16[4,96,1024]{2,1,0:T(8,128)(2,1)S(1)}, bf16[4,96,1024]{2,1,0:T(8,128)(2,1)S(1)}, u32[]{:S(2)}, u32[]{:S(2)}) collective-permute-start(bf16[4,96,1024]{2,1,0:T(8,128)(2,1)S(1)} %get-tuple-element.114.refs_1_), channel_id=1, source_target_pairs={{0,4},{4,0},{8,12},{12,8},{16,20},{20,16},{24,28},{28,24},{1,5},{5... | collective-permute-start | bytes 2359304 | tf_op jit(solution)/shard_map/ppermute | solution.py:432
  64.1 20.9 %collective-permute-start.11 = (bf16[1024,256]{1,0:T(8,128)(2,1)S(1)}, bf16[1024,256]{1,0:T(8,128)(2,1)S(1)}, u32[]{:S(2)}, u32[]{:S(2)}) collective-permute-start(bf16[1024,256]{1,0:T(8,128)(2,1)S(1)} %get-tuple-element.76.refs_2_), channel_id=1, source_target_pairs={{16,8},{20,12},{24,16},{28,20},{8,24},{12,28},{17,9},{21,13},{25,1... | collective-permute-start | bytes 1572872 | tf_op jit(solution)/shard_map/ppermute | solution.py:599
  71.5 32.2 %collective-permute-start.21 = (bf16[1024,256]{1,0:T(8,128)(2,1)S(1)}, bf16[1024,256]{1,0:T(8,128)(2,1)S(1)}, u32[]{:S(2)}, u32[]{:S(2)}) collective-permute-start(bf16[1024,256]{1,0:T(8,128)(2,1)S(1)} %get-tuple-element.88.refs_2_), channel_id=1, source_target_pairs={{24,8},{28,12},{8,24},{12,28},{25,9},{29,13},{9,25},{13,29},{26,10... | collective-permute-start | bytes 1572872 | tf_op jit(solution)/shard_map/ppermute | solution.py:600
  82.7 20.9 %collective-permute-start.20 = (bf16[1024,256]{1,0:T(8,128)(2,1)S(1)}, bf16[1024,256]{1,0:T(8,128)(2,1)S(1)}, u32[]{:S(2)}, u32[]{:S(2)}) collective-permute-start(bf16[1024,256]{1,0:T(8,128)(2,1)S(1)} %get-tuple-element.88.refs_2_), channel_id=1, source_target_pairs={{16,8},{20,12},{24,16},{28,20},{8,24},{12,28},{17,9},{21,13},{25,1... | collective-permute-start | bytes 1572872 | tf_op jit(solution)/shard_map/ppermute | solution.py:599
  85.8 25.0 %collective-permute-start.17 = (bf16[1024,256]{1,0:T(8,128)(2,1)S(1)}, bf16[1024,256]{1,0:T(8,128)(2,1)S(1)}, u32[]{:S(2)}, u32[]{:S(2)}) collective-permute-start(bf16[1024,256]{1,0:T(8,128)(2,1)S(1)} %get-tuple-element.86), channel_id=1, source_target_pairs={{8,0},{12,4},{0,8},{4,12},{9,1},{13,5},{1,9},{5,13},{10,2},{14,6},... | collective-permute-start | bytes 1572872 | tf_op jit(solution)/shard_map/ppermute | solution.py:605
  105.3 55.2 %collective-permute-start.27 = (bf16[2,4,96,1024]{3,2,1,0:T(8,128)(2,1)S(1)}, bf16[2,4,96,1024]{3,2,1,0:T(8,128)(2,1)S(1)}, u32[]{:S(2)}, u32[]{:S(2)}) collective-permute-start(bf16[2,4,96,1024]{3,2,1,0:T(8,128)(2,1)S(1)} %get-tuple-element.101.refs_1_), channel_id=1, source_target_pairs={{0,4},{4,0},{8,12},{12,8},{16,20},{20,16},{24,28},{28,24},{1,5},{5... | collective-permute-start | bytes 4718600 | tf_op jit(solution)/shard_map/ppermute | solution.py:432
  106.7 54.8 %collective-permute-start.26 = (bf16[2,4,96,1024]{3,2,1,0:T(8,128)(2,1)S(1)}, bf16[2,4,96,1024]{3,2,1,0:T(8,128)(2,1)S(1)}, u32[]{:S(2)}, u32[]{:S(2)}) collective-permute-start(bf16[2,4,96,1024]{3,2,1,0:T(8,128)(2,1)S(1)} %get-tuple-element.100.refs_1_), channel_id=1, source_target_pairs={{0,2},{1,3},{2,0},{3,1},{4,6},{5,7},{6,4},{7,5},{8,10},{9,11},{10,... | collective-permute-start | bytes 4718600 | tf_op jit(solution)/shard_map/ppermute | solution.py:432
  106.8 16.8 %collective-permute-start.24 = (bf16[1024,256]{1,0:T(8,128)(2,1)S(1)}, bf16[1024,256]{1,0:T(8,128)(2,1)S(1)}, u32[]{:S(2)}, u32[]{:S(2)}) collective-permute-start(bf16[1024,256]{1,0:T(8,128)(2,1)S(1)} %get-tuple-element.95.refs_2_), channel_id=1, source_target_pairs={{24,8},{28,12},{8,24},{12,28},{25,9},{29,13},{9,25},{13,29},{26,10... | collective-permute-start | bytes 1572872 | tf_op jit(solution)/shard_map/ppermute | solution.py:600
  107.5 16.8 %collective-permute-start.23 = (bf16[1024,256]{1,0:T(8,128)(2,1)S(1)}, bf16[1024,256]{1,0:T(8,128)(2,1)S(1)}, u32[]{:S(2)}, u32[]{:S(2)}) collective-permute-start(bf16[1024,256]{1,0:T(8,128)(2,1)S(1)} %get-tuple-element.95.refs_2_), channel_id=1, source_target_pairs={{16,8},{20,12},{24,16},{28,20},{8,24},{12,28},{17,9},{21,13},{25,1... | collective-permute-start | bytes 1572872 | tf_op jit(solution)/shard_map/ppermute | solution.py:599
  110.8 22.1 %collective-permute-start.22 = (bf16[1024,256]{1,0:T(8,128)(2,1)S(1)}, bf16[1024,256]{1,0:T(8,128)(2,1)S(1)}, u32[]{:S(2)}, u32[]{:S(2)}) collective-permute-start(bf16[1024,256]{1,0:T(8,128)(2,1)S(1)} %get-tuple-element.94), channel_id=1, source_target_pairs={{8,0},{12,4},{0,8},{4,12},{9,1},{13,5},{1,9},{5,13},{10,2},{14,6},... | collective-permute-start | bytes 1572872 | tf_op jit(solution)/shard_map/ppermute | solution.py:605
  123.6 26.4 %collective-permute-start.29 = (bf16[1024,256]{1,0:T(8,128)(2,1)S(1)}, bf16[1024,256]{1,0:T(8,128)(2,1)S(1)}, u32[]{:S(2)}, u32[]{:S(2)}) collective-permute-start(bf16[1024,256]{1,0:T(8,128)(2,1)S(1)} %get-tuple-element.102.refs_2_), channel_id=1, source_target_pairs={{24,8},{28,12},{8,24},{12,28},{25,9},{29,13},{9,25},{13,29},{26,10... | collective-permute-start | bytes 1572872 | tf_op jit(solution)/shard_map/ppermute | solution.py:600
  124.3 25.7 %collective-permute-start.28 = (bf16[1024,256]{1,0:T(8,128)(2,1)S(1)}, bf16[1024,256]{1,0:T(8,128)(2,1)S(1)}, u32[]{:S(2)}, u32[]{:S(2)}) collective-permute-start(bf16[1024,256]{1,0:T(8,128)(2,1)S(1)} %get-tuple-element.102.refs_2_), channel_id=1, source_target_pairs={{16,8},{20,12},{24,16},{28,20},{8,24},{12,28},{17,9},{21,13},{25,1... | collective-permute-start | bytes 1572872 | tf_op jit(solution)/shard_map/ppermute | solution.py:599
  132.9 26.8 %collective-permute-start.25 = (bf16[1024,256]{1,0:T(8,128)(2,1)S(1)}, bf16[1024,256]{1,0:T(8,128)(2,1)S(1)}, u32[]{:S(2)}, u32[]{:S(2)}) collective-permute-start(bf16[1024,256]{1,0:T(8,128)(2,1)S(1)} %get-tuple-element.99), channel_id=1, source_target_pairs={{8,0},{12,4},{0,8},{4,12},{9,1},{13,5},{1,9},{5,13},{10,2},{14,6},... | collective-permute-start | bytes 1572872 | tf_op jit(solution)/shard_map/ppermute | solution.py:605
  162.5 19.4 %collective-permute-start.32 = (bf16[4,4,96,1024]{3,2,1,0:T(8,128)(2,1)S(1)}, bf16[4,4,96,1024]{3,2,1,0:T(8,128)(2,1)S(1)}, u32[]{:S(2)}, u32[]{:S(2)}) collective-permute-start(bf16[4,4,96,1024]{3,2,1,0:T(8,128)(2,1)S(1)} %bitcast.13), channel_id=1, source_target_pairs={{0,1},{1,0},{2,3},{3,2},{4,5},{5,4},{6,7},{7,6},{8,9},{9,8},{10,11... | collective-permute-start | bytes 9437192 | tf_op jit(solution)/shard_map/ppermute | solution.py:432
  162.6 19.3 %collective-permute-start.31 = (bf16[4,4,96,1024]{3,2,1,0:T(8,128)(2,1)S(1)}, bf16[4,4,96,1024]{3,2,1,0:T(8,128)(2,1)S(1)}, u32[]{:S(2)}, u32[]{:S(2)}) collective-permute-start(bf16[4,4,96,1024]{3,2,1,0:T(8,128)(2,1)S(1)} %bitcast.11), channel_id=1, source_target_pairs={{0,1},{1,0},{2,3},{3,2},{4,5},{5,4},{6,7},{7,6},{8,9},{9,8},{10,11... | collective-permute-start | bytes 9437192 | tf_op jit(solution)/shard_map/ppermute | solution.py:432
  163.1 17.4 %collective-permute-start.30 = (bf16[1024,256]{1,0:T(8,128)(2,1)S(1)}, bf16[1024,256]{1,0:T(8,128)(2,1)S(1)}, u32[]{:S(2)}, u32[]{:S(2)}) collective-permute-start(bf16[1024,256]{1,0:T(8,128)(2,1)S(1)} %get-tuple-element.108), channel_id=1, source_target_pairs={{8,0},{12,4},{0,8},{4,12},{9,1},{13,5},{1,9},{5,13},{10,2},{14,6},... | collective-permute-start | bytes 1572872 | tf_op jit(solution)/shard_map/ppermute | solution.py:605
  (9 other events, 59.7 us)

commit v5 on v4

--- a/solution.py
+++ b/solution.py
@@ -596,7 +596,7 @@
 
     def join(k):
         value = chained("join", join_parity, *place, held["own", k], held["got", k])[0]
-        held["one", k] = lax.ppermute(value, "page", [(4, 2), (5, 3), (6, 4), (7, 5), (2, 6), (3, 7)])
+        held["one", k] = lax.ppermute(value, "page", [(4, 2), (5, 3), (6, 4), (7, 5)])
         held["two", k] = lax.ppermute(value, "page", [(6, 2), (7, 3), (2, 6), (3, 7)])
         held["own", k] = value
 

time: 199 us -> 198 us (level)
  starting transfers between devices: 76.1 us -> 74 us
    ppermute x4, starting transfers between devices: 51.5 us -> 49.4 us  [forward(): lax.ppermute(value, 'page', [(2, 0), (3, 1), (0, 2), (1, 3)])]
where the time goes in v5:
time: 198 us
  waiting for transfers between devices  79.7 us (40%)
  starting transfers between devices  74 us (37%)
  Pallas kernels  38.5 us (19%)
  local copies, waits for them, and re-layouts  4.23 us (2%)
    ppermute x4, starting transfers between devices, forward(): lax.ppermute(value, 'page', [(2, 0), (3, 1), (0, 2), (1, 3)])  49.4 us
    ppermute x21, waiting for transfers between devices, swap(): lax.ppermute(value, axis, [(i, i ^ bit) for i in range(lax.axis_size(axis...  47.5 us
    ppermute x4, waiting for transfers between devices, forward(): lax.ppermute(value, 'page', [(2, 0), (3, 1), (0, 2), (1, 3)])  32.1 us
    pallas_call x23, Pallas kernels, run(): *results, token = call(*operands, *after)  22.3 us
    ppermute x21, starting transfers between devices, swap(): lax.ppermute(value, axis, [(i, i ^ bit) for i in range(lax.axis_size(axis...  19.1 us
    pallas_call x1, Pallas kernels, packed_mlp(): pl.pallas_call(functools.partial(mlp_kernel, len(sources)), in_specs=[SME...  16.2 us
    unnamed x16, local copies, waits for them, and re-layouts  4.11 us
  transfers between devices with their start and end apart: 33, of which 11 were waited for; matrix products, arithmetic and copies ran while one was open for 0% of the time, Pallas kernels for 11%

profile of v5, /device:TPU:0, one launch (start us, length us, event | category | flops | bytes accessed | tf_op | source)
XLA Modules:
  0.0 197.6 jit_solution(5781588366826899111)
XLA Ops:
  0.7 4.1 %collective-permute-start = (s32[8]{0:T(128)S(1)}, s32[8]{0:T(128)S(1)}, u32[]{:S(2)}, u32[]{:S(2)}) collective-permute-start(s32[8]{0:T(128)S(1)} %compare_select_fusion), channel_id=1, source_target_pairs={{0,16},{4,20},{8,24},{12,28},{16,0},{20,4},{24,8},{28,12},{1,17},{... | collective-permute-start | bytes 104 | tf_op jit(solution)/shard_map/ppermute | solution.py:432
  4.9 1.6 copy-done
  8.1 2.4 %first_factor.1 = (bf16[8,32,256]{2,1,0:T(8,128)(2,1)S(1)}, bf16[8,32,256]{2,1,0:T(8,128)(2,1)S(1)}, bf16[8,32,256]{2,1,0:T(8,128)(2,1)S(1)}, bf16[8,32,256]{2,1...) custom-call(s32[2]{0:T(128)S(1)} %pad_add_fusion.refs_0_.ids_ref, ...), custom_call_target="tpu_custom_call" | custom-call | flops 1 | tf_op jit(solution)/shard_map/first_factor/pallas_call | solution.py:162
  10.6 1.6 collective-permute-start.4
  12.4 1.6 collective-permute-start.1
  14.0 2.0 collective-permute-done.1
  17.2 1.7 collective-permute-start.2
  18.8 1.0 spread_stride.1
  20.7 1.2 second_factor.2
  21.9 1.7 collective-permute-start.6
  23.7 1.5 collective-permute-start.8
  25.5 11.3 %collective-permute-done.10.refs_2_ = bf16[192,1024]{1,0:T(8,128)(2,1)S(1)} collective-permute-done((bf16[192,1024]{1,0:T(8,128)(2,1)S(1)}, bf16[192,1024]{1,0:T(8,128)(2,1)S(1)}, u32[]{:S(2)}, u32[]{:S(2)}) %collective-permute-start.10) | collective-permute-done | bytes 393248 | tf_op jit(solution)/shard_map/ppermute | solution.py:432
  36.8 1.0 pair_up.6
  37.9 5.3 %collective-permute-done.9.refs_7_ = bf16[8,32,768]{2,1,0:T(8,128)(2,1)S(1)} collective-permute-done((bf16[8,32,768]{2,1,0:T(8,128)(2,1)S(1)}, bf16[8,32,768]{2,1,0:T(8,128)(2,1)S(1)}, u32[]{:S(2)}, u32[]{:S(2)}) %collective-permute-start.9) | collective-permute-done | bytes 393248 | tf_op jit(solution)/shard_map/ppermute | solution.py:432
  43.2 2.2 %second_factor.3 = (bf16[1024,256]{1,0:T(8,128)(2,1)S(1)}, bf16[1024,256]{1,0:T(8,128)(2,1)S(1)}, bf16[1024,256]{1,0:T(8,128)(2,1)S(1)}, s32[8,128]{1,0:T(8,128)S(1)}) custom-call(s32[2]{0:T(128)S(1)} %pad_add_fusion.refs_0_.ids_ref, s32[8]{0:T(128)S(1)} %add.11.refs_1_, s32[1,8]{1,0:T(1,128)S(1)} %copy-done.7, ...), custom_call_target="tpu_custom_call" | custom-call | flops 1 | tf_op jit(solution)/shard_map/second_factor/pallas_call | solution.py:162
  47.3 1.7 collective-permute-start.13
  49.4 10.8 %collective-permute-done.16.refs_3_ = bf16[1024,256]{1,0:T(8,128)(2,1)S(1)} collective-permute-done((bf16[1024,256]{1,0:T(8,128)(2,1)S(1)}, bf16[1024,256]{1,0:T(8,128)(2,1)S(1)}, u32[]{:S(2)}, u32[]{:S(2)}) %collective-permute-start.16) | collective-permute-done | bytes 524320 | tf_op jit(solution)/shard_map/ppermute | solution.py:432
  61.9 1.6 collective-permute-start.19
  64.8 6.7 %collective-permute-done.13.refs_3_ = bf16[1024,256]{1,0:T(8,128)(2,1)S(1)} collective-permute-done((bf16[1024,256]{1,0:T(8,128)(2,1)S(1)}, bf16[1024,256]{1,0:T(8,128)(2,1)S(1)}, u32[]{:S(2)}, u32[]{:S(2)}) %collective-permute-start.13) | collective-permute-done | bytes 524320 | tf_op jit(solution)/shard_map/ppermute | solution.py:432
  72.2 10.5 %collective-permute-done.14.refs_3_ = bf16[1024,256]{1,0:T(8,128)(2,1)S(1)} collective-permute-done((bf16[1024,256]{1,0:T(8,128)(2,1)S(1)}, bf16[1024,256]{1,0:T(8,128)(2,1)S(1)}, u32[]{:S(2)}, u32[]{:S(2)}) %collective-permute-start.14) | collective-permute-done | bytes 524320 | tf_op jit(solution)/shard_map/ppermute | solution.py:432
  85.8 18.2 %collective-permute-start.17 = (bf16[1024,256]{1,0:T(8,128)(2,1)S(1)}, bf16[1024,256]{1,0:T(8,128)(2,1)S(1)}, u32[]{:S(2)}, u32[]{:S(2)}) collective-permute-start(bf16[1024,256]{1,0:T(8,128)(2,1)S(1)} %get-tuple-element.86), channel_id=1, source_target_pairs={{8,0},{12,4},{0,8},{4,12},{9,1},{13,5},{1,9},{5,13},{10,2},{14,6},... | collective-permute-start | bytes 1572872 | tf_op jit(solution)/shard_map/ppermute | solution.py:605
  108.6 2.5 %collective-permute-done.17.refs_5_ = bf16[1024,256]{1,0:T(8,128)(2,1)S(1)} collective-permute-done((bf16[1024,256]{1,0:T(8,128)(2,1)S(1)}, bf16[1024,256]{1,0:T(8,128)(2,1)S(1)}, u32[]{:S(2)}, u32[]{:S(2)}) %collective-permute-start.17) | collective-permute-done | bytes 524320 | tf_op jit(solution)/shard_map/ppermute | solution.py:605
  111.2 8.1 %collective-permute-start.22 = (bf16[1024,256]{1,0:T(8,128)(2,1)S(1)}, bf16[1024,256]{1,0:T(8,128)(2,1)S(1)}, u32[]{:S(2)}, u32[]{:S(2)}) collective-permute-start(bf16[1024,256]{1,0:T(8,128)(2,1)S(1)} %get-tuple-element.94), channel_id=1, source_target_pairs={{8,0},{12,4},{0,8},{4,12},{9,1},{13,5},{1,9},{5,13},{10,2},{14,6},... | collective-permute-start | bytes 1572872 | tf_op jit(solution)/shard_map/ppermute | solution.py:605
  122.3 7.0 %collective-permute-done.22.refs_5_ = bf16[1024,256]{1,0:T(8,128)(2,1)S(1)} collective-permute-done((bf16[1024,256]{1,0:T(8,128)(2,1)S(1)}, bf16[1024,256]{1,0:T(8,128)(2,1)S(1)}, u32[]{:S(2)}, u32[]{:S(2)}) %collective-permute-start.22) | collective-permute-done | bytes 524320 | tf_op jit(solution)/shard_map/ppermute | solution.py:605
  129.4 17.6 %collective-permute-start.25 = (bf16[1024,256]{1,0:T(8,128)(2,1)S(1)}, bf16[1024,256]{1,0:T(8,128)(2,1)S(1)}, u32[]{:S(2)}, u32[]{:S(2)}) collective-permute-start(bf16[1024,256]{1,0:T(8,128)(2,1)S(1)} %get-tuple-element.99), channel_id=1, source_target_pairs={{8,0},{12,4},{0,8},{4,12},{9,1},{13,5},{1,9},{5,13},{10,2},{14,6},... | collective-permute-start | bytes 1572872 | tf_op jit(solution)/shard_map/ppermute | solution.py:605
  147.8 11.2 %collective-permute-done.25.refs_6_.refs_5_ = bf16[1024,256]{1,0:T(8,128)(2,1)S(1)} collective-permute-done((bf16[1024,256]{1,0:T(8,128)(2,1)S(1)}, bf16[1024,256]{1,0:T(8,128)(2,1)S(1)}, u32[]{:S(2)}, u32[]{:S(2)}) %collective-permute-start.25) | collective-permute-done | bytes 524320 | tf_op jit(solution)/shard_map/ppermute | solution.py:605
  159.8 1.0 pair_up.10
  160.8 1.0 pair_up.11
  162.4 5.4 %collective-permute-start.30 = (bf16[1024,256]{1,0:T(8,128)(2,1)S(1)}, bf16[1024,256]{1,0:T(8,128)(2,1)S(1)}, u32[]{:S(2)}, u32[]{:S(2)}) collective-permute-start(bf16[1024,256]{1,0:T(8,128)(2,1)S(1)} %get-tuple-element.108), channel_id=1, source_target_pairs={{8,0},{12,4},{0,8},{4,12},{9,1},{13,5},{1,9},{5,13},{10,2},{14,6},... | collective-permute-start | bytes 1572872 | tf_op jit(solution)/shard_map/ppermute | solution.py:605
  168.7 11.4 %collective-permute-done.30.refs_5_ = bf16[1024,256]{1,0:T(8,128)(2,1)S(1)} collective-permute-done((bf16[1024,256]{1,0:T(8,128)(2,1)S(1)}, bf16[1024,256]{1,0:T(8,128)(2,1)S(1)}, u32[]{:S(2)}, u32[]{:S(2)}) %collective-permute-start.30) | collective-permute-done | bytes 524320 | tf_op jit(solution)/shard_map/ppermute | solution.py:605
  180.0 1.4 final_merge.7
  181.4 16.2 %packed_mlp.1 = bf16[1,1024,1024]{2,1,0:T(8,128)(2,1)} custom-call(s32[2]{0:T(128)S(1)} %pad_add_fusion.refs_0_.ids_ref, bf16[1024,256]{1,0:T(8,128)(2,1)S(1)} %get-tuple-element.93.refs_0_, bf16[1024,256]{1,0:T(8,128)(2,1)S(1)} %get-tuple-element.98.refs_1_, bf16[1024,256]{1,0:T(8,128)(2,1)S(1)} %get-tuple-element.107.refs_2_, ...), custom_call_target="tpu_custom_call" | custom-call | tf_op jit(solution)/shard_map/packed_mlp/pallas_call | solution.py:421
  (80 shorter events, 24.0 us)
Async XLA Ops:
  0.7 11.7 %collective-permute-start = (s32[8]{0:T(128)S(1)}, s32[8]{0:T(128)S(1)}, u32[]{:S(2)}, u32[]{:S(2)}) collective-permute-start(s32[8]{0:T(128)S(1)} %compare_select_fusion), channel_id=1, source_target_pairs={{0,16},{4,20},{8,24},{12,28},{16,0},{20,4},{24,8},{28,12},{1,17},{... | collective-permute-start | bytes 104 | tf_op jit(solution)/shard_map/ppermute | solution.py:432
  10.5 10.2 %collective-permute-start.3 = (bf16[8,32,256]{2,1,0:T(8,128)(2,1)S(1)}, bf16[8,32,256]{2,1,0:T(8,128)(2,1)S(1)}, u32[]{:S(2)}, u32[]{:S(2)}) collective-permute-start(bf16[8,32,256]{2,1,0:T(8,128)(2,1)S(1)} %get-tuple-element.63), channel_id=1, source_target_pairs={{0,1},{1,0},{2,3},{3,2},{4,5},{5,4},{6,7},{7,6},{8,9},{9,8},{10,11... | collective-permute-start | bytes 393224 | tf_op jit(solution)/shard_map/ppermute | solution.py:432
  10.6 10.1 %collective-permute-start.4 = (bf16[8,32,256]{2,1,0:T(8,128)(2,1)S(1)}, bf16[8,32,256]{2,1,0:T(8,128)(2,1)S(1)}, u32[]{:S(2)}, u32[]{:S(2)}) collective-permute-start(bf16[8,32,256]{2,1,0:T(8,128)(2,1)S(1)} %get-tuple-element.64), channel_id=1, source_target_pairs={{0,2},{1,3},{2,0},{3,1},{4,6},{5,7},{6,4},{7,5},{8,10},{9,11},{10,... | collective-permute-start | bytes 393224 | tf_op jit(solution)/shard_map/ppermute | solution.py:432
  12.2 8.6 %collective-permute-start.5 = (bf16[8,32,256]{2,1,0:T(8,128)(2,1)S(1)}, bf16[8,32,256]{2,1,0:T(8,128)(2,1)S(1)}, u32[]{:S(2)}, u32[]{:S(2)}) collective-permute-start(bf16[8,32,256]{2,1,0:T(8,128)(2,1)S(1)} %get-tuple-element.65), channel_id=1, source_target_pairs={{0,3},{1,2},{2,1},{3,0},{4,7},{5,6},{6,5},{7,4},{8,11},{9,10},{10,... | collective-permute-start | bytes 393224 | tf_op jit(solution)/shard_map/ppermute | solution.py:432
  12.4 3.5 %collective-permute-start.1 = (s32[8]{0:T(128)S(1)}, s32[8]{0:T(128)S(1)}, u32[]{:S(2)}, u32[]{:S(2)}) collective-permute-start(s32[8]{0:T(128)S(1)} %fusion.1), channel_id=1, source_target_pairs={{0,8},{4,12},{8,0},{12,4},{16,24},{20,28},{24,16},{28,20},{1,9},{5... | collective-permute-start | bytes 104 | tf_op jit(solution)/shard_map/ppermute | solution.py:432
  16.9 19.9 %collective-permute-start.10 = (bf16[192,1024]{1,0:T(8,128)(2,1)S(1)}, bf16[192,1024]{1,0:T(8,128)(2,1)S(1)}, u32[]{:S(2)}, u32[]{:S(2)}) collective-permute-start(bf16[192,1024]{1,0:T(8,128)(2,1)S(1)} %get-tuple-element.72.refs_1_), channel_id=1, source_target_pairs={{0,16},{4,20},{8,24},{12,28},{16,0},{20,4},{24,8},{28,12},{1,17},{... | collective-permute-start | bytes 1179656 | tf_op jit(solution)/shard_map/ppermute | solution.py:432
  21.9 23.9 %collective-permute-start.6 = (bf16[1024,256]{1,0:T(8,128)(2,1)S(1)}, bf16[1024,256]{1,0:T(8,128)(2,1)S(1)}, u32[]{:S(2)}, u32[]{:S(2)}) collective-permute-start(bf16[1024,256]{1,0:T(8,128)(2,1)S(1)} %get-tuple-element.67.refs_2_), channel_id=1, source_target_pairs={{0,4},{4,0},{8,12},{12,8},{16,20},{20,16},{24,28},{28,24},{1,5},{5... | collective-permute-start | bytes 1572872 | tf_op jit(solution)/shard_map/ppermute | solution.py:432
  23.7 14.3 %collective-permute-start.7 = (bf16[8,32,768]{2,1,0:T(8,128)(2,1)S(1)}, bf16[8,32,768]{2,1,0:T(8,128)(2,1)S(1)}, u32[]{:S(2)}, u32[]{:S(2)}) collective-permute-start(bf16[8,32,768]{2,1,0:T(8,128)(2,1)S(1)} %get-tuple-element.69), channel_id=1, source_target_pairs={{0,1},{1,0},{2,3},{3,2},{4,5},{5,4},{6,7},{7,6},{8,9},{9,8},{10,11... | collective-permute-start | bytes 1179656 | tf_op jit(solution)/shard_map/ppermute | solution.py:432
  23.7 14.3 %collective-permute-start.8 = (bf16[8,32,768]{2,1,0:T(8,128)(2,1)S(1)}, bf16[8,32,768]{2,1,0:T(8,128)(2,1)S(1)}, u32[]{:S(2)}, u32[]{:S(2)}) collective-permute-start(bf16[8,32,768]{2,1,0:T(8,128)(2,1)S(1)} %get-tuple-element.70), channel_id=1, source_target_pairs={{0,2},{1,3},{2,0},{3,1},{4,6},{5,7},{6,4},{7,5},{8,10},{9,11},{10,... | collective-permute-start | bytes 1179656 | tf_op jit(solution)/shard_map/ppermute | solution.py:432
  25.2 18.0 %collective-permute-start.9 = (bf16[8,32,768]{2,1,0:T(8,128)(2,1)S(1)}, bf16[8,32,768]{2,1,0:T(8,128)(2,1)S(1)}, u32[]{:S(2)}, u32[]{:S(2)}) collective-permute-start(bf16[8,32,768]{2,1,0:T(8,128)(2,1)S(1)} %get-tuple-element.71), channel_id=1, source_target_pairs={{0,3},{1,2},{2,1},{3,0},{4,7},{5,6},{6,5},{7,4},{8,11},{9,10},{10,... | collective-permute-start | bytes 1179656 | tf_op jit(solution)/shard_map/ppermute | solution.py:432
  37.8 23.2 %collective-permute-start.15 = (bf16[2,192,1024]{2,1,0:T(8,128)(2,1)S(1)}, bf16[2,192,1024]{2,1,0:T(8,128)(2,1)S(1)}, u32[]{:S(2)}, u32[]{:S(2)}) collective-permute-start(bf16[2,192,1024]{2,1,0:T(8,128)(2,1)S(1)} %get-tuple-element.79.refs_1_), channel_id=1, source_target_pairs={{0,8},{4,12},{8,0},{12,4},{16,24},{20,28},{24,16},{28,20},{1,9},{5... | collective-permute-start | bytes 2359304 | tf_op jit(solution)/shard_map/ppermute | solution.py:432
  45.4 14.8 %collective-permute-start.16 = (bf16[1024,256]{1,0:T(8,128)(2,1)S(1)}, bf16[1024,256]{1,0:T(8,128)(2,1)S(1)}, u32[]{:S(2)}, u32[]{:S(2)}) collective-permute-start(bf16[1024,256]{1,0:T(8,128)(2,1)S(1)} %get-tuple-element.80.refs_2_), channel_id=1, source_target_pairs={{0,4},{4,0},{8,12},{12,8},{16,20},{20,16},{24,28},{28,24},{1,5},{5... | collective-permute-start | bytes 1572872 | tf_op jit(solution)/shard_map/ppermute | solution.py:432
  46.6 13.6 %collective-permute-start.12 = (bf16[1024,256]{1,0:T(8,128)(2,1)S(1)}, bf16[1024,256]{1,0:T(8,128)(2,1)S(1)}, u32[]{:S(2)}, u32[]{:S(2)}) collective-permute-start(bf16[1024,256]{1,0:T(8,128)(2,1)S(1)} %get-tuple-element.76.refs_2_), channel_id=1, source_target_pairs={{24,8},{28,12},{8,24},{12,28},{25,9},{29,13},{9,25},{13,29},{26,10... | collective-permute-start | bytes 1572872 | tf_op jit(solution)/shard_map/ppermute | solution.py:600
  47.3 24.1 %collective-permute-start.13 = (bf16[1024,256]{1,0:T(8,128)(2,1)S(1)}, bf16[1024,256]{1,0:T(8,128)(2,1)S(1)}, u32[]{:S(2)}, u32[]{:S(2)}) collective-permute-start(bf16[1024,256]{1,0:T(8,128)(2,1)S(1)} %get-tuple-element.77.refs_2_), channel_id=1, source_target_pairs={{0,4},{4,0},{8,12},{12,8},{16,20},{20,16},{24,28},{28,24},{1,5},{5... | collective-permute-start | bytes 1572872 | tf_op jit(solution)/shard_map/ppermute | solution.py:432
  49.1 33.6 %collective-permute-start.14 = (bf16[1024,256]{1,0:T(8,128)(2,1)S(1)}, bf16[1024,256]{1,0:T(8,128)(2,1)S(1)}, u32[]{:S(2)}, u32[]{:S(2)}) collective-permute-start(bf16[1024,256]{1,0:T(8,128)(2,1)S(1)} %get-tuple-element.78.refs_2_), channel_id=1, source_target_pairs={{0,4},{4,0},{8,12},{12,8},{16,20},{20,16},{24,28},{28,24},{1,5},{5... | collective-permute-start | bytes 1572872 | tf_op jit(solution)/shard_map/ppermute | solution.py:432
  61.9 42.9 %collective-permute-start.19 = (bf16[4,96,1024]{2,1,0:T(8,128)(2,1)S(1)}, bf16[4,96,1024]{2,1,0:T(8,128)(2,1)S(1)}, u32[]{:S(2)}, u32[]{:S(2)}) collective-permute-start(bf16[4,96,1024]{2,1,0:T(8,128)(2,1)S(1)} %get-tuple-element.113.refs_1_), channel_id=1, source_target_pairs={{0,2},{1,3},{2,0},{3,1},{4,6},{5,7},{6,4},{7,5},{8,10},{9,11},{10,... | collective-permute-start | bytes 2359304 | tf_op jit(solution)/shard_map/ppermute | solution.py:432
  63.5 42.8 %collective-permute-start.18 = (bf16[4,96,1024]{2,1,0:T(8,128)(2,1)S(1)}, bf16[4,96,1024]{2,1,0:T(8,128)(2,1)S(1)}, u32[]{:S(2)}, u32[]{:S(2)}) collective-permute-start(bf16[4,96,1024]{2,1,0:T(8,128)(2,1)S(1)} %get-tuple-element.114.refs_1_), channel_id=1, source_target_pairs={{0,4},{4,0},{8,12},{12,8},{16,20},{20,16},{24,28},{28,24},{1,5},{5... | collective-permute-start | bytes 2359304 | tf_op jit(solution)/shard_map/ppermute | solution.py:432
  64.1 20.9 %collective-permute-start.11 = (bf16[1024,256]{1,0:T(8,128)(2,1)S(1)}, bf16[1024,256]{1,0:T(8,128)(2,1)S(1)}, u32[]{:S(2)}, u32[]{:S(2)}) collective-permute-start(bf16[1024,256]{1,0:T(8,128)(2,1)S(1)} %get-tuple-element.76.refs_2_), channel_id=1, source_target_pairs={{16,8},{20,12},{24,16},{28,20},{17,9},{21,13},{25,17},{29,21},{18,... | collective-permute-start | bytes 1572872 | tf_op jit(solution)/shard_map/ppermute | solution.py:599
  71.5 32.6 %collective-permute-start.21 = (bf16[1024,256]{1,0:T(8,128)(2,1)S(1)}, bf16[1024,256]{1,0:T(8,128)(2,1)S(1)}, u32[]{:S(2)}, u32[]{:S(2)}) collective-permute-start(bf16[1024,256]{1,0:T(8,128)(2,1)S(1)} %get-tuple-element.88.refs_2_), channel_id=1, source_target_pairs={{24,8},{28,12},{8,24},{12,28},{25,9},{29,13},{9,25},{13,29},{26,10... | collective-permute-start | bytes 1572872 | tf_op jit(solution)/shard_map/ppermute | solution.py:600
  82.7 21.3 %collective-permute-start.20 = (bf16[1024,256]{1,0:T(8,128)(2,1)S(1)}, bf16[1024,256]{1,0:T(8,128)(2,1)S(1)}, u32[]{:S(2)}, u32[]{:S(2)}) collective-permute-start(bf16[1024,256]{1,0:T(8,128)(2,1)S(1)} %get-tuple-element.88.refs_2_), channel_id=1, source_target_pairs={{16,8},{20,12},{24,16},{28,20},{17,9},{21,13},{25,17},{29,21},{18,... | collective-permute-start | bytes 1572872 | tf_op jit(solution)/shard_map/ppermute | solution.py:599
  85.8 25.4 %collective-permute-start.17 = (bf16[1024,256]{1,0:T(8,128)(2,1)S(1)}, bf16[1024,256]{1,0:T(8,128)(2,1)S(1)}, u32[]{:S(2)}, u32[]{:S(2)}) collective-permute-start(bf16[1024,256]{1,0:T(8,128)(2,1)S(1)} %get-tuple-element.86), channel_id=1, source_target_pairs={{8,0},{12,4},{0,8},{4,12},{9,1},{13,5},{1,9},{5,13},{10,2},{14,6},... | collective-permute-start | bytes 1572872 | tf_op jit(solution)/shard_map/ppermute | solution.py:605
  105.7 54.1 %collective-permute-start.27 = (bf16[2,4,96,1024]{3,2,1,0:T(8,128)(2,1)S(1)}, bf16[2,4,96,1024]{3,2,1,0:T(8,128)(2,1)S(1)}, u32[]{:S(2)}, u32[]{:S(2)}) collective-permute-start(bf16[2,4,96,1024]{3,2,1,0:T(8,128)(2,1)S(1)} %get-tuple-element.101.refs_1_), channel_id=1, source_target_pairs={{0,4},{4,0},{8,12},{12,8},{16,20},{20,16},{24,28},{28,24},{1,5},{5... | collective-permute-start | bytes 4718600 | tf_op jit(solution)/shard_map/ppermute | solution.py:432
  107.1 53.7 %collective-permute-start.26 = (bf16[2,4,96,1024]{3,2,1,0:T(8,128)(2,1)S(1)}, bf16[2,4,96,1024]{3,2,1,0:T(8,128)(2,1)S(1)}, u32[]{:S(2)}, u32[]{:S(2)}) collective-permute-start(bf16[2,4,96,1024]{3,2,1,0:T(8,128)(2,1)S(1)} %get-tuple-element.100.refs_1_), channel_id=1, source_target_pairs={{0,2},{1,3},{2,0},{3,1},{4,6},{5,7},{6,4},{7,5},{8,10},{9,11},{10,... | collective-permute-start | bytes 4718600 | tf_op jit(solution)/shard_map/ppermute | solution.py:432
  107.2 12.9 %collective-permute-start.24 = (bf16[1024,256]{1,0:T(8,128)(2,1)S(1)}, bf16[1024,256]{1,0:T(8,128)(2,1)S(1)}, u32[]{:S(2)}, u32[]{:S(2)}) collective-permute-start(bf16[1024,256]{1,0:T(8,128)(2,1)S(1)} %get-tuple-element.95.refs_2_), channel_id=1, source_target_pairs={{24,8},{28,12},{8,24},{12,28},{25,9},{29,13},{9,25},{13,29},{26,10... | collective-permute-start | bytes 1572872 | tf_op jit(solution)/shard_map/ppermute | solution.py:600
  107.9 12.9 %collective-permute-start.23 = (bf16[1024,256]{1,0:T(8,128)(2,1)S(1)}, bf16[1024,256]{1,0:T(8,128)(2,1)S(1)}, u32[]{:S(2)}, u32[]{:S(2)}) collective-permute-start(bf16[1024,256]{1,0:T(8,128)(2,1)S(1)} %get-tuple-element.95.refs_2_), channel_id=1, source_target_pairs={{16,8},{20,12},{24,16},{28,20},{17,9},{21,13},{25,17},{29,21},{18,... | collective-permute-start | bytes 1572872 | tf_op jit(solution)/shard_map/ppermute | solution.py:599
  111.2 18.2 %collective-permute-start.22 = (bf16[1024,256]{1,0:T(8,128)(2,1)S(1)}, bf16[1024,256]{1,0:T(8,128)(2,1)S(1)}, u32[]{:S(2)}, u32[]{:S(2)}) collective-permute-start(bf16[1024,256]{1,0:T(8,128)(2,1)S(1)} %get-tuple-element.94), channel_id=1, source_target_pairs={{8,0},{12,4},{0,8},{4,12},{9,1},{13,5},{1,9},{5,13},{10,2},{14,6},... | collective-permute-start | bytes 1572872 | tf_op jit(solution)/shard_map/ppermute | solution.py:605
  120.1 27.7 %collective-permute-start.29 = (bf16[1024,256]{1,0:T(8,128)(2,1)S(1)}, bf16[1024,256]{1,0:T(8,128)(2,1)S(1)}, u32[]{:S(2)}, u32[]{:S(2)}) collective-permute-start(bf16[1024,256]{1,0:T(8,128)(2,1)S(1)} %get-tuple-element.102.refs_2_), channel_id=1, source_target_pairs={{24,8},{28,12},{8,24},{12,28},{25,9},{29,13},{9,25},{13,29},{26,10... | collective-permute-start | bytes 1572872 | tf_op jit(solution)/shard_map/ppermute | solution.py:600
  120.8 27.0 %collective-permute-start.28 = (bf16[1024,256]{1,0:T(8,128)(2,1)S(1)}, bf16[1024,256]{1,0:T(8,128)(2,1)S(1)}, u32[]{:S(2)}, u32[]{:S(2)}) collective-permute-start(bf16[1024,256]{1,0:T(8,128)(2,1)S(1)} %get-tuple-element.102.refs_2_), channel_id=1, source_target_pairs={{16,8},{20,12},{24,16},{28,20},{17,9},{21,13},{25,17},{29,21},{18,... | collective-permute-start | bytes 1572872 | tf_op jit(solution)/shard_map/ppermute | solution.py:599
  129.4 29.6 %collective-permute-start.25 = (bf16[1024,256]{1,0:T(8,128)(2,1)S(1)}, bf16[1024,256]{1,0:T(8,128)(2,1)S(1)}, u32[]{:S(2)}, u32[]{:S(2)}) collective-permute-start(bf16[1024,256]{1,0:T(8,128)(2,1)S(1)} %get-tuple-element.99), channel_id=1, source_target_pairs={{8,0},{12,4},{0,8},{4,12},{9,1},{13,5},{1,9},{5,13},{10,2},{14,6},... | collective-permute-start | bytes 1572872 | tf_op jit(solution)/shard_map/ppermute | solution.py:605
  161.9 19.5 %collective-permute-start.32 = (bf16[4,4,96,1024]{3,2,1,0:T(8,128)(2,1)S(1)}, bf16[4,4,96,1024]{3,2,1,0:T(8,128)(2,1)S(1)}, u32[]{:S(2)}, u32[]{:S(2)}) collective-permute-start(bf16[4,4,96,1024]{3,2,1,0:T(8,128)(2,1)S(1)} %bitcast.13), channel_id=1, source_target_pairs={{0,1},{1,0},{2,3},{3,2},{4,5},{5,4},{6,7},{7,6},{8,9},{9,8},{10,11... | collective-permute-start | bytes 9437192 | tf_op jit(solution)/shard_map/ppermute | solution.py:432
  161.9 19.5 %collective-permute-start.31 = (bf16[4,4,96,1024]{3,2,1,0:T(8,128)(2,1)S(1)}, bf16[4,4,96,1024]{3,2,1,0:T(8,128)(2,1)S(1)}, u32[]{:S(2)}, u32[]{:S(2)}) collective-permute-start(bf16[4,4,96,1024]{3,2,1,0:T(8,128)(2,1)S(1)} %bitcast.11), channel_id=1, source_target_pairs={{0,1},{1,0},{2,3},{3,2},{4,5},{5,4},{6,7},{7,6},{8,9},{9,8},{10,11... | collective-permute-start | bytes 9437192 | tf_op jit(solution)/shard_map/ppermute | solution.py:432
  162.4 17.6 %collective-permute-start.30 = (bf16[1024,256]{1,0:T(8,128)(2,1)S(1)}, bf16[1024,256]{1,0:T(8,128)(2,1)S(1)}, u32[]{:S(2)}, u32[]{:S(2)}) collective-permute-start(bf16[1024,256]{1,0:T(8,128)(2,1)S(1)} %get-tuple-element.108), channel_id=1, source_target_pairs={{8,0},{12,4},{0,8},{4,12},{9,1},{13,5},{1,9},{5,13},{10,2},{14,6},... | collective-permute-start | bytes 1572872 | tf_op jit(solution)/shard_map/ppermute | solution.py:605
  (9 other events, 59.7 us)
